TPU v7x, 256 devices: a whole 4x4x8 slice. The times are simulated.
256 devices in a mesh: dp: 2 (over core), ctx: 32 (over z, x), tensor: 4 (over y).
Axes of the slice: x: 4, y: 4, z: 8, core: 2. Of those that a mesh axis runs over, the one named last changes fastest.
Arguments:
- features: bfloat16 [2, 8192, 8192], P('dp', 'ctx', 'tensor'), may hold values from -500 to 500
- gate_in: bfloat16 [2, 8192, 8192], P('dp', 'ctx', 'tensor'), may hold values from -6 to 6
- segments: int32 [2, 8192], P('dp', 'ctx'), may hold values from 0 to 3, never falling along the last dimension, each value on 1 to 4096 neighbouring positions
- gain: float32 [8192], P('tensor'), may hold values from 0.25 to 1.75
- residue: float32 [512, 16], P('tensor'), may hold values from -4 to 4
- rates: float32 [512, 16], P('tensor'), may hold values from 0 to 1
- grad_out: bfloat16 [2, 8192, 8192], P('dp', 'ctx', 'tensor'), may hold values from -6 to 6
Outputs:
- mixed: bfloat16 [2, 8192, 8192], P('dp', 'ctx', 'tensor')
- grad_features: bfloat16 [2, 8192, 8192], P('dp', 'ctx', 'tensor')
- grad_gate: bfloat16 [2, 8192, 8192], P('dp', 'ctx', 'tensor')
- grad_residue: float32 [512, 16], P('tensor')
- grad_gain: float32 [8192], P('tensor')
Inputs may be any that keep to these rules, and one draw needn't show every extreme that they name: `segments`: pair ids never fall along a sequence; each of the 4 ids covers 1 to 4096 positions, and one covers exactly 4096.
All inputs are finite; a program needn't handle non-finite values.
Results may differ from a plain program's by a relative error of at most 0.001.
Values sent between devices are 32-bit elements; how exact they have to be, the bound alone decides.
No kernel may reach another device: no remote copies, remote signals or barrier semaphores. Data moves between devices by JAX's collectives and lax.ppermute only.
A program may use at most 128 MiB of HBM per device.

v0:
```python
import math

import jax
import jax.numpy as jnp
from jax import lax
from jax.sharding import PartitionSpec as P

epsilon = 1e-06
highest_level = lax.Precision.HIGHEST


def shards(features, gate_in, segments, gain, residue, rates, grad_out):
    batch_rows, length, width = features.shape
    group_count, mode_count = rates.shape
    group_size = width // group_count
    full_width = width * lax.axis_size("tensor")
    feats = features.astype(jnp.float32)
    square_sum = lax.psum(jnp.sum(feats * feats, axis=2), "tensor")
    inverse_rms = lax.rsqrt(square_sum / full_width + epsilon)
    normed = feats * inverse_rms[:, :, None] * gain
    gate_full = gate_in.astype(jnp.float32)
    grad_full = grad_out.astype(jnp.float32)
    grad_conv = grad_full * gate_full
    grouped_rows = normed.reshape(batch_rows, length, group_count, group_size)
    grouped_gradient = grad_conv.reshape(batch_rows, length, group_count, group_size)
    positions = jnp.arange(length, dtype=jnp.float32)
    decay_target = jnp.exp(-rates[:, :, None] * positions)
    decay_source = jnp.exp(-rates[:, :, None] * (length - 1.0 - positions))
    single_step = jnp.exp(-rates)[:, :, None]
    root_weight = jnp.sqrt(-jnp.expm1(-2.0 * rates))
    weights = residue * root_weight
    first_id = segments[:, 0]
    last_id = segments[:, -1]
    leading_mask = (segments == first_id[:, None]).astype(jnp.float32)
    trailing_mask = (segments == last_id[:, None]).astype(jnp.float32)
    final_state = jnp.einsum(
        "we,zme,wezi->wzim", trailing_mask, decay_source, grouped_rows, precision=highest_level
    )
    start_adjoint = jnp.einsum(
        "we,zme,wezi->wzim", leading_mask, decay_target, grouped_gradient, precision=highest_level
    )
    first_float = first_id.astype(jnp.float32)
    last_float = last_id.astype(jnp.float32)
    own_index = lax.axis_index("ctx")
    id_pair = jnp.stack([first_float, last_float], axis=1)
    state_piece = lax.all_gather(final_state[None], "ctx", axis=0, tiled=True)
    adjoint_piece = lax.all_gather(start_adjoint[None], "ctx", axis=0, tiled=True)
    id_piece = lax.all_gather(id_pair[None], "ctx", axis=0, tiled=True)
    sources = jnp.arange(state_piece.shape[0], dtype=jnp.int32)
    behind = jnp.maximum(own_index - 1 - sources, 0).astype(jnp.float32) * length
    ahead = jnp.maximum(sources - own_index - 1, 0).astype(jnp.float32) * length
    take_behind = (
        (sources < own_index)[:, None] & (id_piece[:, :, 1] == first_float[None, :])
    ).astype(jnp.float32)
    take_ahead = (
        (sources > own_index)[:, None] & (id_piece[:, :, 0] == last_float[None, :])
    ).astype(jnp.float32)
    weight_behind = take_behind[:, :, None, None] * jnp.exp(
        -rates[None, None] * behind[:, None, None, None]
    )
    weight_ahead = take_ahead[:, :, None, None] * jnp.exp(
        -rates[None, None] * ahead[:, None, None, None]
    )
    carry_in_state = jnp.einsum(
        "jbgr,jbgcr->bgcr", weight_behind, state_piece, precision=highest_level
    )
    carry_adjoint = jnp.einsum(
        "jbgr,jbgcr->bgcr", weight_ahead, adjoint_piece, precision=highest_level
    )
    slab = math.gcd(8, group_count)
    same_pair = (
        (segments[:, :, None] == segments[:, None, :]) & (positions[:, None] >= positions[None, :])
    ).astype(jnp.float32)
    middle = 0.5 * (length - 1)
    rising = jnp.exp(-rates[:, :, None] * (positions - middle))
    falling = jnp.exp(-rates[:, :, None] * (middle - positions))

    def local_slab(slab_index):
        offset = slab_index * slab
        rising_portion = lax.dynamic_slice_in_dim(rising, offset, slab, 0)
        falling_portion = lax.dynamic_slice_in_dim(falling, offset, slab, 0)
        weight_portion = lax.dynamic_slice_in_dim(weights, offset, slab, 0)
        input_part = lax.dynamic_slice_in_dim(grouped_rows, offset, slab, 2)
        grad_part = lax.dynamic_slice_in_dim(grouped_gradient, offset, slab, 2)
        kernel = jnp.einsum(
            "jdo,jda->joa",
            weight_portion[:, :, None] * rising_portion,
            falling_portion,
            precision=highest_level,
        )
        kernel = kernel[None] * same_pair[:, None]
        conv_part = jnp.einsum("bgts,bsgc->btgc", kernel, input_part, precision=highest_level)
        back_part = jnp.einsum("bgts,btgc->bsgc", kernel, grad_part, precision=highest_level)
        gram = (
            jnp.einsum("btgc,bsgc->bgts", grad_part, input_part, precision=highest_level)
            * same_pair[:, None]
        )
        running_sum = jnp.einsum("bgts,grs->bgtr", gram, falling_portion, precision=highest_level)
        mode_gradient = jnp.einsum(
            "pqod,qdo->qd", running_sum, rising_portion, precision=highest_level
        )
        return (conv_part, back_part, mode_gradient)

    conv_slabs, back_slabs, mode_slabs = lax.map(
        local_slab, jnp.arange(group_count // slab, dtype=jnp.int32)
    )

    def unslab(stacked):
        return jnp.transpose(stacked, (1, 2, 0, 3, 4)).reshape(batch_rows, length, width)

    reach_length = weights[:, :, None] * decay_target * single_step
    carried_over = (
        jnp.einsum("eni,qepn->qiep", reach_length, carry_in_state, precision=highest_level)
        * leading_mask[:, :, None, None]
    )
    conv = unslab(conv_slabs) + carried_over.reshape(batch_rows, length, width)
    returned = (
        jnp.einsum(
            "grs,bgcr->bsgc",
            weights[:, :, None] * decay_source * single_step,
            carry_adjoint,
            precision=highest_level,
        )
        * trailing_mask[:, :, None, None]
    )
    grad_normed = unslab(back_slabs) + returned.reshape(batch_rows, length, width)
    moment = jnp.einsum(
        "we,zme,wezi->wzim",
        leading_mask,
        decay_target * single_step,
        grouped_gradient,
        precision=highest_level,
    )
    mode_total = mode_slabs.reshape(group_count, mode_count) + jnp.sum(
        moment * carry_in_state, axis=(0, 2)
    )
    mixed = (gate_full * conv).astype(jnp.bfloat16)
    grad_gate = (grad_full * conv).astype(jnp.bfloat16)
    grad_gain_part = jnp.sum(grad_normed * feats * inverse_rms[:, :, None], axis=(0, 1))
    scaled_grad = grad_normed * gain
    inner = lax.psum(jnp.sum(scaled_grad * feats, axis=2), "tensor")
    correction = inner * inverse_rms * inverse_rms / full_width
    grad_features = (
        inverse_rms[:, :, None] * (scaled_grad - feats * correction[:, :, None])
    ).astype(jnp.bfloat16)
    grad_res_sum, grad_gain_sum = lax.psum((mode_total, grad_gain_part), ("dp", "ctx"))
    norm_factor = 1.0 / math.sqrt(batch_rows * lax.axis_size("dp") * length * lax.axis_size("ctx"))
    return (
        mixed,
        grad_features,
        grad_gate,
        grad_res_sum * root_weight * norm_factor,
        grad_gain_sum * norm_factor,
    )


def solution(mesh):
    placed = (
        P("dp", "ctx", "tensor"),
        P("dp", "ctx", "tensor"),
        P("dp", "ctx"),
        P("tensor"),
        P("tensor", None),
        P("tensor", None),
        P("dp", "ctx", "tensor"),
    )
    return jax.shard_map(
        shards,
        mesh=mesh,
        in_specs=placed,
        out_specs=(
            P("dp", "ctx", "tensor"),
            P("dp", "ctx", "tensor"),
            P("dp", "ctx", "tensor"),
            P("tensor", None),
            P("tensor"),
        ),
        check_vma=False,
    )
```

profile of v0, /device:TPU:136, one launch (start us, length us, event | category | flops | bytes accessed | tf_op | source)
XLA Modules:
  0.0 667.3 jit_solution(11414220544543449116)
XLA Ops:
  9.1 8.7 %psum.28 = f32[1,256]{1,0:T(1,128)S(1)} all-reduce(f32[1,256]{1,0:T(1,128)S(1)} %bitcast.169), channel_id=1, replica_groups=mesh['dp'=2,'ctx'=32,'tensor'=4] {'tensor'}, use_global_device_ids=true, to_apply=%region_1.0 | all-reduce | flops 256 | bytes 2048 | tf_op jit(solution)/shard_map/psum | solution.py:18
  37.2 251.7 %while.15 = (s32[]{:T(128)}, f32[16,1,256,8,16]{2,4,3,1,0:T(8,128)}, f32[16,1,256,8,16]{2,4,3,1,0:T(8,128)}, f32[16,8,16]{2,1,0:T(8,128)}, s32[16]{0:T(128)S(1)}...) while((s32[]{:T(128)}, ...), condition=%wide.region_3.0_spmd.clone, body=%wide.region_2.3_spmd.clone.sunk | while | flops 505249664 | bytes 12856039 | solution.py:104
  41.5 3.4 fusion.135
  57.3 3.4 fusion.135
  73.0 3.4 fusion.135
  88.7 3.4 fusion.135
  104.5 3.4 fusion.135
  120.2 3.4 fusion.135
  135.9 3.4 fusion.135
  151.6 3.4 fusion.135
  167.4 3.4 fusion.135
  183.2 3.4 fusion.135
  198.9 3.4 fusion.135
  230.3 3.4 fusion.135
  246.0 3.4 fusion.135
  261.7 3.4 fusion.135
  277.5 3.4 fusion.135
  290.2 37.5 %all-gather.3 = f32[32,1,2]{2,1,0:T(1,128)S(1)} all-gather(f32[1,1,2]{2,1,0:T(1,128)S(1)} %maximum_bitcast_fusion), channel_id=3, replica_groups=mesh['dp'=2,'ctx'=32,'tensor'=4] {'ctx'}, dimensions={0}, use_global_device_ids=true | all-gather | bytes 264 | tf_op jit(solution)/shard_map/all_gather | solution.py:48
  340.8 4.0 bitcast_multiply_fusion.1
  344.9 3.5 fusion.51
  350.6 4.7 fusion.83
  360.5 4.0 bitcast_multiply_fusion
  365.9 10.2 %psum.29 = f32[1,256]{1,0:T(1,128)S(1)} all-reduce(f32[1,256]{1,0:T(1,128)S(1)} %bitcast.168), channel_id=1, replica_groups=mesh['dp'=2,'ctx'=32,'tensor'=4] {'tensor'}, use_global_device_ids=true, to_apply=%region_5.6 | all-reduce | flops 256 | bytes 2048 | tf_op jit(solution)/shard_map/psum | solution.py:141
  382.9 276.3 %all-reduce = (f32[128,16]{0,1:T(8,128)S(1)}, f32[2048]{0:T(1024)S(1)}) all-reduce(f32[128,16]{0,1:T(8,128)S(1)} %add.68, f32[2048]{0:T(1024)S(1)} %get-tuple-element.150), channel_id=1, replica_groups=mesh['dp'=2,'ctx'=32,'tensor'=4] {'dp','ctx'}, use_global_device_ids=true, to_apply=%region_7.8 | all-reduce | flops 4096 | bytes 32768 | tf_op jit(solution)/shard_map/psum | solution.py:146
  (227 shorter events, 241.4 us)
Async XLA Ops:
  7.2 11.1 %copy-start.12 = (f32[128,16]{0,1:T(8,128)S(1)}, f32[128,16]{0,1:T(8,128)}, u32[]{:S(2)}) copy-start(f32[128,16]{0,1:T(8,128)} %param.14) | copy-start | bytes 24580
  7.2 11.1 %copy-start.18 = (f32[128,16]{0,1:T(8,128)S(1)}, f32[128,16]{0,1:T(8,128)}, u32[]{:S(2)}) copy-start(f32[128,16]{0,1:T(8,128)} %param.13) | copy-start | bytes 24580
  7.2 11.3 %copy-start.9 = (s32[1,256]{1,0:T(1,128)S(1)}, s32[1,256]{1,0:T(1,128)}, u32[]{:S(2)}) copy-start(s32[1,256]{1,0:T(1,128)} %param.11) | copy-start | bytes 3076
  7.2 11.8 %copy-start.10 = (f32[2048]{0:T(1024)S(1)}, f32[2048]{0:T(1024)}, u32[]{:S(2)}) copy-start(f32[2048]{0:T(1024)} %param.12) | copy-start | bytes 24580
  7.2 326.8 %all-gather.7.cloned.1.call-start = ((), (), s32[]{:S(2)}) async-start(), calls=%async_computation | async-start | bytes 4325376 | tf_op jit(solution)/shard_map/all_gather | solution.py:46
  7.3 13.4 %copy-start.21 = (f32[256]{0:T(256)}, f32[256]{0:T(256)S(1)}, u32[]{:S(2)}) copy-start(f32[256]{0:T(256)S(1)} %iota_subtract_fusion) | copy-start | bytes 3076
  17.8 0.5 copy-start.16
  18.3 4.8 copy-start.14
  19.4 1.4 copy-start
  20.6 3.5 copy-start.19
  20.6 8.1 %copy-start.20 = (f32[1,256]{1,0:T(1,128)}, f32[1,256]{1,0:T(1,128)S(1)}, u32[]{:S(2)}) copy-start(f32[1,256]{1,0:T(1,128)S(1)} %get-tuple-element.187) | copy-start | bytes 3076
  20.7 3.7 copy-start.7
  24.1 1.6 copy-start.8
  24.2 331.1 %all-gather.9.cloned.1.call-start = ((), (), s32[]{:S(2)}) async-start(), calls=%async_computation.1 | async-start | bytes 4325376 | tf_op jit(solution)/shard_map/all_gather | solution.py:47
  334.0 3.0 copy-start.6
  340.8 4.1 copy-start.1
  340.8 4.1 copy-start.2
  360.5 4.1 copy-start.3
  360.5 4.1 copy-start.15
  364.5 1.3 copy-start.4
  364.6 11.5 %copy-start.17 = (f32[1,256]{1,0:T(1,128)S(1)}, f32[1,256]{1,0:T(1,128)}, u32[]{:S(2)}) copy-start(f32[1,256]{1,0:T(1,128)} %copy-done.16) | copy-start | bytes 3076
  379.1 2.4 copy-start.5
  379.1 3.8 copy-start.11
  379.1 3.8 copy-start.13
Sparse Core Ops, SparseCore 0:
  24.3 81.8 all-gather.6
  108.6 83.6 all-gather.8
where the time goes:
time: 669 us; the launch traced here: 667 us
  blocking collectives  333 us (50%)
  matrix products  238 us (36%)
  local copies, waits for them, and re-layouts  48 us (7%)
  other arithmetic  21.5 us (3%)
  between operations  15.6 us (2%)
  loops' own time  11 us (2%)
    psum x1, blocking collectives, shards(): lax.psum((mode_total, grad_gain_part), ('dp', 'ctx'))  276 us
    dot_general x16, matrix products, local_slab(): jnp.einsum('bgts,bsgc->btgc', kernel, input_part, precision=highest_level)  53.9 us
    dot_general x16, matrix products, local_slab(): jnp.einsum('jdo,jda->joa', weight_portion[:, :, None] * rising_portion, f...  47.4 us
    dot_general x16, matrix products, local_slab(): jnp.einsum('bgts,grs->bgtr', gram, falling_portion, precision=highest_level)  45.6 us
    dot_general x16, matrix products, local_slab(): jnp.einsum('btgc,bsgc->bgts', grad_part, input_part, precision=highest_le...  43.9 us
    all_gather x1, blocking collectives, shards(): id_piece = lax.all_gather(id_pair[None], 'ctx', axis=0, tiled=True)  37.5 us
    dot_general x16, matrix products, local_slab(): jnp.einsum('bgts,btgc->bsgc', kernel, grad_part, precision=highest_level)  29.3 us
    unnamed x55, local copies, waits for them, and re-layouts  19 us
  transfers between devices with their start and end apart: 2, of which 0 were waited for; matrix products, arithmetic and copies ran while one was open for 42% of the time, Pallas kernels for 0%

commit v1 on v0

v1 whole, which is shorter than its diff:
```python
import math

import jax
import jax.numpy as jnp
from jax import lax
from jax.experimental import pallas as pl
from jax.experimental.pallas import tpu as pltpu
from jax.sharding import PartitionSpec as P

epsilon = 1e-06
LANES = 128
TILES = 8
MODES = 16
GROUP = 16
UNROLL = 8
EXTRA = 8
HIGHEST = lax.Precision.HIGHEST
f32 = jnp.float32


def lane_iota(rows):
    return lax.broadcasted_iota(jnp.int32, (rows, LANES), 1)


def swap(value):
    return pltpu.roll(value, LANES // 2, axis=1)


def join(low, high):
    return jnp.where(lane_iota(low.shape[0]) < LANES // 2, low, high)


def column(row_ref, length):
    row = jnp.broadcast_to(row_ref[0:1, :], (8, length))
    return jnp.broadcast_to(jnp.transpose(row)[:, 0:1], (length, LANES))


def block_ones():
    left = lax.broadcasted_iota(jnp.int32, (LANES, LANES), 0) // GROUP
    right = lax.broadcasted_iota(jnp.int32, (LANES, LANES), 1) // GROUP
    return jnp.where(left == right, 1.0, 0.0).astype(f32)


def to_scan(dst, tile, value, length):
    dst[pl.ds(tile, length, stride=TILES), :] = value


def from_scan(src, tile, length):
    return src[pl.ds(tile, length, stride=TILES), :]


def tile_of(ref, tile):
    return ref[:, tile * LANES : (tile + 1) * LANES].astype(f32)


def tree(values):
    values = list(values)
    while len(values) > 1:
        values = [a + b for a, b in zip(values[::2], values[1::2])]
    return values[0]


def scan(length, seg, step, carry, backward):
    groups = length // UNROLL

    def body(index, carry):
        group = groups - 1 - index if backward else index
        base = group * UNROLL
        if backward:
            edge = jnp.minimum(base + UNROLL, length - 1)
            plain = seg[0, base] == seg[0, edge]
        else:
            edge = jnp.maximum(base - 1, 0)
            plain = seg[0, edge] == seg[0, base + UNROLL - 1]

        def fast(carry):
            for u in range(UNROLL):
                t = base + (UNROLL - 1 - u if backward else u)
                carry = step(t, carry, None)
            return carry

        def slow(carry):
            for u in range(UNROLL):
                t = base + (UNROLL - 1 - u if backward else u)
                near = jnp.minimum(t + 1, length - 1) if backward else jnp.maximum(t - 1, 0)
                carry = step(t, carry, seg[0, t] == seg[0, near])
            return carry

        return lax.cond(plain, fast, slow, carry)

    return lax.fori_loop(0, groups, body, carry)


def decayed(decay, state, keep):
    state = decay * state
    return state if keep is None else jnp.where(keep, state, 0.0)


def row_at(ref, t):
    return ref[pl.ds(pl.multiple_of(t * TILES, TILES), TILES), :]


def adjoint_kernel(seg, gate, grad, rates, adj, grad_scan):
    length = gate.shape[0]
    for tile in range(TILES):
        to_scan(grad_scan, tile, tile_of(gate, tile) * tile_of(grad, tile), length)
    decay = [jnp.exp(-rates[r]) for r in range(MODES)]

    def step(t, states, keep):
        value = row_at(grad_scan, t)
        return tuple(decayed(decay[r], states[r], keep) + value for r in range(MODES))

    zero = jnp.zeros((TILES, LANES), f32)
    states = scan(length, seg, step, (zero,) * MODES, True)
    for r in range(MODES):
        adj[pl.ds(r, TILES, stride=MODES), :] = states[r]


def state_kernel(
    seg, feats, gate, grad, inverse, rates, weights, gain, adj, msg, feat_scan, grad_scan, ends, sums
):
    length = gate.shape[0]
    scale = column(inverse, length)
    for tile in range(TILES):
        to_scan(feat_scan, tile, tile_of(feats, tile) * scale, length)
        to_scan(grad_scan, tile, tile_of(gate, tile) * tile_of(grad, tile), length)
    decay = [jnp.exp(-rates[r]) for r in range(MODES)]

    def step(t, carry, keep):
        value = row_at(feat_scan, t)
        grads = row_at(grad_scan, t)
        states = [decayed(decay[r], carry[r], keep) + value for r in range(MODES)]
        totals = [carry[MODES + r] + grads * states[r] for r in range(MODES)]
        return tuple(states) + tuple(totals)

    zero = jnp.zeros((TILES, LANES), f32)
    carry = scan(length, seg, step, (zero,) * (2 * MODES), False)
    gains = gain[...]
    for r in range(MODES):
        ends[pl.ds(r, TILES, stride=MODES), :] = carry[r]
        sums[r * TILES : (r + 1) * TILES, :] = carry[MODES + r] * gains
    gain_row = tree([weights[r] * carry[MODES + r] for r in range(MODES)])
    spread = jnp.dot(sums[...], block_ones(), precision=HIGHEST, preferred_element_type=f32)
    lane_mode = lane_iota(TILES) % GROUP
    mode_row = tree(
        [
            jnp.where(lane_mode == r, spread[r * TILES : (r + 1) * TILES, :], 0.0)
            for r in range(MODES)
        ]
    )
    even = join(gain_row, swap(mode_row))
    odd = join(swap(gain_row), mode_row)
    first = jnp.full((1, LANES), seg[0, 0], jnp.int32).astype(f32)
    last = jnp.full((1, LANES), seg[0, length - 1], jnp.int32).astype(f32)
    near = join(first, last)
    far = join(last, first)
    sub = lax.broadcasted_iota(jnp.int32, (EXTRA, LANES), 0)

    def extra(row):
        return jnp.where(sub == 0, near, jnp.where(sub == 1, far, jnp.where(sub == 2, row, 0.0)))

    for tile in range(TILES):
        state = ends[tile * MODES : (tile + 1) * MODES, :]
        adjoint = adj[tile * MODES : (tile + 1) * MODES, :]
        msg[2 * tile, 0:MODES, :] = join(state, swap(adjoint))
        msg[2 * tile + 1, 0:MODES, :] = join(swap(state), adjoint)
        msg[2 * tile, MODES:, :] = extra(even[tile : tile + 1, :])
        msg[2 * tile + 1, MODES:, :] = extra(odd[tile : tile + 1, :])


def carry_kernel(span, own, msg, rates, weights, gain, out, carries):
    count = msg.shape[0]
    tile = own[0] // 2
    odd = own[0] % 2 == 1
    tiles = gain.shape[0]

    def mine(value):
        other = swap(value)
        return jnp.where(odd, join(other, value), join(value, other))

    rate = mine(rates[pl.ds(tile, MODES, stride=tiles), :])
    weight = mine(weights[pl.ds(tile, MODES, stride=tiles), :])
    gains = mine(gain[pl.ds(tile, 1), :])
    single = jnp.exp(-rate)
    whole = jnp.exp(-rate * float(span))
    state = jnp.zeros((MODES, LANES), f32)
    before = None
    for m in range(count):
        fresh = join(msg[m, 0:MODES, :], msg[count - 1 - m, 0:MODES, :])
        near = join(msg[m, MODES : MODES + 1, :], msg[count - 1 - m, MODES : MODES + 1, :])
        far = join(msg[m, MODES + 1 : MODES + 2, :], msg[count - 1 - m, MODES + 1 : MODES + 2, :])
        if before is None:
            carries[m] = state
            state = fresh
        else:
            carries[m] = jnp.where(near == before, state, 0.0)
            state = fresh + jnp.where(far == before, whole * state, 0.0)
        before = far
    total = jnp.zeros((MODES, LANES), f32)
    row = jnp.zeros((1, LANES), f32)
    for i in range(count):
        carried = join(carries[i], carries[count - 1 - i])
        out[i, 0:MODES, :] = carried
        total = total + carried * swap(msg[i, 0:MODES, :])
        row = row + msg[i, MODES + 2 : MODES + 3, :]
    total = total * single
    gain_row = jnp.sum(weight * total, axis=0, keepdims=True)
    spread = jnp.dot(total * gains, block_ones(), precision=HIGHEST, preferred_element_type=f32)
    pick = lane_iota(MODES) % GROUP == lax.broadcasted_iota(jnp.int32, (MODES, LANES), 0)
    mode_row = jnp.sum(jnp.where(pick, spread, 0.0), axis=0, keepdims=True)
    row = row + join(gain_row, swap(mode_row))
    for i in range(count):
        out[i, MODES:, :] = jnp.broadcast_to(row, (EXTRA, LANES))


def load_carry(back, ends, ahead):
    for tile in range(TILES):
        low = back[2 * tile, 0:MODES, :]
        high = back[2 * tile + 1, 0:MODES, :]
        value = join(swap(low), high) if ahead else join(low, swap(high))
        ends[tile * MODES : (tile + 1) * MODES, :] = value
    return tuple(ends[pl.ds(r, TILES, stride=MODES), :] for r in range(MODES))


def backward_kernel(
    seg, back, feats, gate, grad, rates, weights, gain, scaled, inner, grad_scan, result, ends
):
    length = gate.shape[0]
    for tile in range(TILES):
        to_scan(grad_scan, tile, tile_of(gate, tile) * tile_of(grad, tile), length)
    decay = [jnp.exp(-rates[r]) for r in range(MODES)]
    weight = [weights[r] for r in range(MODES)]

    def step(t, states, keep):
        value = row_at(grad_scan, t)
        states = tuple(decayed(decay[r], states[r], keep) + value for r in range(MODES))
        result[pl.ds(pl.multiple_of(t * TILES, TILES), TILES), :] = tree(
            [weight[r] * states[r] for r in range(MODES)]
        )
        return states

    scan(length, seg, step, load_carry(back, ends, True), True)
    partial = jnp.zeros((length, LANES), f32)
    for tile in range(TILES):
        value = from_scan(result, tile, length) * gain[tile : tile + 1, :]
        scaled[:, tile * LANES : (tile + 1) * LANES] = value
        partial = partial + value * tile_of(feats, tile)
    row = lax.dot_general(
        jnp.ones((8, LANES), f32),
        partial,
        (((1,), (1,)), ((), ())),
        precision=HIGHEST,
        preferred_element_type=f32,
    )

    @pl.when(pl.program_id(0) == 0)
    def _():
        inner[...] = row

    @pl.when(pl.program_id(0) != 0)
    def _():
        inner[...] += row


def forward_kernel(
    seg, back, feats, gate, grad, inverse, rates, weights, gain, mixed, grad_gate, feat_scan, result, ends
):
    length = gate.shape[0]
    scale = column(inverse, length)
    for tile in range(TILES):
        to_scan(feat_scan, tile, tile_of(feats, tile) * scale, length)
    decay = [jnp.exp(-rates[r]) for r in range(MODES)]
    weight = [weights[r] for r in range(MODES)]

    def step(t, states, keep):
        value = row_at(feat_scan, t)
        states = tuple(decayed(decay[r], states[r], keep) + value for r in range(MODES))
        result[pl.ds(pl.multiple_of(t * TILES, TILES), TILES), :] = tree(
            [weight[r] * states[r] for r in range(MODES)]
        )
        return states

    scan(length, seg, step, load_carry(back, ends, False), False)
    for tile in range(TILES):
        conv = from_scan(result, tile, length) * gain[tile : tile + 1, :]
        at = slice(tile * LANES, (tile + 1) * LANES)
        mixed[:, at] = (tile_of(gate, tile) * conv).astype(jnp.bfloat16)
        grad_gate[:, at] = (tile_of(grad, tile) * conv).astype(jnp.bfloat16)


def feature_kernel(full_width, scaled, feats, inverse, inner, out):
    length = feats.shape[0]
    scale = column(inverse, length)
    factor = column(inner, length) * scale * scale / full_width
    for tile in range(feats.shape[1] // LANES):
        at = slice(tile * LANES, (tile + 1) * LANES)
        out[:, at] = (scale * (scaled[:, at] - tile_of(feats, tile) * factor)).astype(jnp.bfloat16)


def params():
    return pltpu.CompilerParams(vmem_limit_bytes=24 * 1024 * 1024)


def cost(flops, moved):
    return pl.CostEstimate(flops=flops, bytes_accessed=moved, transcendentals=0)


def sum_tensor(value):
    size = lax.axis_size("tensor")
    total = value
    for d in range(1, size):
        total = total + lax.ppermute(value, "tensor", [(i, (i + d) % size) for i in range(size)])
    return total


def shards(features, gate_in, segments, gain, residue, rates, grad_out):
    _, length, width = features.shape
    group_count, mode_count = rates.shape
    count = lax.axis_size("ctx")
    full_width = width * lax.axis_size("tensor")
    tiles = width // LANES
    halves = tiles // TILES
    half = TILES * LANES
    feat2 = features[0]
    gate2 = gate_in[0]
    grad2 = grad_out[0]

    feats = features.astype(f32)
    square_sum = sum_tensor(jnp.sum(feats * feats, axis=2))
    inverse = lax.rsqrt(square_sum / full_width + epsilon)

    root_weight = jnp.sqrt(-jnp.expm1(-2.0 * rates))
    tables = jnp.stack([rates, residue * root_weight])
    tables = jnp.transpose(tables, (0, 2, 1)).reshape(2, mode_count, tiles, LANES // GROUP)
    tables = jnp.broadcast_to(tables[..., None], tables.shape + (GROUP,))
    tables = tables.reshape(2, mode_count, tiles, LANES)
    rate_table, weight_table = tables[0], tables[1]
    gain_table = gain.reshape(tiles, LANES)

    whole = pl.BlockSpec((length, half), lambda h: (0, h))
    table = pl.BlockSpec((mode_count, TILES, LANES), lambda h: (0, h, 0))
    gains = pl.BlockSpec((TILES, LANES), lambda h: (h, 0))
    states = pl.BlockSpec((TILES * MODES, LANES), lambda h: (h, 0))
    message = pl.BlockSpec((2 * TILES, MODES + EXTRA, LANES), lambda h: (h, 0, 0))
    vector = pl.BlockSpec((1, length), lambda h: (0, 0))
    ids = pl.BlockSpec(memory_space=pltpu.SMEM)
    scan_scratch = pltpu.VMEM((length * TILES, LANES), f32)
    state_scratch = pltpu.VMEM((TILES * MODES, LANES), f32)
    work = length * width * MODES

    adjoint = pl.pallas_call(
        adjoint_kernel,
        grid=(halves,),
        in_specs=[ids, whole, whole, table],
        out_specs=states,
        out_shape=jax.ShapeDtypeStruct((tiles * MODES, LANES), f32),
        scratch_shapes=[scan_scratch],
        compiler_params=params(),
        cost_estimate=cost(2 * work, 4 * length * width),
        name="adjoint",
    )(segments, gate2, grad2, rate_table)

    msg = pl.pallas_call(
        state_kernel,
        grid=(halves,),
        in_specs=[ids, whole, whole, whole, vector, table, table, gains, states],
        out_specs=message,
        out_shape=jax.ShapeDtypeStruct((count, MODES + EXTRA, LANES), f32),
        scratch_shapes=[scan_scratch, scan_scratch, state_scratch, state_scratch],
        compiler_params=params(),
        cost_estimate=cost(4 * work, 6 * length * width),
        name="states",
    )(segments, feat2, gate2, grad2, inverse, rate_table, weight_table, gain_table, adjoint)

    msg = lax.all_to_all(msg, "ctx", 0, 0, tiled=True)

    own = lax.axis_index("ctx").astype(jnp.int32).reshape(1)
    vmem = pl.BlockSpec(memory_space=pltpu.VMEM)
    flat = (mode_count * tiles, LANES)
    back = pl.pallas_call(
        lambda *refs: carry_kernel(length, *refs),
        in_specs=[ids, vmem, vmem, vmem, vmem],
        out_specs=vmem,
        out_shape=jax.ShapeDtypeStruct((count, MODES + EXTRA, LANES), f32),
        scratch_shapes=[pltpu.VMEM((count, MODES, LANES), f32)],
        compiler_params=params(),
        name="carries",
    )(own, msg, rate_table.reshape(flat), weight_table.reshape(flat), gain_table)

    back = lax.all_to_all(back, "ctx", 0, 0, tiled=True)

    scaled, inner = pl.pallas_call(
        backward_kernel,
        grid=(halves,),
        in_specs=[ids, message, whole, whole, whole, table, table, gains],
        out_specs=[whole, pl.BlockSpec((8, length), lambda h: (0, 0))],
        out_shape=[
            jax.ShapeDtypeStruct((length, width), f32),
            jax.ShapeDtypeStruct((8, length), f32),
        ],
        scratch_shapes=[scan_scratch, scan_scratch, state_scratch],
        compiler_params=params(),
        cost_estimate=cost(4 * work, 10 * length * width),
        name="backward",
    )(segments, back, feat2, gate2, grad2, rate_table, weight_table, gain_table)
    inner = sum_tensor(inner[0:1])

    mixed, grad_gate = pl.pallas_call(
        forward_kernel,
        grid=(halves,),
        in_specs=[ids, message, whole, whole, whole, vector, table, table, gains],
        out_specs=[whole, whole],
        out_shape=[jax.ShapeDtypeStruct((length, width), jnp.bfloat16)] * 2,
        scratch_shapes=[scan_scratch, scan_scratch, state_scratch],
        compiler_params=params(),
        cost_estimate=cost(4 * work, 10 * length * width),
        name="forward",
    )(segments, back, feat2, gate2, grad2, inverse, rate_table, weight_table, gain_table)

    grad_features = pl.pallas_call(
        lambda *refs: feature_kernel(full_width, *refs),
        grid=(halves,),
        in_specs=[whole, whole, vector, vector],
        out_specs=whole,
        out_shape=jax.ShapeDtypeStruct((length, width), jnp.bfloat16),
        compiler_params=params(),
        cost_estimate=cost(4 * length * width, 8 * length * width),
        name="features",
    )(scaled, feat2, inverse, inner)

    totals = back[:, MODES, :]
    size = lax.axis_size("dp")
    for d in range(1, size):
        totals = totals + lax.ppermute(
            back[:, MODES, :], "dp", [(i, (i + d) % size) for i in range(size)]
        )
    norm_factor = 1.0 / math.sqrt(size * length * count)
    grad_gain = totals[:, : LANES // 2].reshape(width) * norm_factor
    mode_total = totals[:, LANES // 2 :].reshape(group_count, mode_count)
    return (
        mixed[None],
        grad_features[None],
        grad_gate[None],
        mode_total * root_weight * norm_factor,
        grad_gain,
    )


def solution(mesh):
    placed = (
        P("dp", "ctx", "tensor"),
        P("dp", "ctx", "tensor"),
        P("dp", "ctx"),
        P("tensor"),
        P("tensor", None),
        P("tensor", None),
        P("dp", "ctx", "tensor"),
    )
    return jax.shard_map(
        shards,
        mesh=mesh,
        in_specs=placed,
        out_specs=(
            P("dp", "ctx", "tensor"),
            P("dp", "ctx", "tensor"),
            P("dp", "ctx", "tensor"),
            P("tensor", None),
            P("tensor"),
        ),
        check_vma=False,
    )
```

time: 669 us -> 100 us (0.15)
  the two profiles are of different devices: /device:TPU:136 before, /device:TPU:1 now
where the time goes in v1:
time: 100 us; the launch traced here: 99.7 us
  Pallas kernels  33.1 us (33%)
  starting transfers between devices  24.4 us (24%)
  blocking collectives  17.9 us (18%)
  local copies, waits for them, and re-layouts  10.6 us (11%)
  waiting for transfers between devices  9.19 us (9%)
  other arithmetic  3.69 us (4%)
    all_to_all x1, blocking collectives, shards(): back = lax.all_to_all(back, 'ctx', 0, 0, tiled=True)  17.9 us
    all_to_all x1, starting transfers between devices, shards(): msg = lax.all_to_all(msg, 'ctx', 0, 0, tiled=True)  11.1 us
    all_to_all x1, waiting for transfers between devices, shards(): msg = lax.all_to_all(msg, 'ctx', 0, 0, tiled=True)  9.17 us
    ppermute x6, starting transfers between devices, sum_tensor(): lax.ppermute(value, 'tensor', [(i, (i + d) % size) for i in range(size)])  8.86 us
    pallas_call x1, Pallas kernels, shards(): pl.pallas_call(forward_kernel, grid=(halves,), in_specs=[ids, message, wh...  8.85 us
    pallas_call x1, Pallas kernels, shards(): pl.pallas_call(state_kernel, grid=(halves,), in_specs=[ids, whole, whole,...  8.3 us
    pallas_call x1, Pallas kernels, shards(): pl.pallas_call(backward_kernel, grid=(halves,), in_specs=[ids, message, w...  7.96 us
    broadcast_in_dim x6, local copies, waits for them, and re-layouts, shards(): tables = jnp.broadcast_to(tables[..., None], tables.shape + (GROUP,))  7.19 us
  transfers between devices with their start and end apart: 8, of which 1 were waited for; matrix products, arithmetic and copies ran while one was open for 9% of the time, Pallas kernels for 15%

profile of v1, /device:TPU:1, one launch (start us, length us, event | category | flops | bytes accessed | tf_op | source)
XLA Modules:
  0.0 99.7 jit_solution(15685964040956177466)
XLA Ops:
  0.6 1.5 %multiply_reduce_fusion = f32[256]{0:T(256)S(1)} fusion(bf16[1,256,2048]{2,1,0:T(8,128)(2,1)} %param.7), kind=kLoop, calls=%fused_computation | loop fusion | flops 1572608 | bytes 1049600 | tf_op jit(solution)/shard_map/reduce_sum | solution.py:329
  2.1 2.2 %collective-permute-start = (f32[1,256]{1,0:T(1,128)S(1)}, f32[1,256]{1,0:T(1,128)S(1)}, u32[]{:S(2)}, u32[]{:S(2)}) collective-permute-start(f32[1,256]{1,0:T(1,128)S(1)} %bitcast.47), channel_id=1, source_target_pairs={{0,1},{1,2},{2,3},{3,0},{4,5},{5,6},{6,7},{7,4},{8,9},{9,10},{10,1... | collective-permute-start | bytes 3080 | tf_op jit(solution)/shard_map/ppermute | solution.py:312
  4.3 2.6 %collective-permute-start.1 = (f32[1,256]{1,0:T(1,128)S(1)}, f32[1,256]{1,0:T(1,128)S(1)}, u32[]{:S(2)}, u32[]{:S(2)}) collective-permute-start(f32[1,256]{1,0:T(1,128)S(1)} %bitcast.48), channel_id=1, source_target_pairs={{0,2},{1,3},{2,0},{3,1},{4,6},{5,7},{6,4},{7,5},{8,10},{9,11},{10,... | collective-permute-start | bytes 3080 | tf_op jit(solution)/shard_map/ppermute | solution.py:312
  7.0 1.1 %collective-permute-start.2 = (f32[1,256]{1,0:T(1,128)S(1)}, f32[1,256]{1,0:T(1,128)S(1)}, u32[]{:S(2)}, u32[]{:S(2)}) collective-permute-start(f32[1,256]{1,0:T(1,128)S(1)} %bitcast.49), channel_id=1, source_target_pairs={{0,3},{1,0},{2,1},{3,2},{4,7},{5,4},{6,5},{7,6},{8,11},{9,8},{10,9... | collective-permute-start | bytes 3080 | tf_op jit(solution)/shard_map/ppermute | solution.py:312
  8.0 0.7 multiply_bitcast_fusion
  8.8 0.7 maximum_bitcast_fusion
  11.2 1.3 %broadcast_in_dim.26 = f32[16,16,8,16]{3,2,1,0:T(8,128)} broadcast(f32[16,16,8]{2,1,0:T(8,128)S(1)} %copy.38), dimensions={0,1,2} | broadcast | bytes 139264 | tf_op jit(solution)/shard_map/broadcast_in_dim | solution.py:335
  12.5 1.5 %broadcast_in_dim.27.weights = f32[16,16,128]{2,1,0:T(8,128)S(1)} reshape(f32[16,16,8,16]{3,2,1,0:T(8,128)} %broadcast_in_dim.26) | data formatting | bytes 262144 | tf_op jit(solution)/shard_map/broadcast_in_dim | solution.py:335
  14.0 4.7 %adjoint.1.adj = f32[256,128]{1,0:T(8,128)S(1)} custom-call(s32[1,256]{1,0:T(1,128)S(1)} %copy-done.6, bf16[256,2048]{1,0:T(8,128)(2,1)S(1)} %bitcast.29, bf16[256,2048]{1,0:T(8,128)(2,1)S(1)} %bitcast.33, f32[16,16,128]{2,1,0:T(8,128)S(1)} %broadcast_in_dim.25.rates), custom_call_target="tpu_custom_call" | custom-call | flops 16777216 | bytes 2097152 | tf_op jit(solution)/shard_map/adjoint/pallas_call | solution.py:351
  18.8 8.3 %states.1 = f32[32,24,128]{2,1,0:T(8,128)S(1)} custom-call(s32[1,256]{1,0:T(1,128)S(1)} %copy-done.6, bf16[256,2048]{1,0:T(8,128)(2,1)S(1)} %bitcast.25, bf16[256,2048]{1,0:T(8,128)(2,1)S(1)} %bitcast.30, bf16[256,2048]{1,0:T(8,128)(2,1)S(1)} %bitcast.34, f32[1,256]{1,0:T(1,128)S(1)} %add_rsqrt_fusion.inverse.refs_2_, ...), custom_call_target="tpu_custom_call" | custom-call | flops 33554432 | bytes 3145728 | tf_op jit(solution)/shard_map/states/pallas_call | solution.py:363
  27.1 0.7 copy-done.3
  27.9 11.1 %all-to-all-start = ((f32[32,24,128]{2,1,0:T(8,128)}), f32[32,24,128]{2,1,0:T(8,128)}, u32[]{:S(2)}, u32[]{:S(2)}) async-start(f32[32,24,128]{2,1,0:T(8,128)} %copy-done.3), calls=%async_computation | async-start | bytes 786432 | tf_op jit(solution)/shard_map/all_to_all | solution.py:375
  39.0 1.5 %broadcast_in_dim.28.refs_2_ = f32[256,128]{1,0:T(8,128)S(1)} reshape(f32[16,16,8,16]{3,2,1,0:T(8,128)} %copy-done.7) | data formatting | bytes 262144 | tf_op jit(solution)/shard_map/broadcast_in_dim | solution.py:335
  40.5 2.2 %broadcast_in_dim.29.refs_3_ = f32[256,128]{1,0:T(8,128)} reshape(f32[16,16,8,16]{3,2,1,0:T(8,128)} %broadcast_in_dim.26) | data formatting | bytes 262144 | tf_op jit(solution)/shard_map/broadcast_in_dim | solution.py:335
  42.7 9.2 %all-to-all-done.refs_1_ = f32[32,24,128]{2,1,0:T(8,128)} async-done(((f32[32,24,128]{2,1,0:T(8,128)}), f32[32,24,128]{2,1,0:T(8,128)}, u32[]{:S(2)}, u32[]{:S(2)}) %all-to-all-start) | async-done | bytes 393248 | tf_op jit(solution)/shard_map/all_to_all | solution.py:375
  51.9 0.9 copy-done.4
  52.8 1.5 %carries.1 = f32[32,24,128]{2,1,0:T(8,128)S(1)} custom-call(s32[1]{0:T(128)} %bitcast.refs_0_, f32[32,24,128]{2,1,0:T(8,128)} %all-to-all-done.refs_1_, f32[256,128]{1,0:T(8,128)S(1)} %broadcast_in_dim.28.refs_2_, f32[256,128]{1,0:T(8,128)S(1)} %copy-done.4, f32[16,128]{1,0:T(8,128)S(1)} %bitcast.38), custom_call_target="tpu_custom_call" | custom-call | tf_op jit(solution)/shard_map/carries/pallas_call | solution.py:380
  54.3 17.9 %all_to_all.10.back = f32[32,24,128]{2,1,0:T(8,128)S(1)} all-to-all(f32[32,24,128]{2,1,0:T(8,128)S(1)} %carries.1), channel_id=1, replica_groups=mesh['dp'=2,'ctx'=32,'tensor'=4] {'ctx'}, dimensions={0} | all-to-all | bytes 786432 | tf_op jit(solution)/shard_map/all_to_all | solution.py:390
  72.2 8.0 %backward.1 = (f32[256,2048]{1,0:T(8,128)S(1)}, f32[8,256]{1,0:T(8,128)S(1)}) custom-call(s32[1,256]{1,0:T(1,128)S(1)} %copy-done.6, f32[32,24,128]{2,1,0:T(8,128)S(1)} %all_to_all.10.back, bf16[256,2048]{1,0:T(8,128)(2,1)S(1)} %bitcast.26, bf16[256,2048]{1,0:T(8,128)(2,1)S(1)} %bitcast.31, bf16[256,2048]{1,0:T(8,128)(2,1)S(1)} %bitcast.35, ...), custom_call_target="tpu_custom_call" | custom-call | flops 33554432 | bytes 5242880 | tf_op jit(solution)/shard_map/backward/pallas_call | solution.py:392
  80.6 0.9 collective-permute-start.4
  81.6 1.6 %collective-permute-start.5 = (f32[1,256]{1,0:T(1,128)S(1)}, f32[1,256]{1,0:T(1,128)S(1)}, u32[]{:S(2)}, u32[]{:S(2)}) collective-permute-start(f32[1,256]{1,0:T(1,128)S(1)} %slice.35), channel_id=1, source_target_pairs={{0,3},{1,0},{2,1},{3,2},{4,7},{5,4},{6,5},{7,6},{8,11},{9,8},{10,9... | collective-permute-start | bytes 3080 | tf_op jit(solution)/shard_map/ppermute | solution.py:312
  83.1 4.4 %collective-permute-start.6 = (f32[32,128]{1,0:T(8,128)S(1)}, f32[32,128]{1,0:T(8,128)S(1)}, u32[]{:S(2)}, u32[]{:S(2)}) collective-permute-start(f32[32,128]{1,0:T(8,128)S(1)} %bitcast.45), channel_id=1, source_target_pairs={{0,128},{128,0},{1,129},{129,1},{2,130},{130,2},{3,131},{131,3},{4... | collective-permute-start | bytes 49160 | tf_op jit(solution)/shard_map/ppermute | solution.py:434
  87.5 8.8 %forward.1 = (bf16[256,2048]{1,0:T(8,128)(2,1)}, bf16[256,2048]{1,0:T(8,128)(2,1)}) custom-call(s32[1,256]{1,0:T(1,128)S(1)} %copy-done.6, f32[32,24,128]{2,1,0:T(8,128)S(1)} %all_to_all.10.back, bf16[256,2048]{1,0:T(8,128)(2,1)S(1)} %bitcast.27, bf16[256,2048]{1,0:T(8,128)(2,1)S(1)} %bitcast.32, bf16[256,2048]{1,0:T(8,128)(2,1)S(1)} %bitcast.36, ...), custom_call_target="tpu_custom_call" | custom-call | flops 33554432 | bytes 5242880 | tf_op jit(solution)/shard_map/forward/pallas_call | solution.py:408
  96.4 1.8 %features.1 = bf16[256,2048]{1,0:T(8,128)(2,1)} custom-call(f32[256,2048]{1,0:T(8,128)S(1)} %get-tuple-element.10.refs_0_, bf16[256,2048]{1,0:T(8,128)(2,1)S(1)} %bitcast.28, f32[1,256]{1,0:T(1,128)S(1)} %add_rsqrt_fusion.inverse.refs_2_, f32[1,256]{1,0:T(1,128)S(1)} %add_add_fusion.refs_3_), custom_call_target="tpu_custom_call" | custom-call | flops 2097152 | bytes 4194304 | tf_op jit(solution)/shard_map/features/pallas_call | solution.py:420
  (41 shorter events, 3.7 us)
Async XLA Ops:
  2.1 16.6 %collective-permute-start = (f32[1,256]{1,0:T(1,128)S(1)}, f32[1,256]{1,0:T(1,128)S(1)}, u32[]{:S(2)}, u32[]{:S(2)}) collective-permute-start(f32[1,256]{1,0:T(1,128)S(1)} %bitcast.47), channel_id=1, source_target_pairs={{0,1},{1,2},{2,3},{3,0},{4,5},{5,6},{6,7},{7,4},{8,9},{9,10},{10,1... | collective-permute-start | bytes 3080 | tf_op jit(solution)/shard_map/ppermute | solution.py:312
  4.3 14.4 %collective-permute-start.1 = (f32[1,256]{1,0:T(1,128)S(1)}, f32[1,256]{1,0:T(1,128)S(1)}, u32[]{:S(2)}, u32[]{:S(2)}) collective-permute-start(f32[1,256]{1,0:T(1,128)S(1)} %bitcast.48), channel_id=1, source_target_pairs={{0,2},{1,3},{2,0},{3,1},{4,6},{5,7},{6,4},{7,5},{8,10},{9,11},{10,... | collective-permute-start | bytes 3080 | tf_op jit(solution)/shard_map/ppermute | solution.py:312
  7.0 11.8 %collective-permute-start.2 = (f32[1,256]{1,0:T(1,128)S(1)}, f32[1,256]{1,0:T(1,128)S(1)}, u32[]{:S(2)}, u32[]{:S(2)}) collective-permute-start(f32[1,256]{1,0:T(1,128)S(1)} %bitcast.49), channel_id=1, source_target_pairs={{0,3},{1,0},{2,1},{3,2},{4,7},{5,4},{6,5},{7,6},{8,11},{9,8},{10,9... | collective-permute-start | bytes 3080 | tf_op jit(solution)/shard_map/ppermute | solution.py:312
  10.0 1.0 copy-start.7
  10.1 3.9 %copy-start.1 = (bf16[1,256,2048]{2,1,0:T(8,128)(2,1)S(1)}, bf16[1,256,2048]{2,1,0:T(8,128)(2,1)}, u32[]{:S(2)}) copy-start(bf16[1,256,2048]{2,1,0:T(8,128)(2,1)} %param.8) | copy-start | bytes 3145732
  10.1 3.9 %copy-start.2 = (bf16[1,256,2048]{2,1,0:T(8,128)(2,1)S(1)}, bf16[1,256,2048]{2,1,0:T(8,128)(2,1)}, u32[]{:S(2)}) copy-start(bf16[1,256,2048]{2,1,0:T(8,128)(2,1)} %param.13) | copy-start | bytes 3145732
  10.1 3.9 %copy-start.6 = (s32[1,256]{1,0:T(1,128)S(1)}, s32[1,256]{1,0:T(1,128)}, u32[]{:S(2)}) copy-start(s32[1,256]{1,0:T(1,128)} %seg.7) | copy-start | bytes 3076
  11.1 7.7 %copy-start = (bf16[1,256,2048]{2,1,0:T(8,128)(2,1)S(1)}, bf16[1,256,2048]{2,1,0:T(8,128)(2,1)}, u32[]{:S(2)}) copy-start(bf16[1,256,2048]{2,1,0:T(8,128)(2,1)} %param.7) | copy-start | bytes 3145732
  11.1 7.7 %copy-start.5 = (f32[2048]{0:T(1024)S(1)}, f32[2048]{0:T(1024)}, u32[]{:S(2)}) copy-start(f32[2048]{0:T(1024)} %param.10) | copy-start | bytes 24580
  27.1 0.8 copy-start.3
  27.9 24.0 %all-to-all-start = ((f32[32,24,128]{2,1,0:T(8,128)}), f32[32,24,128]{2,1,0:T(8,128)}, u32[]{:S(2)}, u32[]{:S(2)}) async-start(f32[32,24,128]{2,1,0:T(8,128)} %copy-done.3), calls=%async_computation | async-start | bytes 786432 | tf_op jit(solution)/shard_map/all_to_all | solution.py:375
  51.9 0.9 copy-start.4
  80.1 16.2 %collective-permute-start.3 = (f32[1,256]{1,0:T(1,128)S(1)}, f32[1,256]{1,0:T(1,128)S(1)}, u32[]{:S(2)}, u32[]{:S(2)}) collective-permute-start(f32[1,256]{1,0:T(1,128)S(1)} %slice.35), channel_id=1, source_target_pairs={{0,1},{1,2},{2,3},{3,0},{4,5},{5,6},{6,7},{7,4},{8,9},{9,10},{10,1... | collective-permute-start | bytes 3080 | tf_op jit(solution)/shard_map/ppermute | solution.py:312
  80.6 15.7 %collective-permute-start.4 = (f32[1,256]{1,0:T(1,128)S(1)}, f32[1,256]{1,0:T(1,128)S(1)}, u32[]{:S(2)}, u32[]{:S(2)}) collective-permute-start(f32[1,256]{1,0:T(1,128)S(1)} %slice.35), channel_id=1, source_target_pairs={{0,2},{1,3},{2,0},{3,1},{4,6},{5,7},{6,4},{7,5},{8,10},{9,11},{10,... | collective-permute-start | bytes 3080 | tf_op jit(solution)/shard_map/ppermute | solution.py:312
  81.6 14.8 %collective-permute-start.5 = (f32[1,256]{1,0:T(1,128)S(1)}, f32[1,256]{1,0:T(1,128)S(1)}, u32[]{:S(2)}, u32[]{:S(2)}) collective-permute-start(f32[1,256]{1,0:T(1,128)S(1)} %slice.35), channel_id=1, source_target_pairs={{0,3},{1,0},{2,1},{3,2},{4,7},{5,4},{6,5},{7,6},{8,11},{9,8},{10,9... | collective-permute-start | bytes 3080 | tf_op jit(solution)/shard_map/ppermute | solution.py:312
  83.1 15.1 %collective-permute-start.6 = (f32[32,128]{1,0:T(8,128)S(1)}, f32[32,128]{1,0:T(8,128)S(1)}, u32[]{:S(2)}, u32[]{:S(2)}) collective-permute-start(f32[32,128]{1,0:T(8,128)S(1)} %bitcast.45), channel_id=1, source_target_pairs={{0,128},{128,0},{1,129},{129,1},{2,130},{130,2},{3,131},{131,3},{4... | collective-permute-start | bytes 49160 | tf_op jit(solution)/shard_map/ppermute | solution.py:434
  96.4 2.0 %copy-start.8 = (f32[128,16]{0,1:T(8,128)S(1)}, f32[128,16]{0,1:T(8,128)}, u32[]{:S(2)}) copy-start(f32[128,16]{0,1:T(8,128)} %param.12) | copy-start | bytes 24580

commit v2 on v0

v2 whole, which is shorter than its diff:
```python
import math

import jax
import jax.numpy as jnp
from jax import lax
from jax.experimental import pallas as pl
from jax.experimental.pallas import tpu as pltpu
from jax.sharding import PartitionSpec as P

epsilon = 1e-06
LANES = 128
TILES = 8
HALVES = 2
MODES = 16
GROUP = 16
UNROLL = 16
COUNT = 4
COPIES = 8
WIDE = 2 * LANES
EXTRA = 8
HIGHEST = lax.Precision.HIGHEST
f32 = jnp.float32


def lane_iota(rows):
    return lax.broadcasted_iota(jnp.int32, (rows, LANES), 1)


def swap(value):
    return pltpu.roll(value, LANES // 2, axis=1)


def join(low, high):
    return jnp.where(lane_iota(low.shape[0]) < LANES // 2, low, high)


def total_row(parts):
    return tree([part[...] for part in parts])


def inverse_of(parts, full_width):
    return lax.rsqrt(total_row(parts) / full_width + epsilon)


def column(row):
    length = row.shape[1]
    row = jnp.broadcast_to(row, (8, length))
    return jnp.broadcast_to(jnp.transpose(row)[:, 0:1], (length, LANES))


def block_ones():
    left = lax.broadcasted_iota(jnp.int32, (LANES, LANES), 0) // GROUP
    right = lax.broadcasted_iota(jnp.int32, (LANES, LANES), 1) // GROUP
    return jnp.where(left == right, 1.0, 0.0).astype(f32)


def lanes_of(half, tile):
    return pl.ds(pl.multiple_of((half * TILES + tile) * LANES, LANES), LANES)


def tile_of(ref, half, tile):
    return ref[:, lanes_of(half, tile)].astype(f32)


def scan_rows(half, tile, length):
    return pl.ds(half * length * TILES + tile, length, stride=TILES)


def table_of(table, half, first):
    at = pl.ds(pl.multiple_of(half * TILES, TILES), TILES)
    return [table[first + r, at, :] for r in range(MODES)]


def decay_of(table, half):
    return [jnp.exp(-rate) for rate in table_of(table, half, 0)]


def weight_of(table, half):
    return table_of(table, half, MODES)


def state_rows(half, r):
    return pl.ds(half * TILES * MODES + r, TILES, stride=MODES)


def tree(values):
    values = list(values)
    while len(values) > 1:
        values = [a + b for a, b in zip(values[::2], values[1::2])]
    return values[0]


def scan(length, seg, cuts, step, carry, backward):
    groups = length // UNROLL

    def run(group, carry, masked):
        base = group * UNROLL
        for u in range(UNROLL):
            t = base + (UNROLL - 1 - u if backward else u)
            keep = None
            if masked:
                near = jnp.minimum(t + 1, length - 1) if backward else jnp.maximum(t - 1, 0)
                keep = seg[0, t] == seg[0, near]
            carry = step(t, carry, keep)
        return carry

    def stretch(p, carry):
        now, states = carry
        if backward:
            cut = jnp.where(p < COUNT - 1, cuts[jnp.maximum(COUNT - 2 - p, 0)], 0)
            group = (cut - 1) // UNROLL
            stop = jnp.where(
                cut >= length, now, jnp.where(cut <= 0, 0, jnp.minimum(now, group + 1))
            )
            states = lax.fori_loop(
                0, now - stop, lambda i, value: run(now - 1 - i, value, False), states
            )
            broken = (cut > 0) & (cut < length) & (group < now)
            after = group
        else:
            cut = jnp.where(p < COUNT - 1, cuts[jnp.minimum(p, COUNT - 2)], length)
            group = cut // UNROLL
            stop = jnp.where(
                cut <= 0, now, jnp.where(cut >= length, groups, jnp.maximum(now, group))
            )
            states = lax.fori_loop(now, stop, lambda i, value: run(i, value, False), states)
            broken = (cut > 0) & (cut < length) & (group >= now)
            after = group + 1
        states = lax.cond(
            broken, lambda value: run(group, value, True), lambda value: value, states
        )
        return jnp.where(broken, after, stop), states

    start = jnp.int32(groups if backward else 0)
    return lax.fori_loop(0, COUNT, stretch, (start, carry))[1]


def decayed(decay, state, keep):
    state = decay * state
    return state if keep is None else jnp.where(keep, state, 0.0)


def row_at(ref, half, length, t):
    return ref[pl.ds(pl.multiple_of((half * length + t) * TILES, TILES), TILES), :]


def lane_sums(value):
    return lax.dot_general(
        jnp.ones((8, LANES), f32),
        value,
        (((1,), (1,)), ((), ())),
        precision=HIGHEST,
        preferred_element_type=f32,
    )[0:1]


def load_kernel(
    feats_in, gate_in, grad_in, rates_in, residue_in, seg_in,
    feats, grad_scan, squares, table, cuts,
    gate, grad, rates, residue, seg, sems, small_sems,
):
    length, width = feats.shape
    step = length // COPIES
    small = [
        pltpu.make_async_copy(src, dst, small_sems.at[n])
        for n, (src, dst) in enumerate(((rates_in, rates), (residue_in, residue), (seg_in, seg)))
    ]
    copies = []
    for n, (src, dst) in enumerate(((feats_in, feats), (gate_in, gate), (grad_in, grad))):
        for i in range(COPIES):
            at = pl.ds(i * step, step)
            copies.append(pltpu.make_async_copy(src.at[at, :], dst.at[at, :], sems.at[n, i]))
    for copy in small + copies:
        copy.start()
    for copy in small:
        copy.wait()
    expand(rates, residue, seg, table, cuts)
    for i in range(COPIES):
        copies[i].wait()
    partial = jnp.zeros((length, LANES), f32)
    for tile in range(width // LANES):
        value = tile_of(feats, 0, tile)
        partial = partial + value * value
    squares[...] = lane_sums(partial)
    for copy in copies[COPIES:]:
        copy.wait()
    for half in range(HALVES):
        for tile in range(TILES):
            value = tile_of(gate, half, tile) * tile_of(grad, half, tile)
            grad_scan[scan_rows(half, tile, length), :] = value


def mode_params(rates, residue):
    rate = rates[...]
    twice = 2.0 * rate
    series = 1.0 - twice / 6.0
    for n in (5, 4, 3, 2):
        series = 1.0 - twice / n * series
    root = jnp.sqrt(jnp.where(twice < 0.25, twice * series, 1.0 - jnp.exp(-twice)))
    return jnp.concatenate([rate, residue[...] * root, root], axis=0)


def spread_groups(packed, width, first):
    group_count = packed.shape[1]
    group = lax.broadcasted_iota(jnp.int32, (group_count, width), 0)
    lane = lax.broadcasted_iota(jnp.int32, (group_count, width), 1)
    spread = jnp.where(first(lane) == group, 1.0, 0.0).astype(f32)
    return jnp.dot(packed, spread, precision=HIGHEST, preferred_element_type=f32)


def own_mode(value):
    row = lax.broadcasted_iota(jnp.int32, value.shape, 0)
    lane = lax.broadcasted_iota(jnp.int32, value.shape, 1)
    return jnp.sum(jnp.where(row == lane % GROUP, value, 0.0), axis=0, keepdims=True)


def expand(rates, residue, seg, table, cuts):
    width = table.shape[1] * LANES
    full = spread_groups(mode_params(rates, residue), width, lambda lane: lane // GROUP)
    for tile in range(width // LANES):
        at = slice(tile * LANES, (tile + 1) * LANES)
        table[:, tile, :] = full[0 : 2 * MODES, at]
    for p in range(COUNT - 1):
        cuts[p] = jnp.sum(jnp.where(seg[...] <= p, 1, 0))
    cuts[COUNT - 1] = seg.shape[1]


def adjoint_kernel(seg, cuts, grad_scan, table, adj):
    length = seg.shape[1]

    def run(half, _):
        decay = decay_of(table, half)

        def step(t, states, keep):
            value = row_at(grad_scan, half, length, t)
            return tuple(decayed(decay[r], states[r], keep) + value for r in range(MODES))

        zero = jnp.zeros((TILES, LANES), f32)
        states = scan(length, seg, cuts, step, (zero,) * MODES, True)
        for r in range(MODES):
            adj[state_rows(half, r), :] = states[r]
        return _

    lax.fori_loop(0, HALVES, run, 0)


def state_kernel(
    full_width, seg, cuts, feats, grad_scan, part0, part1, part2, part3, table, gain, adj,
    msg_out, inverse, msg, feat_scan, ends, sums, sems,
):
    length = feats.shape[0]
    inverse[...] = inverse_of((part0, part1, part2, part3), full_width)
    scale = column(inverse[...])
    share = msg.shape[0] // HALVES

    def send(half):
        at = pl.ds(half * share, share)
        return pltpu.make_async_copy(msg.at[at], msg_out.at[at], sems.at[half])

    for half in range(HALVES):
        state_half(
            length, half, scale, seg, cuts, feats, grad_scan, table, gain, adj,
            msg, feat_scan, ends, sums,
        )
        send(half).start()
    for half in range(HALVES):
        send(half).wait()


def state_half(
    length, half, scale, seg, cuts, feats, grad_scan, table, gain, adj,
    msg, feat_scan, ends, sums,
):
    for tile in range(TILES):
        feat_scan[scan_rows(0, tile, length), :] = tile_of(feats, half, tile) * scale
    decay = decay_of(table, half)

    def step(t, carry, keep):
        value = row_at(feat_scan, 0, length, t)
        grads = row_at(grad_scan, half, length, t)
        states = [decayed(decay[r], carry[r], keep) + value for r in range(MODES)]
        totals = [carry[MODES + r] + grads * states[r] for r in range(MODES)]
        return tuple(states) + tuple(totals)

    zero = jnp.zeros((TILES, LANES), f32)
    carry = scan(length, seg, cuts, step, (zero,) * (2 * MODES), False)
    gains = gain[pl.ds(pl.multiple_of(half * TILES, TILES), TILES), :]
    weights = weight_of(table, half)
    for r in range(MODES):
        ends[pl.ds(r, TILES, stride=MODES), :] = carry[r]
        sums[r * TILES : (r + 1) * TILES, :] = carry[MODES + r] * gains
    gain_row = tree([weights[r] * carry[MODES + r] for r in range(MODES)])
    spread = jnp.dot(sums[...], block_ones(), precision=HIGHEST, preferred_element_type=f32)
    lane_mode = lane_iota(TILES) % GROUP
    mode_row = tree(
        [
            jnp.where(lane_mode == r, spread[r * TILES : (r + 1) * TILES, :], 0.0)
            for r in range(MODES)
        ]
    )
    even = join(gain_row, swap(mode_row))
    odd = join(swap(gain_row), mode_row)
    first = jnp.full((1, LANES), seg[0, 0], jnp.int32).astype(f32)
    last = jnp.full((1, LANES), seg[0, length - 1], jnp.int32).astype(f32)
    near = join(first, last)
    far = join(last, first)
    sub = lax.broadcasted_iota(jnp.int32, (EXTRA, LANES), 0)

    def extra(row):
        return jnp.where(sub == 0, near, jnp.where(sub == 1, far, jnp.where(sub == 2, row, 0.0)))

    for tile in range(TILES):
        state = ends[tile * MODES : (tile + 1) * MODES, :]
        own = (half * TILES + tile) * MODES
        adjoint = adj[pl.ds(pl.multiple_of(own, MODES), MODES), :]
        at = 2 * (half * TILES + tile)
        msg[at, 0:MODES, :] = join(state, swap(adjoint))
        msg[at + 1, 0:MODES, :] = join(swap(state), adjoint)
        msg[at, MODES:, :] = extra(even[tile : tile + 1, :])
        msg[at + 1, MODES:, :] = extra(odd[tile : tile + 1, :])


def carry_kernel(
    span, norm_factor, own, msg, rates, residue, gain, out_hbm, out, carries, sems
):
    count = msg.shape[0]
    share = rates.shape[1] // count
    first = own[0] * share
    full = spread_groups(
        mode_params(rates, residue), LANES, lambda lane: first + lane % (LANES // 2) // GROUP
    )
    rate, weight = full[0:MODES], full[MODES : 2 * MODES]
    root = own_mode(full[2 * MODES :])
    at = pl.ds(pl.multiple_of(own[0] // 2 * LANES, LANES), LANES)
    gains = gain[:, at]
    odd = own[0] % 2 == 1
    gains = jnp.where(odd, join(swap(gains), gains), join(gains, swap(gains)))
    single = jnp.exp(-rate)
    whole = jnp.exp(-rate * float(span))
    state = jnp.zeros((MODES, LANES), f32)
    before = None
    for m in range(count):
        fresh = join(msg[m, 0:MODES, :], msg[count - 1 - m, 0:MODES, :])
        near = join(msg[m, MODES : MODES + 1, :], msg[count - 1 - m, MODES : MODES + 1, :])
        far = join(msg[m, MODES + 1 : MODES + 2, :], msg[count - 1 - m, MODES + 1 : MODES + 2, :])
        if before is None:
            carries[m] = state
            state = fresh
        else:
            carries[m] = jnp.where(near == before, state, 0.0)
            state = fresh + jnp.where(far == before, whole * state, 0.0)
        before = far
    total = jnp.zeros((MODES, LANES), f32)
    row = jnp.zeros((1, LANES), f32)
    for i in range(count):
        carried = join(carries[i], carries[count - 1 - i])
        out[i, 0:MODES, :] = carried
        total = total + carried * swap(msg[i, 0:MODES, :])
        row = row + msg[i, MODES + 2 : MODES + 3, :]
    total = total * single
    gain_row = jnp.sum(weight * total, axis=0, keepdims=True)
    spread = jnp.dot(total * gains, block_ones(), precision=HIGHEST, preferred_element_type=f32)
    pick = lane_iota(MODES) % GROUP == lax.broadcasted_iota(jnp.int32, (MODES, LANES), 0)
    mode_row = jnp.sum(jnp.where(pick, spread, 0.0), axis=0, keepdims=True)
    row = (row + join(gain_row, swap(mode_row))) * join(jnp.ones((1, LANES), f32), root)
    row = row * norm_factor
    modes = join(own_mode(rate), own_mode(weight))
    sub = lax.broadcasted_iota(jnp.int32, (EXTRA, LANES), 0)
    for i in range(count):
        out[i, MODES:, :] = jnp.where(sub == 0, row, modes)
    copies = []
    part = count // COPIES
    for i in range(COPIES):
        at = pl.ds(i * part, part)
        copies.append(pltpu.make_async_copy(out.at[at], out_hbm.at[at], sems.at[i]))
        copies[-1].start()
    for copy in copies:
        copy.wait()


def local_kernel(backward, seg, cuts, source, table, *refs):
    if backward:
        out, result, value_out, sems = refs
    else:
        inverse, out, result, value_out, sems, scan_in = refs
    length = seg.shape[1]
    scale = None if backward else column(inverse[...])
    copies = []
    for half in range(HALVES):
        if backward:
            values, at_half = source, half
        else:
            values, at_half = scan_in, 0
            for tile in range(TILES):
                values[scan_rows(0, tile, length), :] = tile_of(source, half, tile) * scale
        decay = decay_of(table, half)
        weight = weight_of(table, half)

        def step(t, states, keep):
            value = row_at(values, at_half, length, t)
            states = tuple(decayed(decay[r], states[r], keep) + value for r in range(MODES))
            result[pl.ds(pl.multiple_of(t * TILES, TILES), TILES), :] = tree(
                [weight[r] * states[r] for r in range(MODES)]
            )
            return states

        zero = jnp.zeros((TILES, LANES), f32)
        scan(length, seg, cuts, step, (zero,) * MODES, backward)
        for tile in range(TILES):
            value_out[:, lanes_of(half, tile)] = result[pl.ds(tile, length, stride=TILES), :]
        at = pl.ds(half * TILES * LANES, TILES * LANES)
        copies.append(pltpu.make_async_copy(value_out.at[:, at], out.at[:, at], sems.at[half]))
        copies[-1].start()
    wait_all(copies)


def from_owners(back, pair, rows, upper):
    parts = []
    for n in range(2):
        low = back[4 * pair + 2 * n, rows, :]
        high = back[4 * pair + 2 * n + 1, rows, :]
        parts.append(join(swap(low), high) if upper else join(low, swap(high)))
    return jnp.concatenate(parts, axis=1)


def powers(cuts, back, pair, length, ahead):
    t = lax.broadcasted_iota(jnp.int32, (length, WIDE), 0)
    modes = slice(MODES + 1, MODES + 2)
    rate = from_owners(back, pair, modes, False)
    weight = from_owners(back, pair, modes, True)
    sub = lax.broadcasted_iota(jnp.int32, (8, WIDE), 0).astype(f32)
    further = jnp.exp(-8.0 * rate)
    if ahead:
        edge = jnp.int32(0)
        for p in range(COUNT - 1):
            edge = jnp.maximum(edge, jnp.where(cuts[p] < length, cuts[p], 0))
        linked = t >= edge
        lag = 8.0 - sub
    else:
        edge = jnp.int32(length)
        for p in range(COUNT - 1):
            edge = jnp.minimum(edge, jnp.where(cuts[p] > 0, cuts[p], length))
        linked = t < edge
        lag = sub + 1.0
    blocks = [jnp.exp(-lag * rate) * weight]
    for _ in range(length // 8 - 1):
        blocks.append(blocks[-1] * further)
    power = jnp.concatenate(blocks[::-1] if ahead else blocks, axis=0)
    return split(jnp.where(linked, power, 0.0))


def split(value):
    high = value.astype(jnp.bfloat16)
    return high, (value - high.astype(f32)).astype(jnp.bfloat16)


def from_carry(cuts, back, pair, length, ahead):
    carry = from_owners(back, pair, slice(0, MODES), ahead)
    own = lax.broadcasted_iota(jnp.int32, (WIDE, WIDE), 0) // MODES == (
        lax.broadcasted_iota(jnp.int32, (WIDE, WIDE), 1) // GROUP
    )

    def spread(value):
        value = jnp.concatenate([value.astype(f32)] * (WIDE // MODES), axis=0)
        return jnp.where(own, value, 0.0).astype(jnp.bfloat16)

    high, low = (spread(value) for value in split(carry))
    near, far = powers(cuts, back, pair, length, ahead)
    dot = lambda x, y: jnp.dot(x, y, preferred_element_type=f32)
    return dot(near, high) + (dot(far, high) + dot(near, low))


def row_copies(src, dst, sems):
    step = dst.shape[0] // COPIES
    copies = []
    for i in range(COPIES):
        at = pl.ds(i * step, step)
        copies.append(pltpu.make_async_copy(src.at[at, :], dst.at[at, :], sems.at[i]))
        copies[-1].start()
    return copies


def wait_all(copies):
    for copy in copies:
        copy.wait()


def tiles_at(width):
    return [slice(tile * LANES, (tile + 1) * LANES) for tile in range(width // LANES)]


def backward_kernel(
    cuts, back, local_in, feats, gain, scaled, inner, totals, partial, local, sems
):
    length, width = feats.shape
    copies = row_copies(local_in, local, sems)
    for n in range(back.shape[0]):
        totals[n : n + 1, :] = back[n, MODES : MODES + 1, :]
    for pair in range(width // WIDE):
        at = slice(pair * WIDE, (pair + 1) * WIDE)
        scaled[:, at] = from_carry(cuts, back, pair, length, True)
    step = length // COPIES
    for i in range(COPIES):
        copies[i].wait()
        here = slice(i * step, (i + 1) * step)
        sums = []
        for at in tiles_at(width):
            value = (local[here, at] + scaled[here, at]) * gain[:, at]
            scaled[here, at] = value
            sums.append(value * feats[here, at].astype(f32))
        partial[here, :] = tree(sums)
    inner[...] = lane_sums(partial[...])


def forward_kernel(
    cuts, back, local, gate, grad_in, gain, mixed, grad_gate,
    carried, grad, mixed_v, grad_gate_v, sems, sems_in,
):
    length, width = gate.shape
    copies_in = row_copies(grad_in, grad, sems_in)
    for pair in range(width // WIDE):
        at = slice(pair * WIDE, (pair + 1) * WIDE)
        carried[:, at] = from_carry(cuts, back, pair, length, False)
    copies = []
    step = length // COPIES
    for i in range(COPIES):
        copies_in[i].wait()
        here = slice(i * step, (i + 1) * step)
        for at in tiles_at(width):
            conv = (local[here, at] + carried[here, at]) * gain[:, at]
            mixed_v[here, at] = (gate[here, at].astype(f32) * conv).astype(jnp.bfloat16)
            grad_gate_v[here, at] = (grad[here, at].astype(f32) * conv).astype(jnp.bfloat16)
        at = pl.ds(i * step, step)
        for n, (src, dst) in enumerate(((mixed_v, mixed), (grad_gate_v, grad_gate))):
            copies.append(pltpu.make_async_copy(src.at[at, :], dst.at[at, :], sems.at[n, i]))
            copies[-1].start()
    wait_all(copies)


def feature_kernel(
    full_width, scaled, feats, inverse, i0, i1, i2, i3, own, other,
    out, modes, gains, out_v, sems,
):
    length, width = feats.shape
    scale = column(inverse[...])
    factor = column(total_row((i0, i1, i2, i3))) * scale * scale / full_width
    copies = []
    step = length // COPIES
    for i in range(COPIES):
        here = slice(i * step, (i + 1) * step)
        for at in tiles_at(width):
            value = scale[here] * (scaled[here, at] - feats[here, at].astype(f32) * factor[here])
            out_v[here, at] = value.astype(jnp.bfloat16)
        at = pl.ds(i * step, step)
        copies.append(pltpu.make_async_copy(out_v.at[at, :], out.at[at, :], sems.at[i]))
        copies[-1].start()

    total = own[...] + other[...]
    count = total.shape[0]
    groups = modes.shape[1]
    share = groups // count
    slot = lax.broadcasted_iota(jnp.int32, (count, groups), 1) // share
    pick = jnp.where(slot == lax.broadcasted_iota(jnp.int32, (count, groups), 0), 1.0, 0.0)
    spread = lax.dot_general(
        total,
        pick.astype(f32),
        (((0,), (0,)), ((), ())),
        precision=HIGHEST,
        preferred_element_type=f32,
    )
    member = lax.broadcasted_iota(jnp.int32, (MODES, groups), 1) % share
    parts = [
        jnp.where(member == n, spread[LANES // 2 + n * MODES : LANES // 2 + (n + 1) * MODES], 0.0)
        for n in range(share)
    ]
    modes[...] = tree(parts)
    for n in range(count // 2):
        gains[n : n + 1, :] = join(total[2 * n : 2 * n + 1, :], swap(total[2 * n + 1 : 2 * n + 2, :]))
    for copy in copies:
        copy.wait()


def all_parts(value):
    size = lax.axis_size("tensor")
    others = [
        lax.ppermute(value, "tensor", [(i, (i + d) % size) for i in range(size)])
        for d in range(1, size)
    ]
    return [value] + others


def shards(features, gate_in, segments, gain, residue, rates, grad_out):
    _, length, width = features.shape
    group_count, mode_count = rates.shape
    count = lax.axis_size("ctx")
    full_width = width * lax.axis_size("tensor")
    size = lax.axis_size("dp")
    norm_factor = 1.0 / math.sqrt(size * length * count)
    tiles = width // LANES
    gain_table = gain.reshape(tiles, LANES)
    gain_row = gain.reshape(1, width)

    smem = pl.BlockSpec(memory_space=pltpu.SMEM)
    vmem = pl.BlockSpec(memory_space=pltpu.VMEM)
    hbm = pl.BlockSpec(memory_space=pl.ANY)
    here = pltpu.VMEM
    work = length * width * MODES
    wide = (length, width)
    scan_shape = here((length * tiles, LANES), f32)
    message = pltpu.HBM((count, MODES + EXTRA, LANES), f32)
    state_scratch = pltpu.VMEM((TILES * MODES, LANES), f32)

    def call(kernel, name, in_specs, out_specs, out_shape, scratch, flops):
        return pl.pallas_call(
            kernel,
            in_specs=in_specs,
            out_specs=out_specs,
            out_shape=out_shape,
            scratch_shapes=scratch,
            compiler_params=pltpu.CompilerParams(vmem_limit_bytes=16 * 1024 * 1024),
            cost_estimate=pl.CostEstimate(
                flops=flops // 10**6, bytes_accessed=1, transcendentals=0
            ),
            name=name,
        )

    def in_hbm(*values):
        return [pltpu.with_memory_space_constraint(value, pltpu.HBM) for value in values]

    raw = in_hbm(features[0], gate_in[0], grad_out[0], rates.T, residue.T, segments)
    dma = pltpu.SemaphoreType.DMA
    feats, grad_scan, squares, table, cuts = call(
        load_kernel,
        "load",
        [hbm] * 6,
        [vmem] * 4 + [smem],
        [
            here(wide, jnp.bfloat16),
            scan_shape,
            here((1, length), f32),
            here((2 * mode_count, tiles, LANES), f32),
            jax.ShapeDtypeStruct((COUNT,), jnp.int32),
        ],
        [
            pltpu.VMEM(wide, jnp.bfloat16),
            pltpu.VMEM(wide, jnp.bfloat16),
            pltpu.VMEM((mode_count, group_count), f32),
            pltpu.VMEM((mode_count, group_count), f32),
            pltpu.VMEM((1, length), jnp.int32),
            dma((3, COPIES)),
            dma((3,)),
        ],
        2 * length * width,
    )(*raw)
    squares = all_parts(squares)

    adjoint = call(
        adjoint_kernel,
        "adjoint",
        [smem, smem] + [vmem] * 2,
        vmem,
        here((tiles * MODES, LANES), f32),
        [],
        2 * work,
    )(segments, cuts, grad_scan, table)

    scan_scratch = pltpu.VMEM((length * TILES, LANES), f32)
    message_scratch = pltpu.VMEM(message.shape, f32)
    msg, inverse = call(
        lambda *refs: state_kernel(full_width, *refs),
        "states",
        [smem, smem] + [vmem] * 9,
        [hbm, vmem],
        [message, here((1, length), f32)],
        [message_scratch, scan_scratch, state_scratch, state_scratch, dma((HALVES,))],
        4 * work,
    )(segments, cuts, feats, grad_scan, *squares, table, gain_table, adjoint)

    def local(backward, cuts, *sources):
        return call(
            lambda *refs: local_kernel(backward, *refs),
            "local_backward" if backward else "local_forward",
            [smem, smem] + [vmem] * len(sources),
            hbm,
            pltpu.HBM(wide, f32),
            [scan_scratch, pltpu.VMEM(wide, f32), dma((HALVES,))]
            + ([] if backward else [scan_scratch]),
            4 * work,
        )(segments, cuts, *sources)

    conv_local = local(False, cuts, feats, table, inverse)
    msg = lax.all_to_all(msg, "ctx", 0, 0, tiled=True)
    late_cuts, msg, conv_local = lax.optimization_barrier((cuts, msg, conv_local))

    own = lax.axis_index("ctx").astype(jnp.int32).reshape(1)
    back = call(
        lambda *refs: carry_kernel(length, norm_factor, *refs),
        "carries",
        [smem] + [vmem] * 4,
        hbm,
        message,
        [message_scratch, pltpu.VMEM((count, MODES, LANES), f32), dma((COPIES,))],
        32 * count * MODES * LANES,
    )(own, msg, rates.T, residue.T, gain_row)

    grad_local = local(True, late_cuts, grad_scan, table)
    back = lax.all_to_all(back, "ctx", 0, 0, tiled=True)

    matmuls = 3 * 2 * length * width * WIDE
    scaled, inner, totals = call(
        backward_kernel,
        "backward",
        [smem, vmem, hbm, vmem, vmem],
        [vmem] * 3,
        [here(wide, f32), here((1, length), f32), here((count, LANES), f32)],
        [pltpu.VMEM((length, LANES), f32), pltpu.VMEM(wide, f32), dma((COPIES,))],
        matmuls,
    )(cuts, back, *in_hbm(grad_local), feats, gain_row)
    inner = all_parts(inner)
    other = lax.ppermute(totals, "dp", [(i, (i + 1) % size) for i in range(size)])

    mixed, grad_gate = call(
        forward_kernel,
        "forward",
        [smem] + [vmem] * 3 + [hbm, vmem],
        [hbm] * 2,
        [jax.ShapeDtypeStruct(wide, jnp.bfloat16)] * 2,
        [pltpu.VMEM(wide, f32)]
        + [pltpu.VMEM(wide, jnp.bfloat16)] * 3
        + [dma((2, COPIES)), dma((COPIES,))],
        matmuls,
    )(cuts, back, conv_local, gate_in[0], raw[2], gain_row)

    grad_features, grad_residue, grad_gain = call(
        lambda *refs: feature_kernel(full_width, *refs),
        "features",
        [vmem] * 9,
        [hbm, vmem, vmem],
        [
            jax.ShapeDtypeStruct(wide, jnp.bfloat16),
            jax.ShapeDtypeStruct((mode_count, group_count), f32),
            jax.ShapeDtypeStruct((tiles, LANES), f32),
        ],
        [pltpu.VMEM(wide, jnp.bfloat16), dma((COPIES,))],
        4 * length * width,
    )(scaled, feats, inverse, *inner, totals, other)
    return (
        mixed[None],
        grad_features[None],
        grad_gate[None],
        grad_residue.T,
        grad_gain.reshape(width),
    )


def solution(mesh):
    placed = (
        P("dp", "ctx", "tensor"),
        P("dp", "ctx", "tensor"),
        P("dp", "ctx"),
        P("tensor"),
        P("tensor", None),
        P("tensor", None),
        P("dp", "ctx", "tensor"),
    )
    return jax.shard_map(
        shards,
        mesh=mesh,
        in_specs=placed,
        out_specs=(
            P("dp", "ctx", "tensor"),
            P("dp", "ctx", "tensor"),
            P("dp", "ctx", "tensor"),
            P("tensor", None),
            P("tensor"),
        ),
        check_vma=False,
    )
```

time: 669 us -> 82.5 us (0.12)
  the two profiles are of different devices: /device:TPU:136 before, /device:TPU:1 now
where the time goes in v2:
time: 82.5 us; the launch traced here: 82.1 us
  Pallas kernels  40.2 us (49%)
  starting transfers between devices  29.9 us (36%)
  waiting for transfers between devices  10.9 us (13%)
  between operations  0.99 us (1%)
    pallas_call x2, Pallas kernels, local(): call(lambda *refs: local_kernel(backward, *refs), 'local_backward' if bac...  13.9 us
    all_to_all x1, starting transfers between devices, shards(): msg = lax.all_to_all(msg, 'ctx', 0, 0, tiled=True)  11.2 us
    ppermute x6, starting transfers between devices, all_parts(): lax.ppermute(value, 'tensor', [(i, (i + d) % size) for i in range(size)])  8.69 us
    pallas_call x1, Pallas kernels, shards(): call(lambda *refs: state_kernel(full_width, *refs), 'states', [smem, smem...  7.47 us
    all_to_all x1, starting transfers between devices, shards(): back = lax.all_to_all(back, 'ctx', 0, 0, tiled=True)  5.69 us
    all_to_all x1, waiting for transfers between devices, shards(): msg = lax.all_to_all(msg, 'ctx', 0, 0, tiled=True)  5.65 us
    all_to_all x1, waiting for transfers between devices, shards(): back = lax.all_to_all(back, 'ctx', 0, 0, tiled=True)  5.24 us
    ppermute x1, starting transfers between devices, shards(): lax.ppermute(totals, 'dp', [(i, (i + 1) % size) for i in range(size)])  4.39 us
  transfers between devices with their start and end apart: 9, of which 2 were waited for; matrix products, arithmetic and copies ran while one was open for 0% of the time, Pallas kernels for 26%

profile of v2, /device:TPU:1, one launch (start us, length us, event | category | flops | bytes accessed | tf_op | source)
XLA Modules:
  0.0 82.1 jit_solution(17262906310117418953)
XLA Ops:
  0.7 3.7 %load.1 = (bf16[256,2048]{1,0:T(8,128)(2,1)S(1)}, f32[4096,128]{1,0:T(8,128)S(1)}, f32[1,256]{1,0:T(1,128)S(1)}, f32[32,16,128]{2,1,0:T(8,128)S(1)}, s32[4]{0:T(128)S(1)}) custom-call(bf16[256,2048]{1,0:T(8,128)(2,1)} %bitcast.25, bf16[256,2048]{1,0:T(8,128)(2,1)} %bitcast.13, bf16[256,2048]{1,0:T(8,128)(2,1)} %bitcast.23, f32[16,128]{1,0:T(8,128)} %bitcast.19, ...), custom_call_target="tpu_custom_call" | custom-call | flops 1 | bytes 1 | tf_op jit(solution)/shard_map/load/pallas_call | solution.py:632
  4.3 2.2 %collective-permute-start = (f32[1,256]{1,0:T(1,128)S(1)}, f32[1,256]{1,0:T(1,128)S(1)}, u32[]{:S(2)}, u32[]{:S(2)}) collective-permute-start(f32[1,256]{1,0:T(1,128)S(1)} %get-tuple-element.26.refs_4_), channel_id=1, source_target_pairs={{0,1},{1,2},{2,3},{3,0},{4,5},{5,6},{6,7},{7,4},{8,9},{9,10},{10,1... | collective-permute-start | bytes 3080 | tf_op jit(solution)/shard_map/ppermute | solution.py:586
  6.5 2.6 %collective-permute-start.1 = (f32[1,256]{1,0:T(1,128)S(1)}, f32[1,256]{1,0:T(1,128)S(1)}, u32[]{:S(2)}, u32[]{:S(2)}) collective-permute-start(f32[1,256]{1,0:T(1,128)S(1)} %get-tuple-element.26.refs_4_), channel_id=1, source_target_pairs={{0,2},{1,3},{2,0},{3,1},{4,6},{5,7},{6,4},{7,5},{8,10},{9,11},{10,... | collective-permute-start | bytes 3080 | tf_op jit(solution)/shard_map/ppermute | solution.py:586
  9.1 1.1 %collective-permute-start.2 = (f32[1,256]{1,0:T(1,128)S(1)}, f32[1,256]{1,0:T(1,128)S(1)}, u32[]{:S(2)}, u32[]{:S(2)}) collective-permute-start(f32[1,256]{1,0:T(1,128)S(1)} %get-tuple-element.26.refs_4_), channel_id=1, source_target_pairs={{0,3},{1,0},{2,1},{3,2},{4,7},{5,4},{6,5},{7,6},{8,11},{9,8},{10,9... | collective-permute-start | bytes 3080 | tf_op jit(solution)/shard_map/ppermute | solution.py:586
  10.2 3.2 %adjoint.1.refs_10_ = f32[256,128]{1,0:T(8,128)S(1)} custom-call(s32[1,256]{1,0:T(1,128)S(1)} %copy-done.5, s32[4]{0:T(128)S(1)} %get-tuple-element.33.cuts.refs_1_, f32[4096,128]{1,0:T(8,128)S(1)} %get-tuple-element.25.grad_scan.refs_3_.refs_2_, f32[32,16,128]{2,1,0:T(8,128)S(1)} %get-tuple-element.27.table.refs_8_.refs_3_), custom_call_target="tpu_custom_call" | custom-call | flops 16 | bytes 1 | tf_op jit(solution)/shard_map/adjoint/pallas_call | solution.py:657
  13.4 0.0 collective-permute-done.1.refs_6_
  13.4 0.0 collective-permute-done.2.refs_7_
  13.4 7.5 %states.1 = (f32[32,24,128]{2,1,0:T(8,128)}, f32[1,256]{1,0:T(1,128)S(1)}) custom-call(s32[1,256]{1,0:T(1,128)S(1)} %copy-done.5, s32[4]{0:T(128)S(1)} %get-tuple-element.33.cuts.refs_1_, bf16[256,2048]{1,0:T(8,128)(2,1)S(1)} %get-tuple-element.24.refs_2_.feats.refs_1_, f32[4096,128]{1,0:T(8,128)S(1)} %get-tuple-element.25.grad_scan.refs_3_.refs_2_, ...), custom_call_target="tpu_custom_call" | custom-call | flops 33 | bytes 1 | tf_op jit(solution)/shard_map/states/pallas_call | solution.py:669
  20.9 0.0 copy-start.3
  20.9 0.0 copy-start.4
  20.9 11.2 %all-to-all-start = ((f32[32,24,128]{2,1,0:T(8,128)}), f32[32,24,128]{2,1,0:T(8,128)}, u32[]{:S(2)}, u32[]{:S(2)}) async-start(f32[32,24,128]{2,1,0:T(8,128)} %get-tuple-element.28), calls=%async_computation | async-start | bytes 786432 | tf_op jit(solution)/shard_map/all_to_all | solution.py:692
  32.1 7.2 %local_forward.1.local = f32[256,2048]{1,0:T(8,128)} custom-call(s32[1,256]{1,0:T(1,128)S(1)} %copy-done.5, s32[4]{0:T(128)S(1)} %get-tuple-element.33.cuts.refs_1_, bf16[256,2048]{1,0:T(8,128)(2,1)S(1)} %get-tuple-element.24.refs_2_.feats.refs_1_, f32[32,16,128]{2,1,0:T(8,128)S(1)} %get-tuple-element.27.table.refs_8_.refs_3_, ...), custom_call_target="tpu_custom_call" | custom-call | flops 33 | bytes 1 | tf_op jit(solution)/shard_map/local_forward/pallas_call | solution.py:680
  39.4 5.7 %all-to-all-done.refs_1_ = f32[32,24,128]{2,1,0:T(8,128)} async-done(((f32[32,24,128]{2,1,0:T(8,128)}), f32[32,24,128]{2,1,0:T(8,128)}, u32[]{:S(2)}, u32[]{:S(2)}) %all-to-all-start) | async-done | bytes 393248 | tf_op jit(solution)/shard_map/all_to_all | solution.py:692
  45.0 2.5 %carries.1 = f32[32,24,128]{2,1,0:T(8,128)} custom-call(s32[1]{0:T(128)} %bitcast.5.refs_0_, f32[32,24,128]{2,1,0:T(8,128)} %all-to-all-done.refs_1_, f32[16,128]{1,0:T(8,128)S(1)} %bitcast.20, f32[16,128]{1,0:T(8,128)S(1)} %bitcast.22, f32[1,2048]{1,0:T(1,128)S(1)} %bitcast.16), custom_call_target="tpu_custom_call" | custom-call | flops 2 | bytes 1 | tf_op jit(solution)/shard_map/carries/pallas_call | solution.py:696
  47.5 5.7 %all-to-all-start.1 = ((f32[32,24,128]{2,1,0:T(8,128)}), f32[32,24,128]{2,1,0:T(8,128)}, u32[]{:S(2)}, u32[]{:S(2)}) async-start(f32[32,24,128]{2,1,0:T(8,128)} %carries.1), calls=%async_computation.1 | async-start | bytes 786432 | tf_op jit(solution)/shard_map/all_to_all | solution.py:707
  53.2 6.7 %local_backward.1.local_in = f32[256,2048]{1,0:T(8,128)} custom-call(s32[1,256]{1,0:T(1,128)S(1)} %copy-done.5, s32[4]{0:T(128)S(1)} %get-tuple-element.33.cuts.refs_1_, f32[4096,128]{1,0:T(8,128)S(1)} %get-tuple-element.25.grad_scan.refs_3_.refs_2_, f32[32,16,128]{2,1,0:T(8,128)S(1)} %get-tuple-element.27.table.refs_8_.refs_3_), custom_call_target="tpu_custom_call" | custom-call | flops 33 | bytes 1 | tf_op jit(solution)/shard_map/local_backward/pallas_call | solution.py:680
  59.9 5.2 %all-to-all-done.1.back = f32[32,24,128]{2,1,0:T(8,128)} async-done(((f32[32,24,128]{2,1,0:T(8,128)}), f32[32,24,128]{2,1,0:T(8,128)}, u32[]{:S(2)}, u32[]{:S(2)}) %all-to-all-start.1) | async-done | bytes 393248 | tf_op jit(solution)/shard_map/all_to_all | solution.py:707
  65.1 3.6 %backward.1 = (f32[256,2048]{1,0:T(8,128)S(1)}, f32[1,256]{1,0:T(1,128)S(1)}, f32[32,128]{1,0:T(8,128)S(1)}) custom-call(s32[4]{0:T(128)S(1)} %get-tuple-element.33.cuts.refs_1_, f32[32,24,128]{2,1,0:T(8,128)} %all-to-all-done.1.back, f32[256,2048]{1,0:T(8,128)} %local_backward.1.local_in, bf16[256,2048]{1,0:T(8,128)(2,1)S(1)} %get-tuple-element.24.refs_2_.feats.refs_1_, ...), custom_call_target="tpu_custom_call" | custom-call | flops 805 | bytes 1 | tf_op jit(solution)/shard_map/backward/pallas_call | solution.py:710
  68.8 4.4 %collective-permute-start.6 = (f32[32,128]{1,0:T(8,128)S(1)}, f32[32,128]{1,0:T(8,128)S(1)}, u32[]{:S(2)}, u32[]{:S(2)}) collective-permute-start(f32[32,128]{1,0:T(8,128)S(1)} %get-tuple-element.36.refs_7_), channel_id=1, source_target_pairs={{0,128},{128,0},{1,129},{129,1},{2,130},{130,2},{3,131},{131,3},{4... | collective-permute-start | bytes 49160 | tf_op jit(solution)/shard_map/ppermute | solution.py:720
  73.2 0.4 collective-permute-start.3
  73.6 0.3 collective-permute-start.4
  73.9 2.1 %collective-permute-start.5 = (f32[1,256]{1,0:T(1,128)S(1)}, f32[1,256]{1,0:T(1,128)S(1)}, u32[]{:S(2)}, u32[]{:S(2)}) collective-permute-start(f32[1,256]{1,0:T(1,128)S(1)} %get-tuple-element.35.refs_3_), channel_id=1, source_target_pairs={{0,3},{1,0},{2,1},{3,2},{4,7},{5,4},{6,5},{7,6},{8,11},{9,8},{10,9... | collective-permute-start | bytes 3080 | tf_op jit(solution)/shard_map/ppermute | solution.py:586
  76.0 4.0 %forward.1 = (bf16[256,2048]{1,0:T(8,128)(2,1)}, bf16[256,2048]{1,0:T(8,128)(2,1)}) custom-call(s32[4]{0:T(128)S(1)} %get-tuple-element.33.cuts.refs_1_, f32[32,24,128]{2,1,0:T(8,128)} %all-to-all-done.1.back, f32[256,2048]{1,0:T(8,128)S(1)} %copy-done, bf16[256,2048]{1,0:T(8,128)(2,1)S(1)} %bitcast.14, bf16[256,2048]{1,0:T(8,128)(2,1)} %bitcast.24, ...), custom_call_target="tpu_custom_call" | custom-call | flops 805 | bytes 1 | tf_op jit(solution)/shard_map/forward/pallas_call | solution.py:722
  80.0 2.0 %features.1 = (bf16[256,2048]{1,0:T(8,128)(2,1)}, f32[16,128]{1,0:T(8,128)}, f32[16,128]{1,0:T(8,128)}) custom-call(f32[256,2048]{1,0:T(8,128)S(1)} %get-tuple-element.34.refs_0_, bf16[256,2048]{1,0:T(8,128)(2,1)S(1)} %get-tuple-element.24.refs_2_.feats.refs_1_, f32[1,256]{1,0:T(1,128)S(1)} %get-tuple-element.29.refs_4_.refs_2_, ...), custom_call_target="tpu_custom_call" | custom-call | flops 2 | bytes 1 | tf_op jit(solution)/shard_map/features/pallas_call | solution.py:734
  (15 shorter events, 0.0 us)
Async XLA Ops:
  0.6 9.6 %copy-start.5 = (s32[1,256]{1,0:T(1,128)S(1)}, s32[1,256]{1,0:T(1,128)}, u32[]{:S(2)}) copy-start(s32[1,256]{1,0:T(1,128)} %refs_0_.5) | copy-start | bytes 3076
  0.6 12.8 %copy-start.2 = (f32[2048]{0:T(1024)S(1)}, f32[2048]{0:T(1024)}, u32[]{:S(2)}) copy-start(f32[2048]{0:T(1024)} %param.10) | copy-start | bytes 24580
  4.3 9.1 %collective-permute-start = (f32[1,256]{1,0:T(1,128)S(1)}, f32[1,256]{1,0:T(1,128)S(1)}, u32[]{:S(2)}, u32[]{:S(2)}) collective-permute-start(f32[1,256]{1,0:T(1,128)S(1)} %get-tuple-element.26.refs_4_), channel_id=1, source_target_pairs={{0,1},{1,2},{2,3},{3,0},{4,5},{5,6},{6,7},{7,4},{8,9},{9,10},{10,1... | collective-permute-start | bytes 3080 | tf_op jit(solution)/shard_map/ppermute | solution.py:586
  6.5 6.9 %collective-permute-start.1 = (f32[1,256]{1,0:T(1,128)S(1)}, f32[1,256]{1,0:T(1,128)S(1)}, u32[]{:S(2)}, u32[]{:S(2)}) collective-permute-start(f32[1,256]{1,0:T(1,128)S(1)} %get-tuple-element.26.refs_4_), channel_id=1, source_target_pairs={{0,2},{1,3},{2,0},{3,1},{4,6},{5,7},{6,4},{7,5},{8,10},{9,11},{10,... | collective-permute-start | bytes 3080 | tf_op jit(solution)/shard_map/ppermute | solution.py:586
  9.1 4.3 %collective-permute-start.2 = (f32[1,256]{1,0:T(1,128)S(1)}, f32[1,256]{1,0:T(1,128)S(1)}, u32[]{:S(2)}, u32[]{:S(2)}) collective-permute-start(f32[1,256]{1,0:T(1,128)S(1)} %get-tuple-element.26.refs_4_), channel_id=1, source_target_pairs={{0,3},{1,0},{2,1},{3,2},{4,7},{5,4},{6,5},{7,6},{8,11},{9,8},{10,9... | collective-permute-start | bytes 3080 | tf_op jit(solution)/shard_map/ppermute | solution.py:586
  20.9 24.1 %copy-start.3 = (f32[128,16]{0,1:T(8,128)S(1)}, f32[128,16]{0,1:T(8,128)}, u32[]{:S(2)}) copy-start(f32[128,16]{0,1:T(8,128)} %param.12) | copy-start | bytes 24580
  20.9 24.1 %copy-start.4 = (f32[128,16]{0,1:T(8,128)S(1)}, f32[128,16]{0,1:T(8,128)}, u32[]{:S(2)}) copy-start(f32[128,16]{0,1:T(8,128)} %param.11) | copy-start | bytes 24580
  20.9 24.1 %all-to-all-start = ((f32[32,24,128]{2,1,0:T(8,128)}), f32[32,24,128]{2,1,0:T(8,128)}, u32[]{:S(2)}, u32[]{:S(2)}) async-start(f32[32,24,128]{2,1,0:T(8,128)} %get-tuple-element.28), calls=%async_computation | async-start | bytes 786432 | tf_op jit(solution)/shard_map/all_to_all | solution.py:692
  47.5 17.6 %all-to-all-start.1 = ((f32[32,24,128]{2,1,0:T(8,128)}), f32[32,24,128]{2,1,0:T(8,128)}, u32[]{:S(2)}, u32[]{:S(2)}) async-start(f32[32,24,128]{2,1,0:T(8,128)} %carries.1), calls=%async_computation.1 | async-start | bytes 786432 | tf_op jit(solution)/shard_map/all_to_all | solution.py:707
  59.9 16.1 %copy-start = (f32[256,2048]{1,0:T(8,128)S(1)}, f32[256,2048]{1,0:T(8,128)}, u32[]{:S(2)}) copy-start(f32[256,2048]{1,0:T(8,128)} %local_forward.1.local) | copy-start | bytes 6291460
  65.1 10.9 %copy-start.1 = (bf16[1,256,2048]{2,1,0:T(8,128)(2,1)S(1)}, bf16[1,256,2048]{2,1,0:T(8,128)(2,1)}, u32[]{:S(2)}) copy-start(bf16[1,256,2048]{2,1,0:T(8,128)(2,1)} %param.8) | copy-start | bytes 3145732
  68.8 11.2 %collective-permute-start.6 = (f32[32,128]{1,0:T(8,128)S(1)}, f32[32,128]{1,0:T(8,128)S(1)}, u32[]{:S(2)}, u32[]{:S(2)}) collective-permute-start(f32[32,128]{1,0:T(8,128)S(1)} %get-tuple-element.36.refs_7_), channel_id=1, source_target_pairs={{0,128},{128,0},{1,129},{129,1},{2,130},{130,2},{3,131},{131,3},{4... | collective-permute-start | bytes 49160 | tf_op jit(solution)/shard_map/ppermute | solution.py:720
  73.2 6.8 %collective-permute-start.3 = (f32[1,256]{1,0:T(1,128)S(1)}, f32[1,256]{1,0:T(1,128)S(1)}, u32[]{:S(2)}, u32[]{:S(2)}) collective-permute-start(f32[1,256]{1,0:T(1,128)S(1)} %get-tuple-element.35.refs_3_), channel_id=1, source_target_pairs={{0,1},{1,2},{2,3},{3,0},{4,5},{5,6},{6,7},{7,4},{8,9},{9,10},{10,1... | collective-permute-start | bytes 3080 | tf_op jit(solution)/shard_map/ppermute | solution.py:586
  73.6 6.4 %collective-permute-start.4 = (f32[1,256]{1,0:T(1,128)S(1)}, f32[1,256]{1,0:T(1,128)S(1)}, u32[]{:S(2)}, u32[]{:S(2)}) collective-permute-start(f32[1,256]{1,0:T(1,128)S(1)} %get-tuple-element.35.refs_3_), channel_id=1, source_target_pairs={{0,2},{1,3},{2,0},{3,1},{4,6},{5,7},{6,4},{7,5},{8,10},{9,11},{10,... | collective-permute-start | bytes 3080 | tf_op jit(solution)/shard_map/ppermute | solution.py:586
  73.9 6.1 %collective-permute-start.5 = (f32[1,256]{1,0:T(1,128)S(1)}, f32[1,256]{1,0:T(1,128)S(1)}, u32[]{:S(2)}, u32[]{:S(2)}) collective-permute-start(f32[1,256]{1,0:T(1,128)S(1)} %get-tuple-element.35.refs_3_), channel_id=1, source_target_pairs={{0,3},{1,0},{2,1},{3,2},{4,7},{5,4},{6,5},{7,6},{8,11},{9,8},{10,9... | collective-permute-start | bytes 3080 | tf_op jit(solution)/shard_map/ppermute | solution.py:586

commit v3 on v2

--- a/solution.py
+++ b/solution.py
@@ -15,9 +15,10 @@
 GROUP = 16
 UNROLL = 16
 COUNT = 4
-COPIES = 8
+COPIES = 2
+BLOCKS = 8
 WIDE = 2 * LANES
-EXTRA = 8
+ROWS = MODES + 2
 HIGHEST = lax.Precision.HIGHEST
 f32 = jnp.float32
 
@@ -51,7 +52,16 @@
 def block_ones():
     left = lax.broadcasted_iota(jnp.int32, (LANES, LANES), 0) // GROUP
     right = lax.broadcasted_iota(jnp.int32, (LANES, LANES), 1) // GROUP
-    return jnp.where(left == right, 1.0, 0.0).astype(f32)
+    return jnp.where(left == right, 1.0, 0.0).astype(jnp.bfloat16)
+
+
+def exact_dot(value, ones):
+    high = value.astype(jnp.bfloat16).astype(f32)
+    middle = (value - high).astype(jnp.bfloat16).astype(f32)
+    parts = jnp.concatenate([high, middle, value - high - middle], axis=0)
+    full = jnp.dot(parts.astype(jnp.bfloat16), ones, preferred_element_type=f32)
+    rows = value.shape[0]
+    return full[0:rows] + (full[rows : 2 * rows] + full[2 * rows :])
 
 
 def lanes_of(half, tile):
@@ -160,30 +170,24 @@
     gate, grad, rates, residue, seg, sems, small_sems,
 ):
     length, width = feats.shape
-    step = length // COPIES
     small = [
         pltpu.make_async_copy(src, dst, small_sems.at[n])
         for n, (src, dst) in enumerate(((rates_in, rates), (residue_in, residue), (seg_in, seg)))
     ]
-    copies = []
-    for n, (src, dst) in enumerate(((feats_in, feats), (gate_in, gate), (grad_in, grad))):
-        for i in range(COPIES):
-            at = pl.ds(i * step, step)
-            copies.append(pltpu.make_async_copy(src.at[at, :], dst.at[at, :], sems.at[n, i]))
-    for copy in small + copies:
+    for copy in small:
         copy.start()
+    feat_copies = row_copies(feats_in, feats, sems.at[0])
+    copies = row_copies(gate_in, gate, sems.at[1]) + row_copies(grad_in, grad, sems.at[2])
     for copy in small:
         copy.wait()
     expand(rates, residue, seg, table, cuts)
-    for i in range(COPIES):
-        copies[i].wait()
+    wait_all(feat_copies)
     partial = jnp.zeros((length, LANES), f32)
     for tile in range(width // LANES):
         value = tile_of(feats, 0, tile)
         partial = partial + value * value
     squares[...] = lane_sums(partial)
-    for copy in copies[COPIES:]:
-        copy.wait()
+    wait_all(copies)
     for half in range(HALVES):
         for tile in range(TILES):
             value = tile_of(gate, half, tile) * tile_of(grad, half, tile)
@@ -204,8 +208,8 @@
     group_count = packed.shape[1]
     group = lax.broadcasted_iota(jnp.int32, (group_count, width), 0)
     lane = lax.broadcasted_iota(jnp.int32, (group_count, width), 1)
-    spread = jnp.where(first(lane) == group, 1.0, 0.0).astype(f32)
-    return jnp.dot(packed, spread, precision=HIGHEST, preferred_element_type=f32)
+    spread = jnp.where(first(lane) == group, 1.0, 0.0).astype(jnp.bfloat16)
+    return exact_dot(packed, spread)
 
 
 def own_mode(value):
@@ -246,16 +250,17 @@
 
 def state_kernel(
     full_width, seg, cuts, feats, grad_scan, part0, part1, part2, part3, table, gain, adj,
-    msg_out, inverse, msg, feat_scan, ends, sums, sems,
+    msg_out, inverse, grad_out, msg, feat_scan, ends, sums, sems, grad_sems,
 ):
     length = feats.shape[0]
+    grad_copies = row_copies(grad_scan, grad_out, grad_sems)
     inverse[...] = inverse_of((part0, part1, part2, part3), full_width)
     scale = column(inverse[...])
     share = msg.shape[0] // HALVES
 
     def send(half):
         at = pl.ds(half * share, share)
-        return pltpu.make_async_copy(msg.at[at], msg_out.at[at], sems.at[half])
+        return pltpu.make_async_copy(msg.at[at, :], msg_out.at[at, :], sems.at[half])
 
     for half in range(HALVES):
         state_half(
@@ -265,6 +270,7 @@
         send(half).start()
     for half in range(HALVES):
         send(half).wait()
+    wait_all(grad_copies)
 
 
 def state_half(
@@ -290,7 +296,7 @@
         ends[pl.ds(r, TILES, stride=MODES), :] = carry[r]
         sums[r * TILES : (r + 1) * TILES, :] = carry[MODES + r] * gains
     gain_row = tree([weights[r] * carry[MODES + r] for r in range(MODES)])
-    spread = jnp.dot(sums[...], block_ones(), precision=HIGHEST, preferred_element_type=f32)
+    spread = exact_dot(sums[...], block_ones())
     lane_mode = lane_iota(TILES) % GROUP
     mode_row = tree(
         [
@@ -303,27 +309,25 @@
     first = jnp.full((1, LANES), seg[0, 0], jnp.int32).astype(f32)
     last = jnp.full((1, LANES), seg[0, length - 1], jnp.int32).astype(f32)
     near = join(first, last)
-    far = join(last, first)
-    sub = lax.broadcasted_iota(jnp.int32, (EXTRA, LANES), 0)
-
-    def extra(row):
-        return jnp.where(sub == 0, near, jnp.where(sub == 1, far, jnp.where(sub == 2, row, 0.0)))
 
     for tile in range(TILES):
         state = ends[tile * MODES : (tile + 1) * MODES, :]
         own = (half * TILES + tile) * MODES
         adjoint = adj[pl.ds(pl.multiple_of(own, MODES), MODES), :]
-        at = 2 * (half * TILES + tile)
-        msg[at, 0:MODES, :] = join(state, swap(adjoint))
-        msg[at + 1, 0:MODES, :] = join(swap(state), adjoint)
-        msg[at, MODES:, :] = extra(even[tile : tile + 1, :])
-        msg[at + 1, MODES:, :] = extra(odd[tile : tile + 1, :])
+        at = 2 * (half * TILES + tile) * ROWS
+        msg[at : at + MODES, :] = join(state, swap(adjoint))
+        msg[at + MODES : at + MODES + 1, :] = even[tile : tile + 1, :]
+        msg[at + MODES + 1 : at + ROWS, :] = near
+        at += ROWS
+        msg[at : at + MODES, :] = join(swap(state), adjoint)
+        msg[at + MODES : at + MODES + 1, :] = odd[tile : tile + 1, :]
+        msg[at + MODES + 1 : at + ROWS, :] = near
 
 
 def carry_kernel(
     span, norm_factor, own, msg, rates, residue, gain, out_hbm, out, carries, sems
 ):
-    count = msg.shape[0]
+    count = msg.shape[0] // ROWS
     share = rates.shape[1] // count
     first = own[0] * share
     full = spread_groups(
@@ -339,10 +343,13 @@
     whole = jnp.exp(-rate * float(span))
     state = jnp.zeros((MODES, LANES), f32)
     before = None
+    ends = [msg[i * ROWS : i * ROWS + MODES, :] for i in range(count)]
+    ids = [msg[i * ROWS + MODES + 1 : (i + 1) * ROWS, :] for i in range(count)]
     for m in range(count):
-        fresh = join(msg[m, 0:MODES, :], msg[count - 1 - m, 0:MODES, :])
-        near = join(msg[m, MODES : MODES + 1, :], msg[count - 1 - m, MODES : MODES + 1, :])
-        far = join(msg[m, MODES + 1 : MODES + 2, :], msg[count - 1 - m, MODES + 1 : MODES + 2, :])
+        other = count - 1 - m
+        fresh = join(ends[m], ends[other])
+        near = join(ids[m], ids[other])
+        far = join(swap(ids[m]), swap(ids[other]))
         if before is None:
             carries[m] = state
             state = fresh
@@ -354,45 +361,59 @@
     row = jnp.zeros((1, LANES), f32)
     for i in range(count):
         carried = join(carries[i], carries[count - 1 - i])
-        out[i, 0:MODES, :] = carried
-        total = total + carried * swap(msg[i, 0:MODES, :])
-        row = row + msg[i, MODES + 2 : MODES + 3, :]
+        out[i * ROWS : i * ROWS + MODES, :] = carried
+        total = total + carried * swap(ends[i])
+        row = row + msg[i * ROWS + MODES : i * ROWS + MODES + 1, :]
     total = total * single
     gain_row = jnp.sum(weight * total, axis=0, keepdims=True)
-    spread = jnp.dot(total * gains, block_ones(), precision=HIGHEST, preferred_element_type=f32)
+    spread = exact_dot(total * gains, block_ones())
     pick = lane_iota(MODES) % GROUP == lax.broadcasted_iota(jnp.int32, (MODES, LANES), 0)
     mode_row = jnp.sum(jnp.where(pick, spread, 0.0), axis=0, keepdims=True)
     row = (row + join(gain_row, swap(mode_row))) * join(jnp.ones((1, LANES), f32), root)
     row = row * norm_factor
     modes = join(own_mode(rate), own_mode(weight))
-    sub = lax.broadcasted_iota(jnp.int32, (EXTRA, LANES), 0)
     for i in range(count):
-        out[i, MODES:, :] = jnp.where(sub == 0, row, modes)
+        out[i * ROWS + MODES : i * ROWS + MODES + 1, :] = row
+        out[i * ROWS + MODES + 1 : (i + 1) * ROWS, :] = modes
     copies = []
-    part = count // COPIES
+    part = out.shape[0] // COPIES
     for i in range(COPIES):
         at = pl.ds(i * part, part)
-        copies.append(pltpu.make_async_copy(out.at[at], out_hbm.at[at], sems.at[i]))
+        copies.append(pltpu.make_async_copy(out.at[at, :], out_hbm.at[at, :], sems.at[i]))
         copies[-1].start()
     for copy in copies:
         copy.wait()
 
 
-def local_kernel(backward, seg, cuts, source, table, *refs):
+def local_kernel(backward, seg, cuts, table_in, *refs):
     if backward:
-        out, result, value_out, sems = refs
+        grad_in, feats_in, gain, out, inner, feats, result, feat_sems, *rest = refs
+        value_out, sems, partial, grad_scan, grad_sems, table, table_sem = rest
+        table_copy = pltpu.make_async_copy(table_in, table, table_sem.at[0])
+        table_copy.start()
+        grad_copies = row_copies(grad_in, grad_scan, grad_sems)
     else:
-        inverse, out, result, value_out, sems, scan_in = refs
+        feats_in, inverse, value_out, table_out, result, feat_sems, scan_in, feats, table_sem = refs
+        table = table_in
+        table_copy = pltpu.make_async_copy(table, table_out, table_sem.at[0])
+        table_copy.start()
     length = seg.shape[1]
-    scale = None if backward else column(inverse[...])
+    feat_copies = row_copies(feats_in, feats, feat_sems)
+    if not backward:
+        scale = column(inverse[...])
+        wait_all(feat_copies)
     copies = []
     for half in range(HALVES):
         if backward:
-            values, at_half = source, half
+            values, at_half = grad_scan, half
+            part = COPIES // HALVES
+            wait_all(grad_copies[half * part : (half + 1) * part])
+            if half == 0:
+                table_copy.wait()
         else:
             values, at_half = scan_in, 0
             for tile in range(TILES):
-                values[scan_rows(0, tile, length), :] = tile_of(source, half, tile) * scale
+                values[scan_rows(0, tile, length), :] = tile_of(feats, half, tile) * scale
         decay = decay_of(table, half)
         weight = weight_of(table, half)
 
@@ -408,17 +429,38 @@
         scan(length, seg, cuts, step, (zero,) * MODES, backward)
         for tile in range(TILES):
             value_out[:, lanes_of(half, tile)] = result[pl.ds(tile, length, stride=TILES), :]
-        at = pl.ds(half * TILES * LANES, TILES * LANES)
-        copies.append(pltpu.make_async_copy(value_out.at[:, at], out.at[:, at], sems.at[half]))
-        copies[-1].start()
+        if backward:
+            at = pl.ds(half * TILES * LANES, TILES * LANES)
+            copies.append(pltpu.make_async_copy(value_out.at[:, at], out.at[:, at], sems.at[half]))
+            copies[-1].start()
+    if backward:
+        wait_all(feat_copies)
+        inner[...] = inner_sums(value_out, feats, gain, partial)
+    else:
+        table_copy.wait()
     wait_all(copies)
+
+
+def inner_sums(value, feats, gain, partial):
+    length, width = feats.shape
+    step = length // BLOCKS
+    for i in range(BLOCKS):
+        here = slice(i * step, (i + 1) * step)
+        partial[here, :] = tree(
+            [
+                value[here, at] * gain[:, at] * feats[here, at].astype(f32)
+                for at in tiles_at(width)
+            ]
+        )
+    return lane_sums(partial[...])
 
 
 def from_owners(back, pair, rows, upper):
     parts = []
     for n in range(2):
-        low = back[4 * pair + 2 * n, rows, :]
-        high = back[4 * pair + 2 * n + 1, rows, :]
+        first = (4 * pair + 2 * n) * ROWS
+        low = back[first + rows.start : first + rows.stop, :]
+        high = back[first + ROWS + rows.start : first + ROWS + rows.stop, :]
         parts.append(join(swap(low), high) if upper else join(low, swap(high)))
     return jnp.concatenate(parts, axis=1)
 
@@ -470,13 +512,16 @@
     return dot(near, high) + (dot(far, high) + dot(near, low))
 
 
-def row_copies(src, dst, sems):
-    step = dst.shape[0] // COPIES
-    copies = []
-    for i in range(COPIES):
-        at = pl.ds(i * step, step)
-        copies.append(pltpu.make_async_copy(src.at[at, :], dst.at[at, :], sems.at[i]))
-        copies[-1].start()
+def row_copy(src, dst, sems, part, parts=COPIES):
+    step = dst.shape[0] // parts
+    at = pl.ds(part * step, step)
+    return pltpu.make_async_copy(src.at[at, :], dst.at[at, :], sems.at[part])
+
+
+def row_copies(src, dst, sems, parts=COPIES):
+    copies = [row_copy(src, dst, sems, part, parts) for part in range(parts)]
+    for copy in copies:
+        copy.start()
     return copies
 
 
@@ -490,70 +535,63 @@
 
 
 def backward_kernel(
-    cuts, back, local_in, feats, gain, scaled, inner, totals, partial, local, sems
+    cuts, back, inner_local, feats, gain, gate_in, grad_in,
+    carried, inner, totals, gate, grad, partial, sems,
 ):
     length, width = feats.shape
-    copies = row_copies(local_in, local, sems)
-    for n in range(back.shape[0]):
-        totals[n : n + 1, :] = back[n, MODES : MODES + 1, :]
+    copies = []
+    for n, (src, dst) in enumerate(((gate_in, gate), (grad_in, grad))):
+        copies += row_copies(src, dst, sems.at[n], 1)
+    for n in range(totals.shape[0]):
+        totals[n : n + 1, :] = back[n * ROWS + MODES : n * ROWS + MODES + 1, :]
     for pair in range(width // WIDE):
         at = slice(pair * WIDE, (pair + 1) * WIDE)
-        scaled[:, at] = from_carry(cuts, back, pair, length, True)
-    step = length // COPIES
-    for i in range(COPIES):
-        copies[i].wait()
-        here = slice(i * step, (i + 1) * step)
-        sums = []
-        for at in tiles_at(width):
-            value = (local[here, at] + scaled[here, at]) * gain[:, at]
-            scaled[here, at] = value
-            sums.append(value * feats[here, at].astype(f32))
-        partial[here, :] = tree(sums)
-    inner[...] = lane_sums(partial[...])
+        carried[:, at] = from_carry(cuts, back, pair, length, True)
+    inner[...] = inner_local[...] + inner_sums(carried, feats, gain, partial)
+    wait_all(copies)
 
 
 def forward_kernel(
-    cuts, back, local, gate, grad_in, gain, mixed, grad_gate,
-    carried, grad, mixed_v, grad_gate_v, sems, sems_in,
+    cuts, back, local, gate, grad, gain, mixed, grad_gate, carried, mixed_v, grad_gate_v, sems
 ):
     length, width = gate.shape
-    copies_in = row_copies(grad_in, grad, sems_in)
     for pair in range(width // WIDE):
         at = slice(pair * WIDE, (pair + 1) * WIDE)
         carried[:, at] = from_carry(cuts, back, pair, length, False)
     copies = []
-    step = length // COPIES
-    for i in range(COPIES):
-        copies_in[i].wait()
+    step = length // BLOCKS
+    for i in range(BLOCKS):
         here = slice(i * step, (i + 1) * step)
         for at in tiles_at(width):
             conv = (local[here, at] + carried[here, at]) * gain[:, at]
             mixed_v[here, at] = (gate[here, at].astype(f32) * conv).astype(jnp.bfloat16)
             grad_gate_v[here, at] = (grad[here, at].astype(f32) * conv).astype(jnp.bfloat16)
-        at = pl.ds(i * step, step)
-        for n, (src, dst) in enumerate(((mixed_v, mixed), (grad_gate_v, grad_gate))):
-            copies.append(pltpu.make_async_copy(src.at[at, :], dst.at[at, :], sems.at[n, i]))
-            copies[-1].start()
+        if (i + 1) % (BLOCKS // COPIES) == 0:
+            part = (i + 1) // (BLOCKS // COPIES) - 1
+            for n, (src, dst) in enumerate(((mixed_v, mixed), (grad_gate_v, grad_gate))):
+                copies.append(row_copy(src, dst, sems.at[n], part))
+                copies[-1].start()
     wait_all(copies)
 
 
 def feature_kernel(
-    full_width, scaled, feats, inverse, i0, i1, i2, i3, own, other,
+    full_width, local, carried, feats, gain, inverse, i0, i1, i2, i3, own, other,
     out, modes, gains, out_v, sems,
 ):
     length, width = feats.shape
     scale = column(inverse[...])
     factor = column(total_row((i0, i1, i2, i3))) * scale * scale / full_width
     copies = []
-    step = length // COPIES
-    for i in range(COPIES):
+    step = length // BLOCKS
+    for i in range(BLOCKS):
         here = slice(i * step, (i + 1) * step)
         for at in tiles_at(width):
-            value = scale[here] * (scaled[here, at] - feats[here, at].astype(f32) * factor[here])
+            scaled = (local[here, at] + carried[here, at]) * gain[:, at]
+            value = scale[here] * (scaled - feats[here, at].astype(f32) * factor[here])
             out_v[here, at] = value.astype(jnp.bfloat16)
-        at = pl.ds(i * step, step)
-        copies.append(pltpu.make_async_copy(out_v.at[at, :], out.at[at, :], sems.at[i]))
-        copies[-1].start()
+        if (i + 1) % (BLOCKS // COPIES) == 0:
+            copies.append(row_copy(out_v, out, sems, (i + 1) // (BLOCKS // COPIES) - 1))
+            copies[-1].start()
 
     total = own[...] + other[...]
     count = total.shape[0]
@@ -607,7 +645,12 @@
     work = length * width * MODES
     wide = (length, width)
     scan_shape = here((length * tiles, LANES), f32)
-    message = pltpu.HBM((count, MODES + EXTRA, LANES), f32)
+    message = pltpu.HBM((count * ROWS, LANES), f32)
+
+    def exchange(value):
+        value = value.reshape(count, 1, ROWS * LANES)
+        return lax.all_to_all(value, "ctx", 0, 0, tiled=True).reshape(message.shape)
+
     state_scratch = pltpu.VMEM((TILES * MODES, LANES), f32)
 
     def call(kernel, name, in_specs, out_specs, out_shape, scratch, flops):
@@ -666,13 +709,20 @@
 
     scan_scratch = pltpu.VMEM((length * TILES, LANES), f32)
     message_scratch = pltpu.VMEM(message.shape, f32)
-    msg, inverse = call(
+    msg, inverse, late_grad = call(
         lambda *refs: state_kernel(full_width, *refs),
         "states",
         [smem, smem] + [vmem] * 9,
-        [hbm, vmem],
-        [message, here((1, length), f32)],
-        [message_scratch, scan_scratch, state_scratch, state_scratch, dma((HALVES,))],
+        [hbm, vmem, hbm],
+        [message, here((1, length), f32), pltpu.HBM((length * tiles, LANES), f32)],
+        [
+            message_scratch,
+            scan_scratch,
+            state_scratch,
+            state_scratch,
+            dma((HALVES,)),
+            dma((COPIES,)),
+        ],
         4 * work,
     )(segments, cuts, feats, grad_scan, *squares, table, gain_table, adjoint)
 
@@ -680,16 +730,30 @@
         return call(
             lambda *refs: local_kernel(backward, *refs),
             "local_backward" if backward else "local_forward",
-            [smem, smem] + [vmem] * len(sources),
-            hbm,
-            pltpu.HBM(wide, f32),
-            [scan_scratch, pltpu.VMEM(wide, f32), dma((HALVES,))]
-            + ([] if backward else [scan_scratch]),
+            [smem, smem] + ([hbm, hbm, hbm, vmem] if backward else [vmem, hbm, vmem]),
+            [hbm, vmem, vmem] if backward else [vmem, hbm],
+            [pltpu.HBM(wide, f32), here((1, length), f32), here(wide, jnp.bfloat16)]
+            if backward
+            else [here(wide, f32), pltpu.HBM(table.shape, f32)],
+            [scan_scratch, dma((COPIES,))]
+            + (
+                [
+                    pltpu.VMEM(wide, f32),
+                    dma((HALVES,)),
+                    pltpu.VMEM((length, LANES), f32),
+                    pltpu.VMEM((length * tiles, LANES), f32),
+                    dma((COPIES,)),
+                    pltpu.VMEM(table.shape, f32),
+                    dma((1,)),
+                ]
+                if backward
+                else [scan_scratch, pltpu.VMEM(wide, jnp.bfloat16), dma((1,))]
+            ),
             4 * work,
         )(segments, cuts, *sources)
 
-    conv_local = local(False, cuts, feats, table, inverse)
-    msg = lax.all_to_all(msg, "ctx", 0, 0, tiled=True)
+    conv_local, late_table = local(False, cuts, table, raw[0], inverse)
+    msg = exchange(msg)
     late_cuts, msg, conv_local = lax.optimization_barrier((cuts, msg, conv_local))
 
     own = lax.axis_index("ctx").astype(jnp.int32).reshape(1)
@@ -703,38 +767,46 @@
         32 * count * MODES * LANES,
     )(own, msg, rates.T, residue.T, gain_row)
 
-    grad_local = local(True, late_cuts, grad_scan, table)
-    back = lax.all_to_all(back, "ctx", 0, 0, tiled=True)
+    grad_local, inner_local, feats = local(
+        True, late_cuts, *in_hbm(late_table, late_grad), raw[0], gain_row
+    )
+    back = exchange(back)
 
     matmuls = 3 * 2 * length * width * WIDE
-    scaled, inner, totals = call(
+    carried, inner, totals, gate, grad = call(
         backward_kernel,
         "backward",
-        [smem, vmem, hbm, vmem, vmem],
-        [vmem] * 3,
-        [here(wide, f32), here((1, length), f32), here((count, LANES), f32)],
-        [pltpu.VMEM((length, LANES), f32), pltpu.VMEM(wide, f32), dma((COPIES,))],
+        [smem] + [vmem] * 4 + [hbm] * 2,
+        [vmem] * 5,
+        [
+            here(wide, f32),
+            here((1, length), f32),
+            here((count, LANES), f32),
+            here(wide, jnp.bfloat16),
+            here(wide, jnp.bfloat16),
+        ],
+        [pltpu.VMEM((length, LANES), f32), dma((2, COPIES))],
         matmuls,
-    )(cuts, back, *in_hbm(grad_local), feats, gain_row)
+    )(cuts, back, inner_local, feats, gain_row, raw[1], raw[2])
     inner = all_parts(inner)
     other = lax.ppermute(totals, "dp", [(i, (i + 1) % size) for i in range(size)])
 
     mixed, grad_gate = call(
         forward_kernel,
         "forward",
-        [smem] + [vmem] * 3 + [hbm, vmem],
+        [smem] + [vmem] * 5,
         [hbm] * 2,
         [jax.ShapeDtypeStruct(wide, jnp.bfloat16)] * 2,
         [pltpu.VMEM(wide, f32)]
-        + [pltpu.VMEM(wide, jnp.bfloat16)] * 3
-        + [dma((2, COPIES)), dma((COPIES,))],
+        + [pltpu.VMEM(wide, jnp.bfloat16)] * 2
+        + [dma((2, COPIES))],
         matmuls,
-    )(cuts, back, conv_local, gate_in[0], raw[2], gain_row)
+    )(cuts, back, conv_local, gate, grad, gain_row)
 
     grad_features, grad_residue, grad_gain = call(
         lambda *refs: feature_kernel(full_width, *refs),
         "features",
-        [vmem] * 9,
+        [vmem] * 11,
         [hbm, vmem, vmem],
         [
             jax.ShapeDtypeStruct(wide, jnp.bfloat16),
@@ -743,7 +815,7 @@
         ],
         [pltpu.VMEM(wide, jnp.bfloat16), dma((COPIES,))],
         4 * length * width,
-    )(scaled, feats, inverse, *inner, totals, other)
+    )(grad_local, carried, feats, gain_row, inverse, *inner, totals, other)
     return (
         mixed[None],
         grad_features[None],

time: 82.5 us -> 75.7 us (0.918)
  waiting for transfers between devices: 10.9 us -> 5.8 us
  Pallas kernels: 40.2 us -> 38.7 us
    all_to_all x2, waiting for transfers between devices: 10.9 us -> 5.78 us  [exchange(): return lax.all_to_all(value, 'ctx', 0, 0, tiled=True).reshape(message.shape)]
    pallas_call x2, Pallas kernels: 7.61 us -> 5.51 us  [the longest x1 3.29 us: shards(): call(forward_kernel, 'forward', [smem] + [vmem] * 5, [hbm] * 2, [jax.Shap...]
    pallas_call x2, Pallas kernels: 13.9 us -> 15.8 us  [local(): call(lambda *refs: local_kernel(backward, *refs), 'local_backward' if bac...]
    pallas_call x1, Pallas kernels: 2.46 us -> 1.25 us  [shards(): call(lambda *refs: carry_kernel(length, norm_factor, *refs), 'carries', [...]
  transfers between devices with their start and end apart: 9 -> 9, of which waited for: 2 -> 2; matrix products, arithmetic and copies ran while one was open for 0% -> 0% of each run, Pallas kernels for 26% -> 30%
where the time goes in v3:
time: 75.7 us; the launch traced here: 75.4 us
  Pallas kernels  38.7 us (51%)
  starting transfers between devices  29.8 us (39%)
  waiting for transfers between devices  5.8 us (8%)
  between operations  0.98 us (1%)
    all_to_all x2, starting transfers between devices, exchange(): return lax.all_to_all(value, 'ctx', 0, 0, tiled=True).reshape(message.shape)  16.9 us
    pallas_call x2, Pallas kernels, local(): call(lambda *refs: local_kernel(backward, *refs), 'local_backward' if bac...  15.8 us
    ppermute x6, starting transfers between devices, all_parts(): lax.ppermute(value, 'tensor', [(i, (i + d) % size) for i in range(size)])  8.69 us
    pallas_call x1, Pallas kernels, shards(): call(lambda *refs: state_kernel(full_width, *refs), 'states', [smem, smem...  7.44 us
    all_to_all x2, waiting for transfers between devices, exchange(): return lax.all_to_all(value, 'ctx', 0, 0, tiled=True).reshape(message.shape)  5.78 us
    ppermute x1, starting transfers between devices, shards(): lax.ppermute(totals, 'dp', [(i, (i + 1) % size) for i in range(size)])  4.23 us
    pallas_call x1, Pallas kernels, shards(): call(forward_kernel, 'forward', [smem] + [vmem] * 5, [hbm] * 2, [jax.Shap...  3.29 us
    pallas_call x1, Pallas kernels, shards(): call(load_kernel, 'load', [hbm] * 6, [vmem] * 4 + [smem], [here(wide, jnp...  3.19 us
  transfers between devices with their start and end apart: 9, of which 2 were waited for; matrix products, arithmetic and copies ran while one was open for 0% of the time, Pallas kernels for 30%

profile of v3, /device:TPU:1, one launch (start us, length us, event | category | flops | bytes accessed | tf_op | source)
XLA Modules:
  0.0 75.4 jit_solution(17600636248975793722)
XLA Ops:
  0.7 3.2 %load.1 = (bf16[256,2048]{1,0:T(8,128)(2,1)S(1)}, f32[4096,128]{1,0:T(8,128)S(1)}, f32[1,256]{1,0:T(1,128)S(1)}, f32[32,16,128]{2,1,0:T(8,128)S(1)}, s32[4]{0:T(128)S(1)}) custom-call(bf16[256,2048]{1,0:T(8,128)(2,1)} %bitcast.30, bf16[256,2048]{1,0:T(8,128)(2,1)} %bitcast.33, bf16[256,2048]{1,0:T(8,128)(2,1)} %bitcast.35, f32[16,128]{1,0:T(8,128)} %bitcast.26, ...), custom_call_target="tpu_custom_call" | custom-call | flops 1 | bytes 1 | tf_op jit(solution)/shard_map/load/pallas_call | solution.py:675
  3.8 2.2 %collective-permute-start = (f32[1,256]{1,0:T(1,128)S(1)}, f32[1,256]{1,0:T(1,128)S(1)}, u32[]{:S(2)}, u32[]{:S(2)}) collective-permute-start(f32[1,256]{1,0:T(1,128)S(1)} %get-tuple-element.34.refs_4_), channel_id=1, source_target_pairs={{0,1},{1,2},{2,3},{3,0},{4,5},{5,6},{6,7},{7,4},{8,9},{9,10},{10,1... | collective-permute-start | bytes 3080 | tf_op jit(solution)/shard_map/ppermute | solution.py:624
  6.1 2.6 %collective-permute-start.1 = (f32[1,256]{1,0:T(1,128)S(1)}, f32[1,256]{1,0:T(1,128)S(1)}, u32[]{:S(2)}, u32[]{:S(2)}) collective-permute-start(f32[1,256]{1,0:T(1,128)S(1)} %get-tuple-element.34.refs_4_), channel_id=1, source_target_pairs={{0,2},{1,3},{2,0},{3,1},{4,6},{5,7},{6,4},{7,5},{8,10},{9,11},{10,... | collective-permute-start | bytes 3080 | tf_op jit(solution)/shard_map/ppermute | solution.py:624
  8.7 1.1 %collective-permute-start.2 = (f32[1,256]{1,0:T(1,128)S(1)}, f32[1,256]{1,0:T(1,128)S(1)}, u32[]{:S(2)}, u32[]{:S(2)}) collective-permute-start(f32[1,256]{1,0:T(1,128)S(1)} %get-tuple-element.34.refs_4_), channel_id=1, source_target_pairs={{0,3},{1,0},{2,1},{3,2},{4,7},{5,4},{6,5},{7,6},{8,11},{9,8},{10,9... | collective-permute-start | bytes 3080 | tf_op jit(solution)/shard_map/ppermute | solution.py:624
  9.7 3.2 %adjoint.1.refs_10_ = f32[256,128]{1,0:T(8,128)S(1)} custom-call(s32[1,256]{1,0:T(1,128)S(1)} %copy-done.4, s32[4]{0:T(128)S(1)} %get-tuple-element.41.cuts.refs_1_, f32[4096,128]{1,0:T(8,128)S(1)} %get-tuple-element.33.grad_scan.refs_3_, f32[32,16,128]{2,1,0:T(8,128)S(1)} %get-tuple-element.35.table.refs_8_.refs_2_), custom_call_target="tpu_custom_call" | custom-call | flops 16 | bytes 1 | tf_op jit(solution)/shard_map/adjoint/pallas_call | solution.py:700
  13.0 0.0 collective-permute-done.2.refs_7_
  13.0 0.0 copy-start.2
  13.0 0.0 copy-start.3
  13.0 7.4 %states.1 = (f32[576,128]{1,0:T(8,128)}, f32[1,256]{1,0:T(1,128)S(1)}, f32[4096,128]{1,0:T(8,128)}) custom-call(s32[1,256]{1,0:T(1,128)S(1)} %copy-done.4, s32[4]{0:T(128)S(1)} %get-tuple-element.41.cuts.refs_1_, bf16[256,2048]{1,0:T(8,128)(2,1)S(1)} %get-tuple-element.32.refs_2_, f32[4096,128]{1,0:T(8,128)S(1)} %get-tuple-element.33.grad_scan.refs_3_, ...), custom_call_target="tpu_custom_call" | custom-call | flops 33 | bytes 1 | tf_op jit(solution)/shard_map/states/pallas_call | solution.py:712
  20.5 11.0 %all-to-all-start = ((f32[32,1,2304]{2,1,0:T(1,128)}), f32[32,1,2304]{2,1,0:T(1,128)S(1)}, u32[]{:S(2)}, u32[]{:S(2)}) async-start(f32[32,1,2304]{2,1,0:T(1,128)} %bitcast.38), calls=%async_computation | async-start | bytes 589824 | tf_op jit(solution)/shard_map/all_to_all | solution.py:652
  31.5 7.6 %local_forward.1 = (f32[256,2048]{1,0:T(8,128)S(1)}, f32[32,16,128]{2,1,0:T(8,128)}) custom-call(s32[1,256]{1,0:T(1,128)S(1)} %copy-done.4, s32[4]{0:T(128)S(1)} %get-tuple-element.41.cuts.refs_1_, f32[32,16,128]{2,1,0:T(8,128)S(1)} %get-tuple-element.35.table.refs_8_.refs_2_, bf16[256,2048]{1,0:T(8,128)(2,1)} %bitcast.31, ...), custom_call_target="tpu_custom_call" | custom-call | flops 33 | bytes 1 | tf_op jit(solution)/shard_map/local_forward/pallas_call | solution.py:730
  39.1 3.4 %all-to-all-done = f32[32,1,2304]{2,1,0:T(1,128)S(1)} async-done(((f32[32,1,2304]{2,1,0:T(1,128)}), f32[32,1,2304]{2,1,0:T(1,128)S(1)}, u32[]{:S(2)}, u32[]{:S(2)}) %all-to-all-start) | async-done | bytes 294944 | tf_op jit(solution)/shard_map/all_to_all | solution.py:652
  42.5 1.2 %carries.1 = f32[576,128]{1,0:T(8,128)} custom-call(s32[1]{0:T(128)} %bitcast.5.refs_0_, f32[576,128]{1,0:T(8,128)S(1)} %bitcast.19, f32[16,128]{1,0:T(8,128)S(1)} %bitcast.27, f32[16,128]{1,0:T(8,128)S(1)} %bitcast.29, f32[1,2048]{1,0:T(1,128)S(1)} %bitcast.21), custom_call_target="tpu_custom_call" | custom-call | flops 2 | bytes 1 | tf_op jit(solution)/shard_map/carries/pallas_call | solution.py:760
  43.7 5.9 %all-to-all-start.1 = ((f32[32,1,2304]{2,1,0:T(1,128)}), f32[32,1,2304]{2,1,0:T(1,128)S(1)}, u32[]{:S(2)}, u32[]{:S(2)}) async-start(f32[32,1,2304]{2,1,0:T(1,128)} %bitcast.37), calls=%async_computation.1 | async-start | bytes 589824 | tf_op jit(solution)/shard_map/all_to_all | solution.py:652
  49.6 8.2 %local_backward.1 = (f32[256,2048]{1,0:T(8,128)}, f32[1,256]{1,0:T(1,128)S(1)}, bf16[256,2048]{1,0:T(8,128)(2,1)S(1)}) custom-call(s32[1,256]{1,0:T(1,128)S(1)} %copy-done.4, s32[4]{0:T(128)S(1)} %get-tuple-element.41.cuts.refs_1_, f32[32,16,128]{2,1,0:T(8,128)} %get-tuple-element.42.refs_2_, f32[4096,128]{1,0:T(8,128)} %get-tuple-element.43.refs_3_, ...), custom_call_target="tpu_custom_call" | custom-call | flops 33 | bytes 1 | tf_op jit(solution)/shard_map/local_backward/pallas_call | solution.py:730
  57.9 2.4 %all-to-all-done.1 = f32[32,1,2304]{2,1,0:T(1,128)S(1)} async-done(((f32[32,1,2304]{2,1,0:T(1,128)}), f32[32,1,2304]{2,1,0:T(1,128)S(1)}, u32[]{:S(2)}, u32[]{:S(2)}) %all-to-all-start.1) | async-done | bytes 294944 | tf_op jit(solution)/shard_map/all_to_all | solution.py:652
  60.3 2.2 %backward.1 = (f32[256,2048]{1,0:T(8,128)S(1)}, f32[1,256]{1,0:T(1,128)S(1)}, f32[32,128]{1,0:T(8,128)S(1)}, bf16[256,2048]{1,0:T(8,128)(2,1)S(1)}, bf16[256,2048]{1,0:T(8,128)(2,1)S(1)}) custom-call(s32[4]{0:T(128)S(1)} %get-tuple-element.41.cuts.refs_1_, f32[576,128]{1,0:T(8,128)S(1)} %bitcast.17, f32[1,256]{1,0:T(1,128)S(1)} %get-tuple-element.44.inner_local, ...), custom_call_target="tpu_custom_call" | custom-call | flops 805 | bytes 1 | tf_op jit(solution)/shard_map/backward/pallas_call | solution.py:776
  62.5 4.2 %collective-permute-start.6 = (f32[32,128]{1,0:T(8,128)S(1)}, f32[32,128]{1,0:T(8,128)S(1)}, u32[]{:S(2)}, u32[]{:S(2)}) collective-permute-start(f32[32,128]{1,0:T(8,128)S(1)} %get-tuple-element.52.refs_9_), channel_id=1, source_target_pairs={{0,128},{128,0},{1,129},{129,1},{2,130},{130,2},{3,131},{131,3},{4... | collective-permute-start | bytes 49160 | tf_op jit(solution)/shard_map/ppermute | solution.py:792
  66.8 0.4 collective-permute-start.3
  67.2 1.5 %collective-permute-start.4 = (f32[1,256]{1,0:T(1,128)S(1)}, f32[1,256]{1,0:T(1,128)S(1)}, u32[]{:S(2)}, u32[]{:S(2)}) collective-permute-start(f32[1,256]{1,0:T(1,128)S(1)} %get-tuple-element.51.refs_5_), channel_id=1, source_target_pairs={{0,2},{1,3},{2,0},{3,1},{4,6},{5,7},{6,4},{7,5},{8,10},{9,11},{10,... | collective-permute-start | bytes 3080 | tf_op jit(solution)/shard_map/ppermute | solution.py:624
  68.7 0.9 %collective-permute-start.5 = (f32[1,256]{1,0:T(1,128)S(1)}, f32[1,256]{1,0:T(1,128)S(1)}, u32[]{:S(2)}, u32[]{:S(2)}) collective-permute-start(f32[1,256]{1,0:T(1,128)S(1)} %get-tuple-element.51.refs_5_), channel_id=1, source_target_pairs={{0,3},{1,0},{2,1},{3,2},{4,7},{5,4},{6,5},{7,6},{8,11},{9,8},{10,9... | collective-permute-start | bytes 3080 | tf_op jit(solution)/shard_map/ppermute | solution.py:624
  69.5 3.3 %forward.1 = (bf16[256,2048]{1,0:T(8,128)(2,1)}, bf16[256,2048]{1,0:T(8,128)(2,1)}) custom-call(s32[4]{0:T(128)S(1)} %get-tuple-element.41.cuts.refs_1_, f32[576,128]{1,0:T(8,128)S(1)} %bitcast.18, f32[256,2048]{1,0:T(8,128)S(1)} %get-tuple-element.40.local, bf16[256,2048]{1,0:T(8,128)(2,1)S(1)} %get-tuple-element.46.gate, ...), custom_call_target="tpu_custom_call" | custom-call | flops 805 | bytes 1 | tf_op jit(solution)/shard_map/forward/pallas_call | solution.py:794
  72.8 0.0 collective-permute-done.3.refs_6_
  72.9 2.3 %features.1 = (bf16[256,2048]{1,0:T(8,128)(2,1)}, f32[16,128]{1,0:T(8,128)}, f32[16,128]{1,0:T(8,128)}) custom-call(f32[256,2048]{1,0:T(8,128)S(1)} %copy-done, f32[256,2048]{1,0:T(8,128)S(1)} %get-tuple-element.50.refs_1_, bf16[256,2048]{1,0:T(8,128)(2,1)S(1)} %get-tuple-element.45.feats.refs_2_, f32[1,2048]{1,0:T(1,128)S(1)} %bitcast.25, ...), custom_call_target="tpu_custom_call" | custom-call | flops 2 | bytes 1 | tf_op jit(solution)/shard_map/features/pallas_call | solution.py:806
  (13 shorter events, 0.0 us)
Async XLA Ops:
  0.6 9.1 %copy-start.4 = (s32[1,256]{1,0:T(1,128)S(1)}, s32[1,256]{1,0:T(1,128)}, u32[]{:S(2)}) copy-start(s32[1,256]{1,0:T(1,128)} %refs_0_.5) | copy-start | bytes 3076
  0.6 12.3 %copy-start.1 = (f32[2048]{0:T(1024)S(1)}, f32[2048]{0:T(1024)}, u32[]{:S(2)}) copy-start(f32[2048]{0:T(1024)} %param.10) | copy-start | bytes 24580
  3.8 9.1 %collective-permute-start = (f32[1,256]{1,0:T(1,128)S(1)}, f32[1,256]{1,0:T(1,128)S(1)}, u32[]{:S(2)}, u32[]{:S(2)}) collective-permute-start(f32[1,256]{1,0:T(1,128)S(1)} %get-tuple-element.34.refs_4_), channel_id=1, source_target_pairs={{0,1},{1,2},{2,3},{3,0},{4,5},{5,6},{6,7},{7,4},{8,9},{9,10},{10,1... | collective-permute-start | bytes 3080 | tf_op jit(solution)/shard_map/ppermute | solution.py:624
  6.1 6.9 %collective-permute-start.1 = (f32[1,256]{1,0:T(1,128)S(1)}, f32[1,256]{1,0:T(1,128)S(1)}, u32[]{:S(2)}, u32[]{:S(2)}) collective-permute-start(f32[1,256]{1,0:T(1,128)S(1)} %get-tuple-element.34.refs_4_), channel_id=1, source_target_pairs={{0,2},{1,3},{2,0},{3,1},{4,6},{5,7},{6,4},{7,5},{8,10},{9,11},{10,... | collective-permute-start | bytes 3080 | tf_op jit(solution)/shard_map/ppermute | solution.py:624
  8.7 4.3 %collective-permute-start.2 = (f32[1,256]{1,0:T(1,128)S(1)}, f32[1,256]{1,0:T(1,128)S(1)}, u32[]{:S(2)}, u32[]{:S(2)}) collective-permute-start(f32[1,256]{1,0:T(1,128)S(1)} %get-tuple-element.34.refs_4_), channel_id=1, source_target_pairs={{0,3},{1,0},{2,1},{3,2},{4,7},{5,4},{6,5},{7,6},{8,11},{9,8},{10,9... | collective-permute-start | bytes 3080 | tf_op jit(solution)/shard_map/ppermute | solution.py:624
  13.0 29.5 %copy-start.2 = (f32[128,16]{0,1:T(8,128)S(1)}, f32[128,16]{0,1:T(8,128)}, u32[]{:S(2)}) copy-start(f32[128,16]{0,1:T(8,128)} %param.12) | copy-start | bytes 24580
  13.0 29.5 %copy-start.3 = (f32[128,16]{0,1:T(8,128)S(1)}, f32[128,16]{0,1:T(8,128)}, u32[]{:S(2)}) copy-start(f32[128,16]{0,1:T(8,128)} %param.11) | copy-start | bytes 24580
  20.5 22.0 %all-to-all-start = ((f32[32,1,2304]{2,1,0:T(1,128)}), f32[32,1,2304]{2,1,0:T(1,128)S(1)}, u32[]{:S(2)}, u32[]{:S(2)}) async-start(f32[32,1,2304]{2,1,0:T(1,128)} %bitcast.38), calls=%async_computation | async-start | bytes 589824 | tf_op jit(solution)/shard_map/all_to_all | solution.py:652
  43.7 16.6 %all-to-all-start.1 = ((f32[32,1,2304]{2,1,0:T(1,128)}), f32[32,1,2304]{2,1,0:T(1,128)S(1)}, u32[]{:S(2)}, u32[]{:S(2)}) async-start(f32[32,1,2304]{2,1,0:T(1,128)} %bitcast.37), calls=%async_computation.1 | async-start | bytes 589824 | tf_op jit(solution)/shard_map/all_to_all | solution.py:652
  62.5 10.4 %collective-permute-start.6 = (f32[32,128]{1,0:T(8,128)S(1)}, f32[32,128]{1,0:T(8,128)S(1)}, u32[]{:S(2)}, u32[]{:S(2)}) collective-permute-start(f32[32,128]{1,0:T(8,128)S(1)} %get-tuple-element.52.refs_9_), channel_id=1, source_target_pairs={{0,128},{128,0},{1,129},{129,1},{2,130},{130,2},{3,131},{131,3},{4... | collective-permute-start | bytes 49160 | tf_op jit(solution)/shard_map/ppermute | solution.py:792
  66.8 6.1 %collective-permute-start.3 = (f32[1,256]{1,0:T(1,128)S(1)}, f32[1,256]{1,0:T(1,128)S(1)}, u32[]{:S(2)}, u32[]{:S(2)}) collective-permute-start(f32[1,256]{1,0:T(1,128)S(1)} %get-tuple-element.51.refs_5_), channel_id=1, source_target_pairs={{0,1},{1,2},{2,3},{3,0},{4,5},{5,6},{6,7},{7,4},{8,9},{9,10},{10,1... | collective-permute-start | bytes 3080 | tf_op jit(solution)/shard_map/ppermute | solution.py:624
  67.2 5.7 %collective-permute-start.4 = (f32[1,256]{1,0:T(1,128)S(1)}, f32[1,256]{1,0:T(1,128)S(1)}, u32[]{:S(2)}, u32[]{:S(2)}) collective-permute-start(f32[1,256]{1,0:T(1,128)S(1)} %get-tuple-element.51.refs_5_), channel_id=1, source_target_pairs={{0,2},{1,3},{2,0},{3,1},{4,6},{5,7},{6,4},{7,5},{8,10},{9,11},{10,... | collective-permute-start | bytes 3080 | tf_op jit(solution)/shard_map/ppermute | solution.py:624
  68.7 4.2 %collective-permute-start.5 = (f32[1,256]{1,0:T(1,128)S(1)}, f32[1,256]{1,0:T(1,128)S(1)}, u32[]{:S(2)}, u32[]{:S(2)}) collective-permute-start(f32[1,256]{1,0:T(1,128)S(1)} %get-tuple-element.51.refs_5_), channel_id=1, source_target_pairs={{0,3},{1,0},{2,1},{3,2},{4,7},{5,4},{6,5},{7,6},{8,11},{9,8},{10,9... | collective-permute-start | bytes 3080 | tf_op jit(solution)/shard_map/ppermute | solution.py:624
  69.5 3.3 %copy-start = (f32[256,2048]{1,0:T(8,128)S(1)}, f32[256,2048]{1,0:T(8,128)}, u32[]{:S(2)}) copy-start(f32[256,2048]{1,0:T(8,128)} %get-tuple-element.49.refs_0_) | copy-start | bytes 6291460

commit v4 on v3

--- a/solution.py
+++ b/solution.py
@@ -141,8 +141,20 @@
         )
         return jnp.where(broken, after, stop), states
 
-    start = jnp.int32(groups if backward else 0)
-    return lax.fori_loop(0, COUNT, stretch, (start, carry))[1]
+    def general(carry):
+        start = jnp.int32(groups if backward else 0)
+        return lax.fori_loop(0, COUNT, stretch, (start, carry))[1]
+
+    def unbroken(carry):
+        def body(i, carry):
+            return run(groups - 1 - i if backward else i, carry, False)
+
+        return lax.fori_loop(0, groups, body, carry)
+
+    broken = cuts[0] < 0
+    for p in range(COUNT - 1):
+        broken = broken | ((cuts[p] > 0) & (cuts[p] < length))
+    return lax.cond(broken, general, unbroken, carry)
 
 
 def decayed(decay, state, keep):
@@ -166,7 +178,7 @@
 
 def load_kernel(
     feats_in, gate_in, grad_in, rates_in, residue_in, seg_in,
-    feats, grad_scan, squares, table, cuts,
+    feats, grad_scan, squares, table, rates_out, cuts,
     gate, grad, rates, residue, seg, sems, small_sems,
 ):
     length, width = feats.shape
@@ -181,6 +193,7 @@
     for copy in small:
         copy.wait()
     expand(rates, residue, seg, table, cuts)
+    rates_out[...] = rates[...]
     wait_all(feat_copies)
     partial = jnp.zeros((length, LANES), f32)
     for tile in range(width // LANES):
@@ -229,23 +242,34 @@
     cuts[COUNT - 1] = seg.shape[1]
 
 
-def adjoint_kernel(seg, cuts, grad_scan, table, adj):
-    length = seg.shape[1]
-
-    def run(half, _):
-        decay = decay_of(table, half)
-
-        def step(t, states, keep):
-            value = row_at(grad_scan, half, length, t)
-            return tuple(decayed(decay[r], states[r], keep) + value for r in range(MODES))
-
-        zero = jnp.zeros((TILES, LANES), f32)
-        states = scan(length, seg, cuts, step, (zero,) * MODES, True)
-        for r in range(MODES):
-            adj[state_rows(half, r), :] = states[r]
-        return _
-
-    lax.fori_loop(0, HALVES, run, 0)
+def adjoint_kernel(cuts, grad_scan, rates, adj):
+    length = grad_scan.shape[0] // (HALVES * TILES)
+    edge = jnp.int32(length)
+    for p in range(COUNT - 1):
+        edge = jnp.minimum(edge, jnp.where(cuts[p] > 0, cuts[p], length))
+    first = lax.broadcasted_iota(jnp.int32, (length, LANES), 0) < edge
+    lag = lax.broadcasted_iota(jnp.int32, (MODES, LANES), 1).astype(f32)
+    rate = rates[...]
+    further = jnp.exp(-float(LANES) * rate)
+    share = LANES // GROUP
+    row = lax.broadcasted_iota(jnp.int32, (LANES, LANES), 0) // MODES
+    own = row == lax.broadcasted_iota(jnp.int32, (LANES, LANES), 1) // GROUP
+    dot = lambda x, y: jnp.dot(x, y, preferred_element_type=f32)
+    for tile in range(HALVES * TILES):
+        value = grad_scan[scan_rows(tile // TILES, tile % TILES, length), :]
+        high, low = split(jnp.where(first, value, 0.0))
+        blocks = []
+        for group in range(tile * share, (tile + 1) * share):
+            parts = [jnp.exp(-lag * rate[:, group : group + 1])]
+            for _ in range(length // LANES - 1):
+                parts.append(parts[-1] * further[:, group : group + 1])
+            blocks.append(jnp.concatenate(parts, axis=1))
+        near, far = split(jnp.concatenate(blocks, axis=0))
+        full = dot(near, high) + (dot(far, high) + dot(near, low))
+        full = jnp.where(own, full, 0.0)
+        adj[tile * MODES : (tile + 1) * MODES, :] = tree(
+            [full[n * MODES : (n + 1) * MODES, :] for n in range(share)]
+        )
 
 
 def state_kernel(
@@ -552,33 +576,28 @@
 
 
 def forward_kernel(
-    cuts, back, local, gate, grad, gain, mixed, grad_gate, carried, mixed_v, grad_gate_v, sems
+    cuts, back, local, gate, grad, gain, mixed, grad_gate, carried
 ):
     length, width = gate.shape
     for pair in range(width // WIDE):
         at = slice(pair * WIDE, (pair + 1) * WIDE)
         carried[:, at] = from_carry(cuts, back, pair, length, False)
-    copies = []
     step = length // BLOCKS
     for i in range(BLOCKS):
         here = slice(i * step, (i + 1) * step)
         for at in tiles_at(width):
             conv = (local[here, at] + carried[here, at]) * gain[:, at]
-            mixed_v[here, at] = (gate[here, at].astype(f32) * conv).astype(jnp.bfloat16)
-            grad_gate_v[here, at] = (grad[here, at].astype(f32) * conv).astype(jnp.bfloat16)
-        if (i + 1) % (BLOCKS // COPIES) == 0:
-            part = (i + 1) // (BLOCKS // COPIES) - 1
-            for n, (src, dst) in enumerate(((mixed_v, mixed), (grad_gate_v, grad_gate))):
-                copies.append(row_copy(src, dst, sems.at[n], part))
-                copies[-1].start()
-    wait_all(copies)
+            mixed[here, at] = (gate[here, at].astype(f32) * conv).astype(jnp.bfloat16)
+            grad_gate[here, at] = (grad[here, at].astype(f32) * conv).astype(jnp.bfloat16)
 
 
 def feature_kernel(
-    full_width, local, carried, feats, gain, inverse, i0, i1, i2, i3, own, other,
-    out, modes, gains, out_v, sems,
+    full_width, local, carried, feats, gain, inverse, i0, i1, i2, i3, own, other, mixed_v, grad_gate_v,
+    out, modes, gains, mixed, grad_gate, out_v, sems, gate_sems,
 ):
     length, width = feats.shape
+    gate_copies = row_copies(mixed_v, mixed, gate_sems.at[0])
+    gate_copies += row_copies(grad_gate_v, grad_gate, gate_sems.at[1])
     scale = column(inverse[...])
     factor = column(total_row((i0, i1, i2, i3))) * scale * scale / full_width
     copies = []
@@ -614,8 +633,7 @@
     modes[...] = tree(parts)
     for n in range(count // 2):
         gains[n : n + 1, :] = join(total[2 * n : 2 * n + 1, :], swap(total[2 * n + 1 : 2 * n + 2, :]))
-    for copy in copies:
-        copy.wait()
+    wait_all(copies + gate_copies)
 
 
 def all_parts(value):
@@ -672,16 +690,17 @@
 
     raw = in_hbm(features[0], gate_in[0], grad_out[0], rates.T, residue.T, segments)
     dma = pltpu.SemaphoreType.DMA
-    feats, grad_scan, squares, table, cuts = call(
+    feats, grad_scan, squares, table, rates_here, cuts = call(
         load_kernel,
         "load",
         [hbm] * 6,
-        [vmem] * 4 + [smem],
+        [vmem] * 5 + [smem],
         [
             here(wide, jnp.bfloat16),
             scan_shape,
             here((1, length), f32),
             here((2 * mode_count, tiles, LANES), f32),
+            here((mode_count, group_count), f32),
             jax.ShapeDtypeStruct((COUNT,), jnp.int32),
         ],
         [
@@ -700,12 +719,12 @@
     adjoint = call(
         adjoint_kernel,
         "adjoint",
-        [smem, smem] + [vmem] * 2,
+        [smem] + [vmem] * 2,
         vmem,
         here((tiles * MODES, LANES), f32),
         [],
         2 * work,
-    )(segments, cuts, grad_scan, table)
+    )(cuts, grad_scan, rates_here)
 
     scan_scratch = pltpu.VMEM((length * TILES, LANES), f32)
     message_scratch = pltpu.VMEM(message.shape, f32)
@@ -795,27 +814,27 @@
         forward_kernel,
         "forward",
         [smem] + [vmem] * 5,
-        [hbm] * 2,
-        [jax.ShapeDtypeStruct(wide, jnp.bfloat16)] * 2,
-        [pltpu.VMEM(wide, f32)]
-        + [pltpu.VMEM(wide, jnp.bfloat16)] * 2
-        + [dma((2, COPIES))],
+        [vmem] * 2,
+        [here(wide, jnp.bfloat16)] * 2,
+        [pltpu.VMEM(wide, f32)],
         matmuls,
     )(cuts, back, conv_local, gate, grad, gain_row)
 
-    grad_features, grad_residue, grad_gain = call(
+    grad_features, grad_residue, grad_gain, mixed, grad_gate = call(
         lambda *refs: feature_kernel(full_width, *refs),
         "features",
-        [vmem] * 11,
-        [hbm, vmem, vmem],
+        [vmem] * 13,
+        [hbm, vmem, vmem, hbm, hbm],
         [
             jax.ShapeDtypeStruct(wide, jnp.bfloat16),
             jax.ShapeDtypeStruct((mode_count, group_count), f32),
             jax.ShapeDtypeStruct((tiles, LANES), f32),
+            jax.ShapeDtypeStruct(wide, jnp.bfloat16),
+            jax.ShapeDtypeStruct(wide, jnp.bfloat16),
         ],
-        [pltpu.VMEM(wide, jnp.bfloat16), dma((COPIES,))],
+        [pltpu.VMEM(wide, jnp.bfloat16), dma((COPIES,)), dma((2, COPIES))],
         4 * length * width,
-    )(grad_local, carried, feats, gain_row, inverse, *inner, totals, other)
+    )(grad_local, carried, feats, gain_row, inverse, *inner, totals, other, mixed, grad_gate)
     return (
         mixed[None],
         grad_features[None],

time: 75.7 us -> 73.7 us (0.974)
  Pallas kernels: 38.7 us -> 35.7 us
  waiting for transfers between devices: 5.8 us -> 8.21 us
  starting transfers between devices: 29.8 us -> 28.5 us
    pallas_call x3, Pallas kernels: 9.67 us -> 7.36 us  [the longest x1 3.19 us: shards(): call(load_kernel, 'load', [hbm] * 6, [vmem] * 5 + [smem], [here(wide, jnp...]
    ppermute x6, waiting for transfers between devices: 0.02 us -> 2.29 us  [all_parts(): lax.ppermute(value, 'tensor', [(i, (i + d) % size) for i in range(size)])]
    ppermute x6, starting transfers between devices: 8.69 us -> 6.95 us  [all_parts(): lax.ppermute(value, 'tensor', [(i, (i + d) % size) for i in range(size)])]
  transfers between devices with their start and end apart: 9 -> 9, of which waited for: 2 -> 6; matrix products, arithmetic and copies ran while one was open for 0% -> 0% of each run, Pallas kernels for 30% -> 27%
where the time goes in v4:
time: 73.7 us; the launch traced here: 73.4 us
  Pallas kernels  35.7 us (48%)
  starting transfers between devices  28.5 us (39%)
  waiting for transfers between devices  8.21 us (11%)
  between operations  0.92 us (1%)
    all_to_all x2, starting transfers between devices, exchange(): return lax.all_to_all(value, 'ctx', 0, 0, tiled=True).reshape(message.shape)  17 us
    pallas_call x2, Pallas kernels, local(): call(lambda *refs: local_kernel(backward, *refs), 'local_backward' if bac...  15.5 us
    pallas_call x1, Pallas kernels, shards(): call(lambda *refs: state_kernel(full_width, *refs), 'states', [smem, smem...  7.03 us
    ppermute x6, starting transfers between devices, all_parts(): lax.ppermute(value, 'tensor', [(i, (i + d) % size) for i in range(size)])  6.95 us
    all_to_all x2, waiting for transfers between devices, exchange(): return lax.all_to_all(value, 'ctx', 0, 0, tiled=True).reshape(message.shape)  5.91 us
    ppermute x1, starting transfers between devices, shards(): lax.ppermute(totals, 'dp', [(i, (i + 1) % size) for i in range(size)])  4.59 us
    pallas_call x1, Pallas kernels, shards(): call(load_kernel, 'load', [hbm] * 6, [vmem] * 5 + [smem], [here(wide, jnp...  3.19 us
    pallas_call x1, Pallas kernels, shards(): call(lambda *refs: feature_kernel(full_width, *refs), 'features', [vmem]...  2.39 us
  transfers between devices with their start and end apart: 9, of which 6 were waited for; matrix products, arithmetic and copies ran while one was open for 0% of the time, Pallas kernels for 27%

profile of v4, /device:TPU:1, one launch (start us, length us, event | category | flops | bytes accessed | tf_op | source)
XLA Modules:
  0.0 73.4 jit_solution(9904264976544049666)
XLA Ops:
  0.7 3.2 %load.1 = (bf16[256,2048]{1,0:T(8,128)(2,1)S(1)}, f32[4096,128]{1,0:T(8,128)S(1)}, f32[1,256]{1,0:T(1,128)S(1)}, f32[32,16,128]{2,1,0:T(8,128)S(1)}, f32[16,128]{1,0:T(8,128)S(1)}, /*index=5*/s32[4]{0:T(128)S(1)}) custom-call(bf16[256,2048]{1,0:T(8,128)(2,1)} %bitcast.30, bf16[256,2048]{1,0:T(8,128)(2,1)} %bitcast.33, bf16[256,2048]{1,0:T(8,128)(2,1)} %bitcast.35, ...), custom_call_target="tpu_custom_call" | custom-call | flops 1 | bytes 1 | tf_op jit(solution)/shard_map/load/pallas_call | solution.py:693
  3.8 3.6 %collective-permute-start.2 = (f32[1,256]{1,0:T(1,128)S(1)}, f32[1,256]{1,0:T(1,128)S(1)}, u32[]{:S(2)}, u32[]{:S(2)}) collective-permute-start(f32[1,256]{1,0:T(1,128)S(1)} %get-tuple-element.37.refs_4_), channel_id=1, source_target_pairs={{0,3},{1,0},{2,1},{3,2},{4,7},{5,4},{6,5},{7,6},{8,11},{9,8},{10,9... | collective-permute-start | bytes 3080 | tf_op jit(solution)/shard_map/ppermute | solution.py:642
  7.5 0.3 collective-permute-start.1
  7.8 0.7 collective-permute-start
  8.5 2.0 %adjoint.1.refs_10_ = f32[256,128]{1,0:T(8,128)S(1)} custom-call(s32[4]{0:T(128)S(1)} %get-tuple-element.43.cuts.refs_1_, f32[4096,128]{1,0:T(8,128)S(1)} %get-tuple-element.36.grad_scan.refs_3_, f32[16,128]{1,0:T(8,128)S(1)} %get-tuple-element.39.rates), custom_call_target="tpu_custom_call" | custom-call | flops 16 | bytes 1 | tf_op jit(solution)/shard_map/adjoint/pallas_call | solution.py:719
  10.6 0.8 %collective-permute-done.1.refs_6_ = f32[1,256]{1,0:T(1,128)S(1)} collective-permute-done((f32[1,256]{1,0:T(1,128)S(1)}, f32[1,256]{1,0:T(1,128)S(1)}, u32[]{:S(2)}, u32[]{:S(2)}) %collective-permute-start.1) | collective-permute-done | bytes 1056 | tf_op jit(solution)/shard_map/ppermute | solution.py:642
  11.4 0.1 collective-permute-done.refs_5_
  11.5 7.0 %states.1 = (f32[576,128]{1,0:T(8,128)}, f32[1,256]{1,0:T(1,128)S(1)}, f32[4096,128]{1,0:T(8,128)}) custom-call(s32[1,256]{1,0:T(1,128)S(1)} %copy-done.4, s32[4]{0:T(128)S(1)} %get-tuple-element.43.cuts.refs_1_, bf16[256,2048]{1,0:T(8,128)(2,1)S(1)} %get-tuple-element.35.refs_2_, f32[4096,128]{1,0:T(8,128)S(1)} %get-tuple-element.36.grad_scan.refs_3_, ...), custom_call_target="tpu_custom_call" | custom-call | flops 33 | bytes 1 | tf_op jit(solution)/shard_map/states/pallas_call | solution.py:731
  18.5 11.0 %all-to-all-start = ((f32[32,1,2304]{2,1,0:T(1,128)}), f32[32,1,2304]{2,1,0:T(1,128)S(1)}, u32[]{:S(2)}, u32[]{:S(2)}) async-start(f32[32,1,2304]{2,1,0:T(1,128)} %bitcast.38), calls=%async_computation | async-start | bytes 589824 | tf_op jit(solution)/shard_map/all_to_all | solution.py:670
  29.6 7.4 %local_forward.1 = (f32[256,2048]{1,0:T(8,128)S(1)}, f32[32,16,128]{2,1,0:T(8,128)}) custom-call(s32[1,256]{1,0:T(1,128)S(1)} %copy-done.4, s32[4]{0:T(128)S(1)} %get-tuple-element.43.cuts.refs_1_, f32[32,16,128]{2,1,0:T(8,128)S(1)} %get-tuple-element.38.refs_8_.refs_2_, bf16[256,2048]{1,0:T(8,128)(2,1)} %bitcast.31, f32[1,256]{1,0:T(1,128)S(1)} %get-tuple-element.41.refs_4_), custom_call_target="tpu_custom_call" | custom-call | flops 33 | bytes 1 | tf_op jit(solution)/shard_map/local_forward/pallas_call | solution.py:749
  37.0 3.3 %all-to-all-done = f32[32,1,2304]{2,1,0:T(1,128)S(1)} async-done(((f32[32,1,2304]{2,1,0:T(1,128)}), f32[32,1,2304]{2,1,0:T(1,128)S(1)}, u32[]{:S(2)}, u32[]{:S(2)}) %all-to-all-start) | async-done | bytes 294944 | tf_op jit(solution)/shard_map/all_to_all | solution.py:670
  40.3 1.2 %carries.1 = f32[576,128]{1,0:T(8,128)} custom-call(s32[1]{0:T(128)} %bitcast.9.refs_0_, f32[576,128]{1,0:T(8,128)S(1)} %bitcast.19, f32[16,128]{1,0:T(8,128)S(1)} %bitcast.27, f32[16,128]{1,0:T(8,128)S(1)} %bitcast.29, f32[1,2048]{1,0:T(1,128)S(1)} %bitcast.21), custom_call_target="tpu_custom_call" | custom-call | flops 2 | bytes 1 | tf_op jit(solution)/shard_map/carries/pallas_call | solution.py:779
  41.6 5.9 %all-to-all-start.1 = ((f32[32,1,2304]{2,1,0:T(1,128)}), f32[32,1,2304]{2,1,0:T(1,128)S(1)}, u32[]{:S(2)}, u32[]{:S(2)}) async-start(f32[32,1,2304]{2,1,0:T(1,128)} %bitcast.37), calls=%async_computation.1 | async-start | bytes 589824 | tf_op jit(solution)/shard_map/all_to_all | solution.py:670
  47.5 8.1 %local_backward.1 = (f32[256,2048]{1,0:T(8,128)}, f32[1,256]{1,0:T(1,128)S(1)}, bf16[256,2048]{1,0:T(8,128)(2,1)S(1)}) custom-call(s32[1,256]{1,0:T(1,128)S(1)} %copy-done.4, s32[4]{0:T(128)S(1)} %get-tuple-element.43.cuts.refs_1_, f32[32,16,128]{2,1,0:T(8,128)} %get-tuple-element.44.refs_2_, f32[4096,128]{1,0:T(8,128)} %get-tuple-element.45.refs_3_, ...), custom_call_target="tpu_custom_call" | custom-call | flops 33 | bytes 1 | tf_op jit(solution)/shard_map/local_backward/pallas_call | solution.py:749
  55.6 2.6 %all-to-all-done.1 = f32[32,1,2304]{2,1,0:T(1,128)S(1)} async-done(((f32[32,1,2304]{2,1,0:T(1,128)}), f32[32,1,2304]{2,1,0:T(1,128)S(1)}, u32[]{:S(2)}, u32[]{:S(2)}) %all-to-all-start.1) | async-done | bytes 294944 | tf_op jit(solution)/shard_map/all_to_all | solution.py:670
  58.2 2.2 %backward.1 = (f32[256,2048]{1,0:T(8,128)S(1)}, f32[1,256]{1,0:T(1,128)S(1)}, f32[32,128]{1,0:T(8,128)S(1)}, bf16[256,2048]{1,0:T(8,128)(2,1)S(1)}, bf16[256,2048]{1,0:T(8,128)(2,1)S(1)}) custom-call(s32[4]{0:T(128)S(1)} %get-tuple-element.43.cuts.refs_1_, f32[576,128]{1,0:T(8,128)S(1)} %bitcast.17, f32[1,256]{1,0:T(1,128)S(1)} %get-tuple-element.48.inner_local, ...), custom_call_target="tpu_custom_call" | custom-call | flops 805 | bytes 1 | tf_op jit(solution)/shard_map/backward/pallas_call | solution.py:795
  60.4 4.6 %collective-permute-start.6 = (f32[32,128]{1,0:T(8,128)S(1)}, f32[32,128]{1,0:T(8,128)S(1)}, u32[]{:S(2)}, u32[]{:S(2)}) collective-permute-start(f32[32,128]{1,0:T(8,128)S(1)} %get-tuple-element.52.refs_9_), channel_id=1, source_target_pairs={{0,128},{128,0},{1,129},{129,1},{2,130},{130,2},{3,131},{131,3},{4... | collective-permute-start | bytes 49160 | tf_op jit(solution)/shard_map/ppermute | solution.py:811
  65.0 0.8 %collective-permute-start.5 = (f32[1,256]{1,0:T(1,128)S(1)}, f32[1,256]{1,0:T(1,128)S(1)}, u32[]{:S(2)}, u32[]{:S(2)}) collective-permute-start(f32[1,256]{1,0:T(1,128)S(1)} %get-tuple-element.51.refs_5_), channel_id=1, source_target_pairs={{0,3},{1,0},{2,1},{3,2},{4,7},{5,4},{6,5},{7,6},{8,11},{9,8},{10,9... | collective-permute-start | bytes 3080 | tf_op jit(solution)/shard_map/ppermute | solution.py:642
  65.8 1.4 %collective-permute-start.4 = (f32[1,256]{1,0:T(1,128)S(1)}, f32[1,256]{1,0:T(1,128)S(1)}, u32[]{:S(2)}, u32[]{:S(2)}) collective-permute-start(f32[1,256]{1,0:T(1,128)S(1)} %get-tuple-element.51.refs_5_), channel_id=1, source_target_pairs={{0,2},{1,3},{2,0},{3,1},{4,6},{5,7},{6,4},{7,5},{8,10},{9,11},{10,... | collective-permute-start | bytes 3080 | tf_op jit(solution)/shard_map/ppermute | solution.py:642
  67.2 0.1 collective-permute-start.3
  67.3 2.2 %forward.1 = (bf16[256,2048]{1,0:T(8,128)(2,1)S(1)}, bf16[256,2048]{1,0:T(8,128)(2,1)S(1)}) custom-call(s32[4]{0:T(128)S(1)} %get-tuple-element.43.cuts.refs_1_, f32[576,128]{1,0:T(8,128)S(1)} %bitcast.18, f32[256,2048]{1,0:T(8,128)S(1)} %get-tuple-element.53.local, bf16[256,2048]{1,0:T(8,128)(2,1)S(1)} %get-tuple-element.54.gate, ...), custom_call_target="tpu_custom_call" | custom-call | flops 805 | bytes 1 | tf_op jit(solution)/shard_map/forward/pallas_call | solution.py:813
  69.5 0.3 collective-permute-done.4.refs_7_
  69.7 1.1 %collective-permute-done.3.refs_6_ = f32[1,256]{1,0:T(1,128)S(1)} collective-permute-done((f32[1,256]{1,0:T(1,128)S(1)}, f32[1,256]{1,0:T(1,128)S(1)}, u32[]{:S(2)}, u32[]{:S(2)}) %collective-permute-start.3) | collective-permute-done | bytes 1056 | tf_op jit(solution)/shard_map/ppermute | solution.py:642
  70.8 2.4 %features.1 = (bf16[256,2048]{1,0:T(8,128)(2,1)}, f32[16,128]{1,0:T(8,128)}, f32[16,128]{1,0:T(8,128)}, bf16[256,2048]{1,0:T(8,128)(2,1)}, bf16[256,2048]{1,0:T(8,128)(2,1)}) custom-call(f32[256,2048]{1,0:T(8,128)S(1)} %copy-done, f32[256,2048]{1,0:T(8,128)S(1)} %get-tuple-element.50.refs_1_, bf16[256,2048]{1,0:T(8,128)(2,1)S(1)} %get-tuple-element.49.feats.refs_2_, ...), custom_call_target="tpu_custom_call" | custom-call | flops 2 | bytes 1 | tf_op jit(solution)/shard_map/features/pallas_call | solution.py:823
  (13 shorter events, 0.0 us)
Async XLA Ops:
  0.6 10.8 %copy-start.1 = (f32[2048]{0:T(1024)S(1)}, f32[2048]{0:T(1024)}, u32[]{:S(2)}) copy-start(f32[2048]{0:T(1024)} %param.10) | copy-start | bytes 24580
  0.6 10.8 %copy-start.4 = (s32[1,256]{1,0:T(1,128)S(1)}, s32[1,256]{1,0:T(1,128)}, u32[]{:S(2)}) copy-start(s32[1,256]{1,0:T(1,128)} %refs_0_.5) | copy-start | bytes 3076
  3.8 6.7 %collective-permute-start.2 = (f32[1,256]{1,0:T(1,128)S(1)}, f32[1,256]{1,0:T(1,128)S(1)}, u32[]{:S(2)}, u32[]{:S(2)}) collective-permute-start(f32[1,256]{1,0:T(1,128)S(1)} %get-tuple-element.37.refs_4_), channel_id=1, source_target_pairs={{0,3},{1,0},{2,1},{3,2},{4,7},{5,4},{6,5},{7,6},{8,11},{9,8},{10,9... | collective-permute-start | bytes 3080 | tf_op jit(solution)/shard_map/ppermute | solution.py:642
  7.5 3.9 %collective-permute-start.1 = (f32[1,256]{1,0:T(1,128)S(1)}, f32[1,256]{1,0:T(1,128)S(1)}, u32[]{:S(2)}, u32[]{:S(2)}) collective-permute-start(f32[1,256]{1,0:T(1,128)S(1)} %get-tuple-element.37.refs_4_), channel_id=1, source_target_pairs={{0,2},{1,3},{2,0},{3,1},{4,6},{5,7},{6,4},{7,5},{8,10},{9,11},{10,... | collective-permute-start | bytes 3080 | tf_op jit(solution)/shard_map/ppermute | solution.py:642
  7.8 3.6 %collective-permute-start = (f32[1,256]{1,0:T(1,128)S(1)}, f32[1,256]{1,0:T(1,128)S(1)}, u32[]{:S(2)}, u32[]{:S(2)}) collective-permute-start(f32[1,256]{1,0:T(1,128)S(1)} %get-tuple-element.37.refs_4_), channel_id=1, source_target_pairs={{0,1},{1,2},{2,3},{3,0},{4,5},{5,6},{6,7},{7,4},{8,9},{9,10},{10,1... | collective-permute-start | bytes 3080 | tf_op jit(solution)/shard_map/ppermute | solution.py:642
  11.5 28.8 %copy-start.2 = (f32[128,16]{0,1:T(8,128)S(1)}, f32[128,16]{0,1:T(8,128)}, u32[]{:S(2)}) copy-start(f32[128,16]{0,1:T(8,128)} %param.12) | copy-start | bytes 24580
  11.5 28.8 %copy-start.3 = (f32[128,16]{0,1:T(8,128)S(1)}, f32[128,16]{0,1:T(8,128)}, u32[]{:S(2)}) copy-start(f32[128,16]{0,1:T(8,128)} %param.11) | copy-start | bytes 24580
  18.5 21.8 %all-to-all-start = ((f32[32,1,2304]{2,1,0:T(1,128)}), f32[32,1,2304]{2,1,0:T(1,128)S(1)}, u32[]{:S(2)}, u32[]{:S(2)}) async-start(f32[32,1,2304]{2,1,0:T(1,128)} %bitcast.38), calls=%async_computation | async-start | bytes 589824 | tf_op jit(solution)/shard_map/all_to_all | solution.py:670
  41.6 16.6 %all-to-all-start.1 = ((f32[32,1,2304]{2,1,0:T(1,128)}), f32[32,1,2304]{2,1,0:T(1,128)S(1)}, u32[]{:S(2)}, u32[]{:S(2)}) async-start(f32[32,1,2304]{2,1,0:T(1,128)} %bitcast.37), calls=%async_computation.1 | async-start | bytes 589824 | tf_op jit(solution)/shard_map/all_to_all | solution.py:670
  60.4 10.4 %collective-permute-start.6 = (f32[32,128]{1,0:T(8,128)S(1)}, f32[32,128]{1,0:T(8,128)S(1)}, u32[]{:S(2)}, u32[]{:S(2)}) collective-permute-start(f32[32,128]{1,0:T(8,128)S(1)} %get-tuple-element.52.refs_9_), channel_id=1, source_target_pairs={{0,128},{128,0},{1,129},{129,1},{2,130},{130,2},{3,131},{131,3},{4... | collective-permute-start | bytes 49160 | tf_op jit(solution)/shard_map/ppermute | solution.py:811
  65.0 4.4 %collective-permute-start.5 = (f32[1,256]{1,0:T(1,128)S(1)}, f32[1,256]{1,0:T(1,128)S(1)}, u32[]{:S(2)}, u32[]{:S(2)}) collective-permute-start(f32[1,256]{1,0:T(1,128)S(1)} %get-tuple-element.51.refs_5_), channel_id=1, source_target_pairs={{0,3},{1,0},{2,1},{3,2},{4,7},{5,4},{6,5},{7,6},{8,11},{9,8},{10,9... | collective-permute-start | bytes 3080 | tf_op jit(solution)/shard_map/ppermute | solution.py:642
  65.8 3.9 %collective-permute-start.4 = (f32[1,256]{1,0:T(1,128)S(1)}, f32[1,256]{1,0:T(1,128)S(1)}, u32[]{:S(2)}, u32[]{:S(2)}) collective-permute-start(f32[1,256]{1,0:T(1,128)S(1)} %get-tuple-element.51.refs_5_), channel_id=1, source_target_pairs={{0,2},{1,3},{2,0},{3,1},{4,6},{5,7},{6,4},{7,5},{8,10},{9,11},{10,... | collective-permute-start | bytes 3080 | tf_op jit(solution)/shard_map/ppermute | solution.py:642
  67.2 3.6 %collective-permute-start.3 = (f32[1,256]{1,0:T(1,128)S(1)}, f32[1,256]{1,0:T(1,128)S(1)}, u32[]{:S(2)}, u32[]{:S(2)}) collective-permute-start(f32[1,256]{1,0:T(1,128)S(1)} %get-tuple-element.51.refs_5_), channel_id=1, source_target_pairs={{0,1},{1,2},{2,3},{3,0},{4,5},{5,6},{6,7},{7,4},{8,9},{9,10},{10,1... | collective-permute-start | bytes 3080 | tf_op jit(solution)/shard_map/ppermute | solution.py:642
  67.3 3.6 %copy-start = (f32[256,2048]{1,0:T(8,128)S(1)}, f32[256,2048]{1,0:T(8,128)}, u32[]{:S(2)}) copy-start(f32[256,2048]{1,0:T(8,128)} %get-tuple-element.46.refs_0_) | copy-start | bytes 6291460

commit v5 on v4

--- a/solution.py
+++ b/solution.py
@@ -13,7 +13,7 @@
 HALVES = 2
 MODES = 16
 GROUP = 16
-UNROLL = 16
+UNROLL = 32
 COUNT = 4
 COPIES = 2
 BLOCKS = 8
@@ -167,13 +167,16 @@
 
 
 def lane_sums(value):
-    return lax.dot_general(
-        jnp.ones((8, LANES), f32),
-        value,
-        (((1,), (1,)), ((), ())),
-        precision=HIGHEST,
-        preferred_element_type=f32,
-    )[0:1]
+    high = value.astype(jnp.bfloat16)
+    rest = value - high.astype(f32)
+    middle = rest.astype(jnp.bfloat16)
+    low = (rest - middle.astype(f32)).astype(jnp.bfloat16)
+    ones = jnp.ones((16, LANES), jnp.bfloat16)
+    sums = [
+        lax.dot_general(ones, part, (((1,), (1,)), ((), ())), preferred_element_type=f32)
+        for part in (high, middle, low)
+    ]
+    return (sums[0] + (sums[1] + sums[2]))[0:1]
 
 
 def load_kernel(
@@ -188,8 +191,8 @@
     ]
     for copy in small:
         copy.start()
-    feat_copies = row_copies(feats_in, feats, sems.at[0])
-    copies = row_copies(gate_in, gate, sems.at[1]) + row_copies(grad_in, grad, sems.at[2])
+    feat_copies = row_copies(feats_in, feats, sems.at[0], 1)
+    copies = row_copies(gate_in, gate, sems.at[1], 1) + row_copies(grad_in, grad, sems.at[2], 1)
     for copy in small:
         copy.wait()
     expand(rates, residue, seg, table, cuts)
@@ -277,7 +280,7 @@
     msg_out, inverse, grad_out, msg, feat_scan, ends, sums, sems, grad_sems,
 ):
     length = feats.shape[0]
-    grad_copies = row_copies(grad_scan, grad_out, grad_sems)
+    grad_copies = row_copies(grad_scan, grad_out, grad_sems, 1)
     inverse[...] = inverse_of((part0, part1, part2, part3), full_width)
     scale = column(inverse[...])
     share = msg.shape[0] // HALVES
@@ -596,8 +599,8 @@
     out, modes, gains, mixed, grad_gate, out_v, sems, gate_sems,
 ):
     length, width = feats.shape
-    gate_copies = row_copies(mixed_v, mixed, gate_sems.at[0])
-    gate_copies += row_copies(grad_gate_v, grad_gate, gate_sems.at[1])
+    gate_copies = row_copies(mixed_v, mixed, gate_sems.at[0], 1)
+    gate_copies += row_copies(grad_gate_v, grad_gate, gate_sems.at[1], 1)
     scale = column(inverse[...])
     factor = column(total_row((i0, i1, i2, i3))) * scale * scale / full_width
     copies = []

time: 73.7 us -> 74 us (level)
  no operation moved by 1% of the time
where the time goes in v5:
time: 74 us; the launch traced here: 73.6 us
  Pallas kernels  35.9 us (49%)
  starting transfers between devices  28.4 us (38%)
  waiting for transfers between devices  8.33 us (11%)
  between operations  0.92 us (1%)
    all_to_all x2, starting transfers between devices, exchange(): return lax.all_to_all(value, 'ctx', 0, 0, tiled=True).reshape(message.shape)  16.9 us
    pallas_call x2, Pallas kernels, local(): call(lambda *refs: local_kernel(backward, *refs), 'local_backward' if bac...  15.3 us
    ppermute x6, starting transfers between devices, all_parts(): lax.ppermute(value, 'tensor', [(i, (i + d) % size) for i in range(size)])  6.95 us
    pallas_call x1, Pallas kernels, shards(): call(lambda *refs: state_kernel(full_width, *refs), 'states', [smem, smem...  6.9 us
    all_to_all x2, waiting for transfers between devices, exchange(): return lax.all_to_all(value, 'ctx', 0, 0, tiled=True).reshape(message.shape)  6.04 us
    ppermute x1, starting transfers between devices, shards(): lax.ppermute(totals, 'dp', [(i, (i + 1) % size) for i in range(size)])  4.59 us
    pallas_call x1, Pallas kernels, shards(): call(load_kernel, 'load', [hbm] * 6, [vmem] * 5 + [smem], [here(wide, jnp...  3.07 us
    pallas_call x1, Pallas kernels, shards(): call(backward_kernel, 'backward', [smem] + [vmem] * 4 + [hbm] * 2, [vmem]...  2.8 us
  transfers between devices with their start and end apart: 9, of which 6 were waited for; matrix products, arithmetic and copies ran while one was open for 0% of the time, Pallas kernels for 27%

profile of v5, /device:TPU:1, one launch (start us, length us, event | category | flops | bytes accessed | tf_op | source)
XLA Modules:
  0.0 73.6 jit_solution(1577235449462746082)
XLA Ops:
  0.7 3.1 %load.1 = (bf16[256,2048]{1,0:T(8,128)(2,1)S(1)}, f32[4096,128]{1,0:T(8,128)S(1)}, f32[1,256]{1,0:T(1,128)S(1)}, f32[32,16,128]{2,1,0:T(8,128)S(1)}, f32[16,128]{1,0:T(8,128)S(1)}, /*index=5*/s32[4]{0:T(128)S(1)}) custom-call(bf16[256,2048]{1,0:T(8,128)(2,1)} %bitcast.30, bf16[256,2048]{1,0:T(8,128)(2,1)} %bitcast.33, bf16[256,2048]{1,0:T(8,128)(2,1)} %bitcast.35, ...), custom_call_target="tpu_custom_call" | custom-call | flops 1 | bytes 1 | tf_op jit(solution)/shard_map/load/pallas_call | solution.py:696
  3.7 3.6 %collective-permute-start.2 = (f32[1,256]{1,0:T(1,128)S(1)}, f32[1,256]{1,0:T(1,128)S(1)}, u32[]{:S(2)}, u32[]{:S(2)}) collective-permute-start(f32[1,256]{1,0:T(1,128)S(1)} %get-tuple-element.37.refs_4_), channel_id=1, source_target_pairs={{0,3},{1,0},{2,1},{3,2},{4,7},{5,4},{6,5},{7,6},{8,11},{9,8},{10,9... | collective-permute-start | bytes 3080 | tf_op jit(solution)/shard_map/ppermute | solution.py:645
  7.4 0.4 collective-permute-start.1
  7.7 0.7 collective-permute-start
  8.4 2.0 %adjoint.1.refs_10_ = f32[256,128]{1,0:T(8,128)S(1)} custom-call(s32[4]{0:T(128)S(1)} %get-tuple-element.43.cuts.refs_1_, f32[4096,128]{1,0:T(8,128)S(1)} %get-tuple-element.36.grad_scan.refs_3_, f32[16,128]{1,0:T(8,128)S(1)} %get-tuple-element.39.rates), custom_call_target="tpu_custom_call" | custom-call | flops 16 | bytes 1 | tf_op jit(solution)/shard_map/adjoint/pallas_call | solution.py:722
  10.4 0.8 %collective-permute-done.1.refs_6_ = f32[1,256]{1,0:T(1,128)S(1)} collective-permute-done((f32[1,256]{1,0:T(1,128)S(1)}, f32[1,256]{1,0:T(1,128)S(1)}, u32[]{:S(2)}, u32[]{:S(2)}) %collective-permute-start.1) | collective-permute-done | bytes 1056 | tf_op jit(solution)/shard_map/ppermute | solution.py:645
  11.3 0.1 collective-permute-done.refs_5_
  11.4 6.9 %states.1 = (f32[576,128]{1,0:T(8,128)}, f32[1,256]{1,0:T(1,128)S(1)}, f32[4096,128]{1,0:T(8,128)}) custom-call(s32[1,256]{1,0:T(1,128)S(1)} %copy-done.4, s32[4]{0:T(128)S(1)} %get-tuple-element.43.cuts.refs_1_, bf16[256,2048]{1,0:T(8,128)(2,1)S(1)} %get-tuple-element.35.refs_2_, f32[4096,128]{1,0:T(8,128)S(1)} %get-tuple-element.36.grad_scan.refs_3_, ...), custom_call_target="tpu_custom_call" | custom-call | flops 33 | bytes 1 | tf_op jit(solution)/shard_map/states/pallas_call | solution.py:734
  18.3 11.0 %all-to-all-start = ((f32[32,1,2304]{2,1,0:T(1,128)}), f32[32,1,2304]{2,1,0:T(1,128)S(1)}, u32[]{:S(2)}, u32[]{:S(2)}) async-start(f32[32,1,2304]{2,1,0:T(1,128)} %bitcast.38), calls=%async_computation | async-start | bytes 589824 | tf_op jit(solution)/shard_map/all_to_all | solution.py:673
  29.3 7.3 %local_forward.1 = (f32[256,2048]{1,0:T(8,128)S(1)}, f32[32,16,128]{2,1,0:T(8,128)}) custom-call(s32[1,256]{1,0:T(1,128)S(1)} %copy-done.4, s32[4]{0:T(128)S(1)} %get-tuple-element.43.cuts.refs_1_, f32[32,16,128]{2,1,0:T(8,128)S(1)} %get-tuple-element.38.refs_8_.refs_2_, bf16[256,2048]{1,0:T(8,128)(2,1)} %bitcast.31, f32[1,256]{1,0:T(1,128)S(1)} %get-tuple-element.41.refs_4_), custom_call_target="tpu_custom_call" | custom-call | flops 33 | bytes 1 | tf_op jit(solution)/shard_map/local_forward/pallas_call | solution.py:752
  36.7 3.4 %all-to-all-done = f32[32,1,2304]{2,1,0:T(1,128)S(1)} async-done(((f32[32,1,2304]{2,1,0:T(1,128)}), f32[32,1,2304]{2,1,0:T(1,128)S(1)}, u32[]{:S(2)}, u32[]{:S(2)}) %all-to-all-start) | async-done | bytes 294944 | tf_op jit(solution)/shard_map/all_to_all | solution.py:673
  40.1 1.2 %carries.1 = f32[576,128]{1,0:T(8,128)} custom-call(s32[1]{0:T(128)} %bitcast.9.refs_0_, f32[576,128]{1,0:T(8,128)S(1)} %bitcast.19, f32[16,128]{1,0:T(8,128)S(1)} %bitcast.27, f32[16,128]{1,0:T(8,128)S(1)} %bitcast.29, f32[1,2048]{1,0:T(1,128)S(1)} %bitcast.21), custom_call_target="tpu_custom_call" | custom-call | flops 2 | bytes 1 | tf_op jit(solution)/shard_map/carries/pallas_call | solution.py:782
  41.3 5.8 %all-to-all-start.1 = ((f32[32,1,2304]{2,1,0:T(1,128)}), f32[32,1,2304]{2,1,0:T(1,128)S(1)}, u32[]{:S(2)}, u32[]{:S(2)}) async-start(f32[32,1,2304]{2,1,0:T(1,128)} %bitcast.37), calls=%async_computation.1 | async-start | bytes 589824 | tf_op jit(solution)/shard_map/all_to_all | solution.py:673
  47.2 8.0 %local_backward.1 = (f32[256,2048]{1,0:T(8,128)}, f32[1,256]{1,0:T(1,128)S(1)}, bf16[256,2048]{1,0:T(8,128)(2,1)S(1)}) custom-call(s32[1,256]{1,0:T(1,128)S(1)} %copy-done.4, s32[4]{0:T(128)S(1)} %get-tuple-element.43.cuts.refs_1_, f32[32,16,128]{2,1,0:T(8,128)} %get-tuple-element.44.refs_2_, f32[4096,128]{1,0:T(8,128)} %get-tuple-element.45.refs_3_, ...), custom_call_target="tpu_custom_call" | custom-call | flops 33 | bytes 1 | tf_op jit(solution)/shard_map/local_backward/pallas_call | solution.py:752
  55.2 2.6 %all-to-all-done.1 = f32[32,1,2304]{2,1,0:T(1,128)S(1)} async-done(((f32[32,1,2304]{2,1,0:T(1,128)}), f32[32,1,2304]{2,1,0:T(1,128)S(1)}, u32[]{:S(2)}, u32[]{:S(2)}) %all-to-all-start.1) | async-done | bytes 294944 | tf_op jit(solution)/shard_map/all_to_all | solution.py:673
  57.9 2.8 %backward.1 = (f32[256,2048]{1,0:T(8,128)S(1)}, f32[1,256]{1,0:T(1,128)S(1)}, f32[32,128]{1,0:T(8,128)S(1)}, bf16[256,2048]{1,0:T(8,128)(2,1)S(1)}, bf16[256,2048]{1,0:T(8,128)(2,1)S(1)}) custom-call(s32[4]{0:T(128)S(1)} %get-tuple-element.43.cuts.refs_1_, f32[576,128]{1,0:T(8,128)S(1)} %bitcast.17, f32[1,256]{1,0:T(1,128)S(1)} %get-tuple-element.48.inner_local, ...), custom_call_target="tpu_custom_call" | custom-call | flops 805 | bytes 1 | tf_op jit(solution)/shard_map/backward/pallas_call | solution.py:798
  60.7 4.6 %collective-permute-start.6 = (f32[32,128]{1,0:T(8,128)S(1)}, f32[32,128]{1,0:T(8,128)S(1)}, u32[]{:S(2)}, u32[]{:S(2)}) collective-permute-start(f32[32,128]{1,0:T(8,128)S(1)} %get-tuple-element.52.refs_9_), channel_id=1, source_target_pairs={{0,128},{128,0},{1,129},{129,1},{2,130},{130,2},{3,131},{131,3},{4... | collective-permute-start | bytes 49160 | tf_op jit(solution)/shard_map/ppermute | solution.py:814
  65.3 0.8 %collective-permute-start.5 = (f32[1,256]{1,0:T(1,128)S(1)}, f32[1,256]{1,0:T(1,128)S(1)}, u32[]{:S(2)}, u32[]{:S(2)}) collective-permute-start(f32[1,256]{1,0:T(1,128)S(1)} %get-tuple-element.51.refs_5_), channel_id=1, source_target_pairs={{0,3},{1,0},{2,1},{3,2},{4,7},{5,4},{6,5},{7,6},{8,11},{9,8},{10,9... | collective-permute-start | bytes 3080 | tf_op jit(solution)/shard_map/ppermute | solution.py:645
  66.0 1.4 %collective-permute-start.4 = (f32[1,256]{1,0:T(1,128)S(1)}, f32[1,256]{1,0:T(1,128)S(1)}, u32[]{:S(2)}, u32[]{:S(2)}) collective-permute-start(f32[1,256]{1,0:T(1,128)S(1)} %get-tuple-element.51.refs_5_), channel_id=1, source_target_pairs={{0,2},{1,3},{2,0},{3,1},{4,6},{5,7},{6,4},{7,5},{8,10},{9,11},{10,... | collective-permute-start | bytes 3080 | tf_op jit(solution)/shard_map/ppermute | solution.py:645
  67.5 0.1 collective-permute-start.3
  67.5 2.1 %forward.1 = (bf16[256,2048]{1,0:T(8,128)(2,1)S(1)}, bf16[256,2048]{1,0:T(8,128)(2,1)S(1)}) custom-call(s32[4]{0:T(128)S(1)} %get-tuple-element.43.cuts.refs_1_, f32[576,128]{1,0:T(8,128)S(1)} %bitcast.18, f32[256,2048]{1,0:T(8,128)S(1)} %get-tuple-element.53.local, bf16[256,2048]{1,0:T(8,128)(2,1)S(1)} %get-tuple-element.54.gate, ...), custom_call_target="tpu_custom_call" | custom-call | flops 805 | bytes 1 | tf_op jit(solution)/shard_map/forward/pallas_call | solution.py:816
  69.7 0.3 collective-permute-done.4.refs_7_
  70.0 1.1 %collective-permute-done.3.refs_6_ = f32[1,256]{1,0:T(1,128)S(1)} collective-permute-done((f32[1,256]{1,0:T(1,128)S(1)}, f32[1,256]{1,0:T(1,128)S(1)}, u32[]{:S(2)}, u32[]{:S(2)}) %collective-permute-start.3) | collective-permute-done | bytes 1056 | tf_op jit(solution)/shard_map/ppermute | solution.py:645
  71.1 2.4 %features.1 = (bf16[256,2048]{1,0:T(8,128)(2,1)}, f32[16,128]{1,0:T(8,128)}, f32[16,128]{1,0:T(8,128)}, bf16[256,2048]{1,0:T(8,128)(2,1)}, bf16[256,2048]{1,0:T(8,128)(2,1)}) custom-call(f32[256,2048]{1,0:T(8,128)S(1)} %copy-done, f32[256,2048]{1,0:T(8,128)S(1)} %get-tuple-element.50.refs_1_, bf16[256,2048]{1,0:T(8,128)(2,1)S(1)} %get-tuple-element.49.feats.refs_2_, ...), custom_call_target="tpu_custom_call" | custom-call | flops 2 | bytes 1 | tf_op jit(solution)/shard_map/features/pallas_call | solution.py:826
  (13 shorter events, 0.0 us)
Async XLA Ops:
  0.6 10.7 %copy-start.1 = (f32[2048]{0:T(1024)S(1)}, f32[2048]{0:T(1024)}, u32[]{:S(2)}) copy-start(f32[2048]{0:T(1024)} %param.10) | copy-start | bytes 24580
  0.6 10.7 %copy-start.4 = (s32[1,256]{1,0:T(1,128)S(1)}, s32[1,256]{1,0:T(1,128)}, u32[]{:S(2)}) copy-start(s32[1,256]{1,0:T(1,128)} %refs_0_.5) | copy-start | bytes 3076
  3.7 6.7 %collective-permute-start.2 = (f32[1,256]{1,0:T(1,128)S(1)}, f32[1,256]{1,0:T(1,128)S(1)}, u32[]{:S(2)}, u32[]{:S(2)}) collective-permute-start(f32[1,256]{1,0:T(1,128)S(1)} %get-tuple-element.37.refs_4_), channel_id=1, source_target_pairs={{0,3},{1,0},{2,1},{3,2},{4,7},{5,4},{6,5},{7,6},{8,11},{9,8},{10,9... | collective-permute-start | bytes 3080 | tf_op jit(solution)/shard_map/ppermute | solution.py:645
  7.4 3.9 %collective-permute-start.1 = (f32[1,256]{1,0:T(1,128)S(1)}, f32[1,256]{1,0:T(1,128)S(1)}, u32[]{:S(2)}, u32[]{:S(2)}) collective-permute-start(f32[1,256]{1,0:T(1,128)S(1)} %get-tuple-element.37.refs_4_), channel_id=1, source_target_pairs={{0,2},{1,3},{2,0},{3,1},{4,6},{5,7},{6,4},{7,5},{8,10},{9,11},{10,... | collective-permute-start | bytes 3080 | tf_op jit(solution)/shard_map/ppermute | solution.py:645
  7.7 3.6 %collective-permute-start = (f32[1,256]{1,0:T(1,128)S(1)}, f32[1,256]{1,0:T(1,128)S(1)}, u32[]{:S(2)}, u32[]{:S(2)}) collective-permute-start(f32[1,256]{1,0:T(1,128)S(1)} %get-tuple-element.37.refs_4_), channel_id=1, source_target_pairs={{0,1},{1,2},{2,3},{3,0},{4,5},{5,6},{6,7},{7,4},{8,9},{9,10},{10,1... | collective-permute-start | bytes 3080 | tf_op jit(solution)/shard_map/ppermute | solution.py:645
  11.4 28.7 %copy-start.2 = (f32[128,16]{0,1:T(8,128)S(1)}, f32[128,16]{0,1:T(8,128)}, u32[]{:S(2)}) copy-start(f32[128,16]{0,1:T(8,128)} %param.12) | copy-start | bytes 24580
  11.4 28.7 %copy-start.3 = (f32[128,16]{0,1:T(8,128)S(1)}, f32[128,16]{0,1:T(8,128)}, u32[]{:S(2)}) copy-start(f32[128,16]{0,1:T(8,128)} %param.11) | copy-start | bytes 24580
  18.3 21.8 %all-to-all-start = ((f32[32,1,2304]{2,1,0:T(1,128)}), f32[32,1,2304]{2,1,0:T(1,128)S(1)}, u32[]{:S(2)}, u32[]{:S(2)}) async-start(f32[32,1,2304]{2,1,0:T(1,128)} %bitcast.38), calls=%async_computation | async-start | bytes 589824 | tf_op jit(solution)/shard_map/all_to_all | solution.py:673
  41.3 16.5 %all-to-all-start.1 = ((f32[32,1,2304]{2,1,0:T(1,128)}), f32[32,1,2304]{2,1,0:T(1,128)S(1)}, u32[]{:S(2)}, u32[]{:S(2)}) async-start(f32[32,1,2304]{2,1,0:T(1,128)} %bitcast.37), calls=%async_computation.1 | async-start | bytes 589824 | tf_op jit(solution)/shard_map/all_to_all | solution.py:673
  60.7 10.4 %collective-permute-start.6 = (f32[32,128]{1,0:T(8,128)S(1)}, f32[32,128]{1,0:T(8,128)S(1)}, u32[]{:S(2)}, u32[]{:S(2)}) collective-permute-start(f32[32,128]{1,0:T(8,128)S(1)} %get-tuple-element.52.refs_9_), channel_id=1, source_target_pairs={{0,128},{128,0},{1,129},{129,1},{2,130},{130,2},{3,131},{131,3},{4... | collective-permute-start | bytes 49160 | tf_op jit(solution)/shard_map/ppermute | solution.py:814
  65.3 4.4 %collective-permute-start.5 = (f32[1,256]{1,0:T(1,128)S(1)}, f32[1,256]{1,0:T(1,128)S(1)}, u32[]{:S(2)}, u32[]{:S(2)}) collective-permute-start(f32[1,256]{1,0:T(1,128)S(1)} %get-tuple-element.51.refs_5_), channel_id=1, source_target_pairs={{0,3},{1,0},{2,1},{3,2},{4,7},{5,4},{6,5},{7,6},{8,11},{9,8},{10,9... | collective-permute-start | bytes 3080 | tf_op jit(solution)/shard_map/ppermute | solution.py:645
  66.0 3.9 %collective-permute-start.4 = (f32[1,256]{1,0:T(1,128)S(1)}, f32[1,256]{1,0:T(1,128)S(1)}, u32[]{:S(2)}, u32[]{:S(2)}) collective-permute-start(f32[1,256]{1,0:T(1,128)S(1)} %get-tuple-element.51.refs_5_), channel_id=1, source_target_pairs={{0,2},{1,3},{2,0},{3,1},{4,6},{5,7},{6,4},{7,5},{8,10},{9,11},{10,... | collective-permute-start | bytes 3080 | tf_op jit(solution)/shard_map/ppermute | solution.py:645
  67.5 3.6 %collective-permute-start.3 = (f32[1,256]{1,0:T(1,128)S(1)}, f32[1,256]{1,0:T(1,128)S(1)}, u32[]{:S(2)}, u32[]{:S(2)}) collective-permute-start(f32[1,256]{1,0:T(1,128)S(1)} %get-tuple-element.51.refs_5_), channel_id=1, source_target_pairs={{0,1},{1,2},{2,3},{3,0},{4,5},{5,6},{6,7},{7,4},{8,9},{9,10},{10,1... | collective-permute-start | bytes 3080 | tf_op jit(solution)/shard_map/ppermute | solution.py:645
  67.5 3.6 %copy-start = (f32[256,2048]{1,0:T(8,128)S(1)}, f32[256,2048]{1,0:T(8,128)}, u32[]{:S(2)}) copy-start(f32[256,2048]{1,0:T(8,128)} %get-tuple-element.46.refs_0_) | copy-start | bytes 6291460

commit v6 on v5

--- a/solution.py
+++ b/solution.py
@@ -13,7 +13,7 @@
 HALVES = 2
 MODES = 16
 GROUP = 16
-UNROLL = 32
+UNROLL = 16
 COUNT = 4
 COPIES = 2
 BLOCKS = 8
@@ -191,8 +191,8 @@
     ]
     for copy in small:
         copy.start()
-    feat_copies = row_copies(feats_in, feats, sems.at[0], 1)
-    copies = row_copies(gate_in, gate, sems.at[1], 1) + row_copies(grad_in, grad, sems.at[2], 1)
+    feat_copies = row_copies(feats_in, feats, sems.at[0])
+    copies = row_copies(gate_in, gate, sems.at[1]) + row_copies(grad_in, grad, sems.at[2])
     for copy in small:
         copy.wait()
     expand(rates, residue, seg, table, cuts)
@@ -280,7 +280,7 @@
     msg_out, inverse, grad_out, msg, feat_scan, ends, sums, sems, grad_sems,
 ):
     length = feats.shape[0]
-    grad_copies = row_copies(grad_scan, grad_out, grad_sems, 1)
+    grad_copies = row_copies(grad_scan, grad_out, grad_sems)
     inverse[...] = inverse_of((part0, part1, part2, part3), full_width)
     scale = column(inverse[...])
     share = msg.shape[0] // HALVES
@@ -599,8 +599,8 @@
     out, modes, gains, mixed, grad_gate, out_v, sems, gate_sems,
 ):
     length, width = feats.shape
-    gate_copies = row_copies(mixed_v, mixed, gate_sems.at[0], 1)
-    gate_copies += row_copies(grad_gate_v, grad_gate, gate_sems.at[1], 1)
+    gate_copies = row_copies(mixed_v, mixed, gate_sems.at[0])
+    gate_copies += row_copies(grad_gate_v, grad_gate, gate_sems.at[1])
     scale = column(inverse[...])
     factor = column(total_row((i0, i1, i2, i3))) * scale * scale / full_width
     copies = []

time: 74 us -> 74.1 us (level)
  no operation moved by 1% of the time
where the time goes in v6:
time: 74.1 us; the launch traced here: 73.8 us
  Pallas kernels  36.2 us (49%)
  starting transfers between devices  28.5 us (38%)
  waiting for transfers between devices  8.21 us (11%)
  between operations  0.92 us (1%)
    all_to_all x2, starting transfers between devices, exchange(): return lax.all_to_all(value, 'ctx', 0, 0, tiled=True).reshape(message.shape)  17 us
    pallas_call x2, Pallas kernels, local(): call(lambda *refs: local_kernel(backward, *refs), 'local_backward' if bac...  15.5 us
    pallas_call x1, Pallas kernels, shards(): call(lambda *refs: state_kernel(full_width, *refs), 'states', [smem, smem...  7.03 us
    ppermute x6, starting transfers between devices, all_parts(): lax.ppermute(value, 'tensor', [(i, (i + d) % size) for i in range(size)])  6.95 us
    all_to_all x2, waiting for transfers between devices, exchange(): return lax.all_to_all(value, 'ctx', 0, 0, tiled=True).reshape(message.shape)  5.92 us
    ppermute x1, starting transfers between devices, shards(): lax.ppermute(totals, 'dp', [(i, (i + 1) % size) for i in range(size)])  4.58 us
    pallas_call x1, Pallas kernels, shards(): call(load_kernel, 'load', [hbm] * 6, [vmem] * 5 + [smem], [here(wide, jnp...  3.04 us
    pallas_call x1, Pallas kernels, shards(): call(backward_kernel, 'backward', [smem] + [vmem] * 4 + [hbm] * 2, [vmem]...  2.81 us
  transfers between devices with their start and end apart: 9, of which 6 were waited for; matrix products, arithmetic and copies ran while one was open for 0% of the time, Pallas kernels for 27%

profile of v6, /device:TPU:1, one launch (start us, length us, event | category | flops | bytes accessed | tf_op | source)
XLA Modules:
  0.0 73.8 jit_solution(7399547253105150085)
XLA Ops:
  0.7 3.0 %load.1 = (bf16[256,2048]{1,0:T(8,128)(2,1)S(1)}, f32[4096,128]{1,0:T(8,128)S(1)}, f32[1,256]{1,0:T(1,128)S(1)}, f32[32,16,128]{2,1,0:T(8,128)S(1)}, f32[16,128]{1,0:T(8,128)S(1)}, /*index=5*/s32[4]{0:T(128)S(1)}) custom-call(bf16[256,2048]{1,0:T(8,128)(2,1)} %bitcast.30, bf16[256,2048]{1,0:T(8,128)(2,1)} %bitcast.33, bf16[256,2048]{1,0:T(8,128)(2,1)} %bitcast.35, ...), custom_call_target="tpu_custom_call" | custom-call | flops 1 | bytes 1 | tf_op jit(solution)/shard_map/load/pallas_call | solution.py:696
  3.7 3.6 %collective-permute-start.2 = (f32[1,256]{1,0:T(1,128)S(1)}, f32[1,256]{1,0:T(1,128)S(1)}, u32[]{:S(2)}, u32[]{:S(2)}) collective-permute-start(f32[1,256]{1,0:T(1,128)S(1)} %get-tuple-element.37.refs_4_), channel_id=1, source_target_pairs={{0,3},{1,0},{2,1},{3,2},{4,7},{5,4},{6,5},{7,6},{8,11},{9,8},{10,9... | collective-permute-start | bytes 3080 | tf_op jit(solution)/shard_map/ppermute | solution.py:645
  7.3 0.3 collective-permute-start.1
  7.7 0.7 collective-permute-start
  8.4 2.0 %adjoint.1.refs_10_ = f32[256,128]{1,0:T(8,128)S(1)} custom-call(s32[4]{0:T(128)S(1)} %get-tuple-element.43.cuts.refs_1_, f32[4096,128]{1,0:T(8,128)S(1)} %get-tuple-element.36.grad_scan.refs_3_, f32[16,128]{1,0:T(8,128)S(1)} %get-tuple-element.39.rates), custom_call_target="tpu_custom_call" | custom-call | flops 16 | bytes 1 | tf_op jit(solution)/shard_map/adjoint/pallas_call | solution.py:722
  10.4 0.8 %collective-permute-done.1.refs_6_ = f32[1,256]{1,0:T(1,128)S(1)} collective-permute-done((f32[1,256]{1,0:T(1,128)S(1)}, f32[1,256]{1,0:T(1,128)S(1)}, u32[]{:S(2)}, u32[]{:S(2)}) %collective-permute-start.1) | collective-permute-done | bytes 1056 | tf_op jit(solution)/shard_map/ppermute | solution.py:645
  11.3 0.1 collective-permute-done.refs_5_
  11.3 7.0 %states.1 = (f32[576,128]{1,0:T(8,128)}, f32[1,256]{1,0:T(1,128)S(1)}, f32[4096,128]{1,0:T(8,128)}) custom-call(s32[1,256]{1,0:T(1,128)S(1)} %copy-done.4, s32[4]{0:T(128)S(1)} %get-tuple-element.43.cuts.refs_1_, bf16[256,2048]{1,0:T(8,128)(2,1)S(1)} %get-tuple-element.35.refs_2_, f32[4096,128]{1,0:T(8,128)S(1)} %get-tuple-element.36.grad_scan.refs_3_, ...), custom_call_target="tpu_custom_call" | custom-call | flops 33 | bytes 1 | tf_op jit(solution)/shard_map/states/pallas_call | solution.py:734
  18.4 11.0 %all-to-all-start = ((f32[32,1,2304]{2,1,0:T(1,128)}), f32[32,1,2304]{2,1,0:T(1,128)S(1)}, u32[]{:S(2)}, u32[]{:S(2)}) async-start(f32[32,1,2304]{2,1,0:T(1,128)} %bitcast.38), calls=%async_computation | async-start | bytes 589824 | tf_op jit(solution)/shard_map/all_to_all | solution.py:673
  29.4 7.4 %local_forward.1 = (f32[256,2048]{1,0:T(8,128)S(1)}, f32[32,16,128]{2,1,0:T(8,128)}) custom-call(s32[1,256]{1,0:T(1,128)S(1)} %copy-done.4, s32[4]{0:T(128)S(1)} %get-tuple-element.43.cuts.refs_1_, f32[32,16,128]{2,1,0:T(8,128)S(1)} %get-tuple-element.38.refs_8_.refs_2_, bf16[256,2048]{1,0:T(8,128)(2,1)} %bitcast.31, f32[1,256]{1,0:T(1,128)S(1)} %get-tuple-element.41.refs_4_), custom_call_target="tpu_custom_call" | custom-call | flops 33 | bytes 1 | tf_op jit(solution)/shard_map/local_forward/pallas_call | solution.py:752
  36.8 3.3 %all-to-all-done = f32[32,1,2304]{2,1,0:T(1,128)S(1)} async-done(((f32[32,1,2304]{2,1,0:T(1,128)}), f32[32,1,2304]{2,1,0:T(1,128)S(1)}, u32[]{:S(2)}, u32[]{:S(2)}) %all-to-all-start) | async-done | bytes 294944 | tf_op jit(solution)/shard_map/all_to_all | solution.py:673
  40.2 1.2 %carries.1 = f32[576,128]{1,0:T(8,128)} custom-call(s32[1]{0:T(128)} %bitcast.9.refs_0_, f32[576,128]{1,0:T(8,128)S(1)} %bitcast.19, f32[16,128]{1,0:T(8,128)S(1)} %bitcast.27, f32[16,128]{1,0:T(8,128)S(1)} %bitcast.29, f32[1,2048]{1,0:T(1,128)S(1)} %bitcast.21), custom_call_target="tpu_custom_call" | custom-call | flops 2 | bytes 1 | tf_op jit(solution)/shard_map/carries/pallas_call | solution.py:782
  41.4 5.9 %all-to-all-start.1 = ((f32[32,1,2304]{2,1,0:T(1,128)}), f32[32,1,2304]{2,1,0:T(1,128)S(1)}, u32[]{:S(2)}, u32[]{:S(2)}) async-start(f32[32,1,2304]{2,1,0:T(1,128)} %bitcast.37), calls=%async_computation.1 | async-start | bytes 589824 | tf_op jit(solution)/shard_map/all_to_all | solution.py:673
  47.3 8.1 %local_backward.1 = (f32[256,2048]{1,0:T(8,128)}, f32[1,256]{1,0:T(1,128)S(1)}, bf16[256,2048]{1,0:T(8,128)(2,1)S(1)}) custom-call(s32[1,256]{1,0:T(1,128)S(1)} %copy-done.4, s32[4]{0:T(128)S(1)} %get-tuple-element.43.cuts.refs_1_, f32[32,16,128]{2,1,0:T(8,128)} %get-tuple-element.44.refs_2_, f32[4096,128]{1,0:T(8,128)} %get-tuple-element.45.refs_3_, ...), custom_call_target="tpu_custom_call" | custom-call | flops 33 | bytes 1 | tf_op jit(solution)/shard_map/local_backward/pallas_call | solution.py:752
  55.4 2.6 %all-to-all-done.1 = f32[32,1,2304]{2,1,0:T(1,128)S(1)} async-done(((f32[32,1,2304]{2,1,0:T(1,128)}), f32[32,1,2304]{2,1,0:T(1,128)S(1)}, u32[]{:S(2)}, u32[]{:S(2)}) %all-to-all-start.1) | async-done | bytes 294944 | tf_op jit(solution)/shard_map/all_to_all | solution.py:673
  58.0 2.8 %backward.1 = (f32[256,2048]{1,0:T(8,128)S(1)}, f32[1,256]{1,0:T(1,128)S(1)}, f32[32,128]{1,0:T(8,128)S(1)}, bf16[256,2048]{1,0:T(8,128)(2,1)S(1)}, bf16[256,2048]{1,0:T(8,128)(2,1)S(1)}) custom-call(s32[4]{0:T(128)S(1)} %get-tuple-element.43.cuts.refs_1_, f32[576,128]{1,0:T(8,128)S(1)} %bitcast.17, f32[1,256]{1,0:T(1,128)S(1)} %get-tuple-element.48.inner_local, ...), custom_call_target="tpu_custom_call" | custom-call | flops 805 | bytes 1 | tf_op jit(solution)/shard_map/backward/pallas_call | solution.py:798
  60.8 4.6 %collective-permute-start.6 = (f32[32,128]{1,0:T(8,128)S(1)}, f32[32,128]{1,0:T(8,128)S(1)}, u32[]{:S(2)}, u32[]{:S(2)}) collective-permute-start(f32[32,128]{1,0:T(8,128)S(1)} %get-tuple-element.52.refs_9_), channel_id=1, source_target_pairs={{0,128},{128,0},{1,129},{129,1},{2,130},{130,2},{3,131},{131,3},{4... | collective-permute-start | bytes 49160 | tf_op jit(solution)/shard_map/ppermute | solution.py:814
  65.4 0.8 %collective-permute-start.5 = (f32[1,256]{1,0:T(1,128)S(1)}, f32[1,256]{1,0:T(1,128)S(1)}, u32[]{:S(2)}, u32[]{:S(2)}) collective-permute-start(f32[1,256]{1,0:T(1,128)S(1)} %get-tuple-element.51.refs_5_), channel_id=1, source_target_pairs={{0,3},{1,0},{2,1},{3,2},{4,7},{5,4},{6,5},{7,6},{8,11},{9,8},{10,9... | collective-permute-start | bytes 3080 | tf_op jit(solution)/shard_map/ppermute | solution.py:645
  66.2 1.4 %collective-permute-start.4 = (f32[1,256]{1,0:T(1,128)S(1)}, f32[1,256]{1,0:T(1,128)S(1)}, u32[]{:S(2)}, u32[]{:S(2)}) collective-permute-start(f32[1,256]{1,0:T(1,128)S(1)} %get-tuple-element.51.refs_5_), channel_id=1, source_target_pairs={{0,2},{1,3},{2,0},{3,1},{4,6},{5,7},{6,4},{7,5},{8,10},{9,11},{10,... | collective-permute-start | bytes 3080 | tf_op jit(solution)/shard_map/ppermute | solution.py:645
  67.6 0.1 collective-permute-start.3
  67.7 2.2 %forward.1 = (bf16[256,2048]{1,0:T(8,128)(2,1)S(1)}, bf16[256,2048]{1,0:T(8,128)(2,1)S(1)}) custom-call(s32[4]{0:T(128)S(1)} %get-tuple-element.43.cuts.refs_1_, f32[576,128]{1,0:T(8,128)S(1)} %bitcast.18, f32[256,2048]{1,0:T(8,128)S(1)} %get-tuple-element.53.local, bf16[256,2048]{1,0:T(8,128)(2,1)S(1)} %get-tuple-element.54.gate, ...), custom_call_target="tpu_custom_call" | custom-call | flops 805 | bytes 1 | tf_op jit(solution)/shard_map/forward/pallas_call | solution.py:816
  69.9 0.3 collective-permute-done.4.refs_7_
  70.1 1.1 %collective-permute-done.3.refs_6_ = f32[1,256]{1,0:T(1,128)S(1)} collective-permute-done((f32[1,256]{1,0:T(1,128)S(1)}, f32[1,256]{1,0:T(1,128)S(1)}, u32[]{:S(2)}, u32[]{:S(2)}) %collective-permute-start.3) | collective-permute-done | bytes 1056 | tf_op jit(solution)/shard_map/ppermute | solution.py:645
  71.2 2.4 %features.1 = (bf16[256,2048]{1,0:T(8,128)(2,1)}, f32[16,128]{1,0:T(8,128)}, f32[16,128]{1,0:T(8,128)}, bf16[256,2048]{1,0:T(8,128)(2,1)}, bf16[256,2048]{1,0:T(8,128)(2,1)}) custom-call(f32[256,2048]{1,0:T(8,128)S(1)} %copy-done, f32[256,2048]{1,0:T(8,128)S(1)} %get-tuple-element.50.refs_1_, bf16[256,2048]{1,0:T(8,128)(2,1)S(1)} %get-tuple-element.49.feats.refs_2_, ...), custom_call_target="tpu_custom_call" | custom-call | flops 2 | bytes 1 | tf_op jit(solution)/shard_map/features/pallas_call | solution.py:826
  (13 shorter events, 0.0 us)
Async XLA Ops:
  0.6 10.7 %copy-start.1 = (f32[2048]{0:T(1024)S(1)}, f32[2048]{0:T(1024)}, u32[]{:S(2)}) copy-start(f32[2048]{0:T(1024)} %param.10) | copy-start | bytes 24580
  0.6 10.7 %copy-start.4 = (s32[1,256]{1,0:T(1,128)S(1)}, s32[1,256]{1,0:T(1,128)}, u32[]{:S(2)}) copy-start(s32[1,256]{1,0:T(1,128)} %refs_0_.5) | copy-start | bytes 3076
  3.7 6.7 %collective-permute-start.2 = (f32[1,256]{1,0:T(1,128)S(1)}, f32[1,256]{1,0:T(1,128)S(1)}, u32[]{:S(2)}, u32[]{:S(2)}) collective-permute-start(f32[1,256]{1,0:T(1,128)S(1)} %get-tuple-element.37.refs_4_), channel_id=1, source_target_pairs={{0,3},{1,0},{2,1},{3,2},{4,7},{5,4},{6,5},{7,6},{8,11},{9,8},{10,9... | collective-permute-start | bytes 3080 | tf_op jit(solution)/shard_map/ppermute | solution.py:645
  7.3 3.9 %collective-permute-start.1 = (f32[1,256]{1,0:T(1,128)S(1)}, f32[1,256]{1,0:T(1,128)S(1)}, u32[]{:S(2)}, u32[]{:S(2)}) collective-permute-start(f32[1,256]{1,0:T(1,128)S(1)} %get-tuple-element.37.refs_4_), channel_id=1, source_target_pairs={{0,2},{1,3},{2,0},{3,1},{4,6},{5,7},{6,4},{7,5},{8,10},{9,11},{10,... | collective-permute-start | bytes 3080 | tf_op jit(solution)/shard_map/ppermute | solution.py:645
  7.7 3.6 %collective-permute-start = (f32[1,256]{1,0:T(1,128)S(1)}, f32[1,256]{1,0:T(1,128)S(1)}, u32[]{:S(2)}, u32[]{:S(2)}) collective-permute-start(f32[1,256]{1,0:T(1,128)S(1)} %get-tuple-element.37.refs_4_), channel_id=1, source_target_pairs={{0,1},{1,2},{2,3},{3,0},{4,5},{5,6},{6,7},{7,4},{8,9},{9,10},{10,1... | collective-permute-start | bytes 3080 | tf_op jit(solution)/shard_map/ppermute | solution.py:645
  11.3 28.9 %copy-start.2 = (f32[128,16]{0,1:T(8,128)S(1)}, f32[128,16]{0,1:T(8,128)}, u32[]{:S(2)}) copy-start(f32[128,16]{0,1:T(8,128)} %param.12) | copy-start | bytes 24580
  11.3 28.9 %copy-start.3 = (f32[128,16]{0,1:T(8,128)S(1)}, f32[128,16]{0,1:T(8,128)}, u32[]{:S(2)}) copy-start(f32[128,16]{0,1:T(8,128)} %param.11) | copy-start | bytes 24580
  18.4 21.8 %all-to-all-start = ((f32[32,1,2304]{2,1,0:T(1,128)}), f32[32,1,2304]{2,1,0:T(1,128)S(1)}, u32[]{:S(2)}, u32[]{:S(2)}) async-start(f32[32,1,2304]{2,1,0:T(1,128)} %bitcast.38), calls=%async_computation | async-start | bytes 589824 | tf_op jit(solution)/shard_map/all_to_all | solution.py:673
  41.4 16.6 %all-to-all-start.1 = ((f32[32,1,2304]{2,1,0:T(1,128)}), f32[32,1,2304]{2,1,0:T(1,128)S(1)}, u32[]{:S(2)}, u32[]{:S(2)}) async-start(f32[32,1,2304]{2,1,0:T(1,128)} %bitcast.37), calls=%async_computation.1 | async-start | bytes 589824 | tf_op jit(solution)/shard_map/all_to_all | solution.py:673
  60.8 10.4 %collective-permute-start.6 = (f32[32,128]{1,0:T(8,128)S(1)}, f32[32,128]{1,0:T(8,128)S(1)}, u32[]{:S(2)}, u32[]{:S(2)}) collective-permute-start(f32[32,128]{1,0:T(8,128)S(1)} %get-tuple-element.52.refs_9_), channel_id=1, source_target_pairs={{0,128},{128,0},{1,129},{129,1},{2,130},{130,2},{3,131},{131,3},{4... | collective-permute-start | bytes 49160 | tf_op jit(solution)/shard_map/ppermute | solution.py:814
  65.4 4.4 %collective-permute-start.5 = (f32[1,256]{1,0:T(1,128)S(1)}, f32[1,256]{1,0:T(1,128)S(1)}, u32[]{:S(2)}, u32[]{:S(2)}) collective-permute-start(f32[1,256]{1,0:T(1,128)S(1)} %get-tuple-element.51.refs_5_), channel_id=1, source_target_pairs={{0,3},{1,0},{2,1},{3,2},{4,7},{5,4},{6,5},{7,6},{8,11},{9,8},{10,9... | collective-permute-start | bytes 3080 | tf_op jit(solution)/shard_map/ppermute | solution.py:645
  66.2 3.9 %collective-permute-start.4 = (f32[1,256]{1,0:T(1,128)S(1)}, f32[1,256]{1,0:T(1,128)S(1)}, u32[]{:S(2)}, u32[]{:S(2)}) collective-permute-start(f32[1,256]{1,0:T(1,128)S(1)} %get-tuple-element.51.refs_5_), channel_id=1, source_target_pairs={{0,2},{1,3},{2,0},{3,1},{4,6},{5,7},{6,4},{7,5},{8,10},{9,11},{10,... | collective-permute-start | bytes 3080 | tf_op jit(solution)/shard_map/ppermute | solution.py:645
  67.6 3.6 %collective-permute-start.3 = (f32[1,256]{1,0:T(1,128)S(1)}, f32[1,256]{1,0:T(1,128)S(1)}, u32[]{:S(2)}, u32[]{:S(2)}) collective-permute-start(f32[1,256]{1,0:T(1,128)S(1)} %get-tuple-element.51.refs_5_), channel_id=1, source_target_pairs={{0,1},{1,2},{2,3},{3,0},{4,5},{5,6},{6,7},{7,4},{8,9},{9,10},{10,1... | collective-permute-start | bytes 3080 | tf_op jit(solution)/shard_map/ppermute | solution.py:645
  67.7 3.6 %copy-start = (f32[256,2048]{1,0:T(8,128)S(1)}, f32[256,2048]{1,0:T(8,128)}, u32[]{:S(2)}) copy-start(f32[256,2048]{1,0:T(8,128)} %get-tuple-element.46.refs_0_) | copy-start | bytes 6291460
